TPU v7x, 32 devices: a whole 2x2x4 slice. The times are simulated.
32 devices in a mesh: tm: 8 (over z, y), clus: 4 (over x, core).
Axes of the slice: x: 2, y: 2, z: 4, core: 2. Of those that a mesh axis runs over, the one named last changes fastest.
Arguments:
- right_side: float32 [15, 32768], P(None, ('tm', 'clus')), may hold values from -8 to 8
- transition: float32 [15, 15, 32768], P(None, None, ('tm', 'clus')), may hold values from -1.5 to 1.5
- precond: float32 [15, 15, 32768], P(None, None, ('tm', 'clus')), as said below
- slot_of: int32 [32768], P(('tm', 'clus')), may hold values from 0 to 1023, as said below
- cluster_id: int32 [8, 4096], P('tm', 'clus'), may hold values from 0 to 63, never falling along the last dimension, each value on 1 to 128 neighbouring positions
- damping: float32 [8, 64], P('tm'), may hold values from 0.3 to 3
- pair_first: int32 [8, 8192], P('tm', 'clus'), may hold values from 0 to 4095
- pair_second: int32 [8, 8192], P('tm', 'clus'), may hold values from 0 to 4095
- pair_blocks: float32 [15, 15, 8, 8192], P(None, None, 'tm', 'clus'), may hold values from -1.5 to 1.5
Outputs:
- solution_field: float32 [15, 32768], P(None, ('tm', 'clus'))
- residual: float32 [15, 32768], P(None, ('tm', 'clus'))
Inputs may be any that keep to these rules, and one draw needn't show every extreme that they name: `slot_of`: the 1024 entries of each device's block are a permutation of 0 to 1023. `cluster_id`: never falling along each group's keyframes. `precond`: each keyframe's block is symmetric positive definite.
All inputs are finite; a program needn't handle non-finite values.
Results may differ from a plain program's by a relative error of at most 0.00015.
Values sent between devices are 32-bit elements; how exact they have to be, the bound alone decides.
No kernel may reach another device: no remote copies, remote signals or barrier semaphores. Data moves between devices by JAX's collectives and lax.ppermute only.
A program may use at most 128 MiB of HBM per device.

v0:
```python
import functools
import jax
import jax.numpy as jnp
from jax import lax
from jax.experimental import pallas as pl
from jax.experimental.pallas import tpu as pltpu
from jax.sharding import PartitionSpec as P

F32 = jnp.float32
BF16 = jnp.bfloat16
ROWS = 16
SUB = 256
LANE = 128
VMEM_LIMIT = 48 * 1024 * 1024


def iota(shape, axis):
    return lax.broadcasted_iota(jnp.int32, shape, axis)


def halves(value):
    high = value.astype(BF16).astype(F32)
    return high, value - high


def join(pieces):
    return pieces[0] if len(pieces) == 1 else jnp.concatenate(pieces, axis=1)


def hot_table(hot, index_ref, width):
    for start in range(0, width, SUB):
        low = index_ref[0:1, start : start + SUB] & (SUB - 1)
        table = jnp.where(iota((SUB, SUB), 0) == low, 1.0, 0.0)
        hot[:, start : start + SUB] = table.astype(BF16)


def column_to_row(column, state, share):
    spot = iota((ROWS, LANE), 1) % share
    row = iota((ROWS, LANE), 0)
    return jnp.sum(jnp.where((spot == row) & (row < state), column, 0.0), axis=0, keepdims=True)


def row_to_column(row, state):
    width = row.shape[1]
    sub = iota((ROWS, width), 0)
    keep = (sub == iota((ROWS, width), 1)) & (sub < state)
    return jnp.sum(jnp.where(keep, row, 0.0), axis=1, keepdims=True)


def note(column, scalar, state, share):
    spot = iota((1, LANE), 1) % share
    return jnp.where(spot == state, scalar, column_to_row(column, state, share))


def total(value):
    return jnp.sum(jnp.sum(value, axis=0, keepdims=True), axis=1, keepdims=True)


def apply_precond(precond, residual, scaled):
    state, width = residual.shape
    dot = jnp.zeros((state, LANE), F32)
    for start in range(0, width, LANE):
        at = slice(start, start + LANE)
        out = precond[0, :, at] * residual[0:1, at]
        for j in range(1, state):
            out = out + precond[j, :, at] * residual[j : j + 1, at]
        scaled[0:state, at] = out
        scaled[state:ROWS, at] = jnp.zeros((ROWS - state, LANE), F32)
        dot = dot + out * residual[:, at]
    return total(dot)


def send_states(scaled, dot, slot, hot, left, send, state):
    width = scaled.shape[1]
    groups, copies, _, share = send.shape
    parts = width // SUB
    for start in range(0, width, SUB):
        at = slice(start, start + SUB)
        high, low = halves(scaled[:, at])
        part = slot[0:1, at] >> 8
        for k in range(parts):
            left[k * 2 * ROWS : k * 2 * ROWS + ROWS, at] = jnp.where(part == k, high, 0.0).astype(BF16)
            left[k * 2 * ROWS + ROWS : (k + 1) * 2 * ROWS, at] = jnp.where(part == k, low, 0.0).astype(BF16)
    moved = lax.dot_general(left[...], hot[...], (((1,), (1,)), ((), ())), preferred_element_type=F32)
    notes = note(scaled[:, 0:1], dot, state, share)
    sub = iota((ROWS, share), 0)
    for k in range(parts):
        piece = moved[k * 2 * ROWS : k * 2 * ROWS + ROWS] + moved[k * 2 * ROWS + ROWS : (k + 1) * 2 * ROWS]
        for m in range(SUB // share):
            one = jnp.where(sub == state, notes[:, :share], piece[:, m * share : (m + 1) * share])
            for copy in range(copies):
                send[k * (SUB // share) + m, copy] = one


def begin_kernel(right, precond, slot, send, scaled, hot, left):
    state = right.shape[0]
    hot_table(hot, slot, right.shape[1])
    dot = apply_precond(precond, right, scaled)
    send_states(scaled, dot, slot, hot, left, send, state)


def group_kernel(n_time, n_clus, axes, got, heads, tails, blocks, damping, cluster, scaled, transition,
                 send, inertial, sums, field, hot, pulled, values, left, errors):
    state = transition.shape[0]
    width = scaled.shape[1]
    share = got.shape[2]
    pairs = heads.shape[1]
    parts = n_clus * width // SUB
    per_part = SUB // share
    chunks = pairs // LANE
    time_at, clus_at = lax.axis_index(axes[0]), lax.axis_index(axes[1])
    flat = time_at * n_clus + clus_at
    devices = n_time * n_clus

    def source(piece):
        return (piece % n_time) * n_clus + piece // n_time

    sums[...] = jnp.sum(got[:, state : state + 1, :], axis=0)

    following = row_to_column(got[jnp.minimum(flat + 1, devices - 1), state : state + 1, :], state)
    own = scaled[...]
    lane = iota((ROWS, width), 1)
    ahead = jnp.where(lane == width - 1, following, pltpu.roll(own, width - 1, 1))
    errors[...] = ahead
    for i in range(state):
        moved = jnp.sum(transition[i] * scaled[0:state, :], axis=0, keepdims=True)
        errors[i : i + 1, :] = errors[i : i + 1, :] - moved
    closed = (lane == width - 1) & (flat == devices - 1)
    error = jnp.where(closed | (iota((ROWS, width), 0) >= state), 0.0, errors[...])
    errors[...] = error
    prior = jnp.where(lane == 0, 0.0, pltpu.roll(error, 1, 1))
    inertial[state:ROWS, :] = jnp.zeros((ROWS - state, width), F32)
    energy = jnp.zeros((ROWS, LANE), F32)
    for start in range(0, width, LANE):
        at = slice(start, start + LANE)
        back = transition[0, :, at] * errors[0:1, at]
        for j in range(1, state):
            back = back + transition[j, :, at] * errors[j : j + 1, at]
        inertial[0:state, at] = prior[0:state, at] - back
        energy = energy + error[:, at] * error[:, at]
    product = total(energy)

    for k in range(parts):
        high, low = halves(join([got[source(k * per_part + m)] for m in range(per_part)]))
        field[k * 2 * ROWS : k * 2 * ROWS + ROWS, :] = high.astype(BF16)
        field[k * 2 * ROWS + ROWS : (k + 1) * 2 * ROWS, :] = low.astype(BF16)

    def pull(ends, base, n):
        at = pl.ds(pl.multiple_of(n * SUB, SUB), SUB)
        index = ends[0:1, at]
        low, part = index & (SUB - 1), index >> 8
        table = jnp.where(iota((SUB, SUB), 0) == low, 1.0, 0.0).astype(BF16)
        hot[:, pl.ds(pl.multiple_of(base * LANE + n * SUB, SUB), SUB)] = table
        found = jnp.dot(field[...], table, preferred_element_type=F32)
        out = jnp.zeros((ROWS, SUB), F32)
        for k in range(parts):
            one = found[k * 2 * ROWS : k * 2 * ROWS + ROWS] + found[k * 2 * ROWS + ROWS : (k + 1) * 2 * ROWS]
            out = jnp.where(part == k, one, out)
        for m in range(SUB // LANE):
            row = (base + n * (SUB // LANE) + m) * ROWS
            pulled[pl.ds(pl.multiple_of(row, ROWS), ROWS), :] = out[:, m * LANE : (m + 1) * LANE]

    def pull_both(n, carry):
        pull(heads, 0, n)
        pull(tails, chunks, n)
        return carry

    lax.fori_loop(0, pairs // SUB, pull_both, 0)

    squares = jnp.zeros((8, LANE), F32)
    for h in range(0, chunks, 8):
        far = [pulled[pl.ds((chunks + h) * ROWS + j, 8, stride=ROWS), :] for j in range(state)]
        back = [None] * state
        for i in range(state):
            row = [blocks[i * state + j, h : h + 8, :] for j in range(state)]
            f = pulled[pl.ds(h * ROWS + i, 8, stride=ROWS), :]
            for j in range(state):
                f = f - row[j] * far[j]
            squares = squares + f * f
            values[pl.ds(h * ROWS + i, 8, stride=ROWS), :] = f
            for j in range(state):
                back[j] = row[j] * f if i == 0 else back[j] + row[j] * f
        for j in range(state):
            values[pl.ds((chunks + h) * ROWS + j, 8, stride=ROWS), :] = -back[j]
        for j in range(state, ROWS):
            values[pl.ds(h * ROWS + j, 8, stride=ROWS), :] = jnp.zeros((8, LANE), F32)
            values[pl.ds((chunks + h) * ROWS + j, 8, stride=ROWS), :] = jnp.zeros((8, LANE), F32)
    product = product + total(squares)

    def spread(ends, base, n):
        at = pl.ds(pl.multiple_of(base * LANE + n * SUB, SUB), SUB)
        part = ends[0:1, pl.ds(pl.multiple_of(n * SUB, SUB), SUB)] >> 8
        row = (base + n * (SUB // LANE)) * ROWS
        high, low = halves(join([
            values[pl.ds(pl.multiple_of(row + m * ROWS, ROWS), ROWS), :] for m in range(SUB // LANE)
        ]))
        for k in range(parts):
            left[k * 2 * ROWS : k * 2 * ROWS + ROWS, at] = jnp.where(part == k, high, 0.0).astype(BF16)
            left[k * 2 * ROWS + ROWS : (k + 1) * 2 * ROWS, at] = jnp.where(part == k, low, 0.0).astype(BF16)

    def spread_both(n, carry):
        spread(heads, 0, n)
        spread(tails, chunks, n)
        return carry

    lax.fori_loop(0, pairs // SUB, spread_both, 0)
    summed = lax.dot_general(left[...], hot[...], (((1,), (1,)), ((), ())), preferred_element_type=F32)

    lam = jnp.zeros((1, width), F32)
    for label in range(damping.shape[1]):
        lam = jnp.where(cluster[...] == label, damping[0:1, label : label + 1], lam)
    sub = iota((ROWS, share), 0)
    damped = jnp.zeros((ROWS, share), F32)
    out = {}
    for k in range(parts):
        one = summed[k * 2 * ROWS : k * 2 * ROWS + ROWS] + summed[k * 2 * ROWS + ROWS : (k + 1) * 2 * ROWS]
        for m in range(per_part):
            piece = k * per_part + m
            c, t = piece // n_time, piece % n_time
            here = jnp.where(clus_at == c, lam[:, t * share : (t + 1) * share], 0.0)
            states = jnp.where(sub < state, got[source(piece)], 0.0)
            extra = here * states
            damped = damped + extra * states
            send[source(piece)] = one[:, m * share : (m + 1) * share] + extra
    product = product + total(damped)
    notes = note(error[:, width - 1 : width], product, state, share)
    for d in range(devices):
        send[d, state : state + 1, :] = notes[:, :share]


def image_of(n_time, n_clus, axes, got, inertial, slot, hot, field, image, state):
    width = image.shape[1]
    share = got.shape[2]
    per_part = SUB // share
    parts = width // SUB
    flat = lax.axis_index(axes[0]) * n_clus + lax.axis_index(axes[1])
    for k in range(parts):
        pieces = []
        for m in range(per_part):
            t = k * per_part + m
            one = got[t * n_clus]
            for c in range(1, n_clus):
                one = one + got[t * n_clus + c]
            pieces.append(one)
        high, low = halves(join(pieces))
        field[k * 2 * ROWS : k * 2 * ROWS + ROWS, :] = high.astype(BF16)
        field[k * 2 * ROWS + ROWS : (k + 1) * 2 * ROWS, :] = low.astype(BF16)
    prior = row_to_column(got[jnp.maximum(flat - 1, 0), state : state + 1, :], state)
    prior = jnp.where(flat == 0, 0.0, prior)
    for start in range(0, width, SUB):
        at = slice(start, start + SUB)
        found = jnp.dot(field[...], hot[:, at], preferred_element_type=F32)
        part = slot[0:1, at] >> 8
        out = jnp.zeros((ROWS, SUB), F32)
        for k in range(parts):
            one = found[k * 2 * ROWS : k * 2 * ROWS + ROWS] + found[k * 2 * ROWS + ROWS : (k + 1) * 2 * ROWS]
            out = jnp.where(part == k, one, out)
        out = out + inertial[:, at]
        if start == 0:
            out = jnp.where(iota((ROWS, SUB), 1) == 0, out + prior, out)
        image[:, at] = out
    return jnp.sum(got[:, state : state + 1, :], axis=0)[:, state : state + 1]


def step_kernel(n_time, n_clus, axes, got, right, inertial, precond, slot, sums,
                send, scaled, residual, image, scalars, hot, field, left):
    state, width = right.shape
    hot_table(hot, slot, width)
    product = image_of(n_time, n_clus, axes, got, inertial, slot, hot, field, image, state)
    alpha = sums[0:1, state : state + 1] / product
    residual[...] = right[...] - alpha * image[0:state, :]
    dot = apply_precond(precond, residual, scaled)
    send_states(scaled, dot, slot, hot, left, send, state)
    scalars[...] = jnp.broadcast_to(alpha, scalars.shape)


def end_kernel(n_time, n_clus, axes, got, residual, inertial, slot, first, scaled, along, sums, sums_next, scalars,
               solution_field, residual_out, hot, field, image):
    state, width = residual.shape
    hot_table(hot, slot, width)
    product = image_of(n_time, n_clus, axes, got, inertial, slot, hot, field, image, state)
    alpha = scalars[0:1, 0:1]
    rz, rz_next = sums[0:1, state : state + 1], sums_next[0:1, state : state + 1]
    ratio = rz_next / rz
    step = rz_next / (product - ratio * rz_next / alpha)
    direction = scaled[0:state, :] + ratio * first[0:state, :]
    solution_field[...] = alpha * first[0:state, :] + step * direction
    residual_out[...] = residual[...] - step * (image[0:state, :] + ratio * along[0:state, :])


def on_device(
    right_side,
    transition,
    precond,
    slot_of,
    cluster_id,
    damping,
    pair_first,
    pair_second,
    pair_blocks,
):
    axes = ("tm", "clus")
    state, width = right_side.shape
    n_time = lax.axis_size("tm")
    n_clus = lax.axis_size("clus")
    devices = n_time * n_clus
    share = width // n_time
    pairs = pair_first.shape[1]
    positions = n_clus * width
    slot = slot_of.reshape(1, width)
    blocks = pair_blocks.reshape(state * state, pairs // LANE, LANE)
    params = pltpu.CompilerParams(vmem_limit_bytes=VMEM_LIMIT)

    def like(*shape):
        return jax.ShapeDtypeStruct(shape, F32)

    message = like(devices, ROWS, share)
    outgoing = like(n_time, n_clus, ROWS, share)
    row = like(1, share)
    tile = like(ROWS, width)
    hot = pltpu.VMEM((SUB, width), BF16)
    left = pltpu.VMEM((2 * ROWS * width // SUB, width), BF16)
    field = pltpu.VMEM((2 * ROWS * width // SUB, SUB), BF16)

    def exchange(sent):
        return lax.all_to_all(sent.reshape(devices, ROWS, share), axes, split_axis=0, concat_axis=0, tiled=True)

    def grouped(got, scaled):
        return pl.pallas_call(
            functools.partial(group_kernel, n_time, n_clus, axes),
            out_shape=(message, tile, row),
            scratch_shapes=[
                pltpu.VMEM((2 * ROWS * positions // SUB, SUB), BF16),
                pltpu.VMEM((SUB, 2 * pairs), BF16),
                pltpu.VMEM((2 * pairs // LANE * ROWS, LANE), F32),
                pltpu.VMEM((2 * pairs // LANE * ROWS, LANE), F32),
                pltpu.VMEM((2 * ROWS * positions // SUB, 2 * pairs), BF16),
                pltpu.VMEM((ROWS, width), F32),
            ],
            compiler_params=params,
            name="group",
        )(got, pair_first, pair_second, blocks, damping, cluster_id, scaled, transition)

    sent, first = pl.pallas_call(
        begin_kernel,
        out_shape=(outgoing, tile),
        scratch_shapes=[hot, left],
        compiler_params=params,
        name="begin",
    )(right_side, precond, slot)
    back, inertial, sums = grouped(exchange(sent), first)
    sent, scaled, residual, along, scalars = pl.pallas_call(
        functools.partial(step_kernel, n_time, n_clus, axes),
        out_shape=(outgoing, tile, like(state, width), tile, like(1, LANE)),
        scratch_shapes=[hot, field, left],
        compiler_params=params,
        name="step",
    )(exchange(back), right_side, inertial, precond, slot, sums)
    back, inertial, sums_next = grouped(exchange(sent), scaled)
    return pl.pallas_call(
        functools.partial(end_kernel, n_time, n_clus, axes),
        out_shape=(like(state, width), like(state, width)),
        scratch_shapes=[hot, field, pltpu.VMEM((ROWS, width), F32)],
        compiler_params=params,
        name="end",
    )(exchange(back), residual, inertial, slot, first, scaled, along, sums, sums_next, scalars)


def solution(mesh):
    placed = (
        P(None, ("tm", "clus")),
        P(None, None, ("tm", "clus")),
        P(None, None, ("tm", "clus")),
        P(("tm", "clus")),
        P("tm", "clus"),
        P("tm", None),
        P("tm", "clus"),
        P("tm", "clus"),
        P(None, None, "tm", "clus"),
    )
    return jax.shard_map(
        on_device,
        mesh=mesh,
        in_specs=placed,
        out_specs=(P(None, ("tm", "clus")), P(None, ("tm", "clus"))),
        check_vma=False,
    )
```

profile of v0, /device:TPU:0, one launch (start us, length us, event | category | flops | bytes accessed | tf_op | source)
XLA Modules:
  0.0 78.4 jit_solution(13276305592185840610)
XLA Ops:
  0.6 0.0 copy-start.2
  0.6 1.2 %copy-done.2 = f32[15,15,1024]{2,1,0:T(8,128)S(1)} copy-done((f32[15,15,1024]{2,1,0:T(8,128)S(1)}, f32[15,15,1024]{2,1,0:T(8,128)}, u32[]{:S(2)}) %copy-start.2) | copy-done | bytes 921624
  1.8 0.0 copy-start.5
  1.8 0.8 %copy-done.5 = f32[15,1024]{1,0:T(8,128)S(1)} copy-done((f32[15,1024]{1,0:T(8,128)S(1)}, f32[15,1024]{1,0:T(8,128)}, u32[]{:S(2)}) %copy-start.5) | copy-done | bytes 61464
  2.7 0.0 copy-start.7
  2.7 0.7 copy-done.7
  3.4 0.0 copy-start.4
  3.4 0.4 begin.1
  3.7 17.7 %all_to_all.20.got = f32[32,16,128]{2,1,0:T(8,128)S(1)} all-to-all(f32[32,16,128]{2,1,0:T(8,128)S(1)} %bitcast.7), channel_id=1, replica_groups=mesh['tm'=8,'clus'=4] {'tm','clus'}, dimensions={0} | all-to-all | bytes 524288 | tf_op jit(solution)/shard_map/all_to_all | solution.py:326
  21.4 0.0 copy-done.4
  21.4 0.0 copy-start
  21.4 1.5 %copy-done = f32[15,15,1,2048]{3,2,1,0:T(1,128)S(1)} copy-done((f32[15,15,1,2048]{3,2,1,0:T(1,128)S(1)}, f32[15,15,1,2048]{3,2,1,0:T(1,128)}, u32[]{:S(2)}) %copy-start) | copy-done | bytes 1843224
  22.9 0.0 copy-start.9
  22.9 0.7 copy-done.9
  23.6 0.0 copy-start.11
  23.6 0.7 copy-done.11
  24.3 0.0 copy-start.13
  24.3 0.7 copy-done.13
  25.0 0.0 copy-start.14
  25.0 0.7 copy-done.14
  25.7 0.0 copy-start.3
  25.7 0.0 copy-start.6
  25.7 0.0 copy-start.8
  25.7 6.3 %group.2 = (f32[32,16,128]{2,1,0:T(8,128)S(1)}, f32[16,1024]{1,0:T(8,128)S(1)}, f32[1,128]{1,0:T(1,128)S(1)}) custom-call(f32[32,16,128]{2,1,0:T(8,128)S(1)} %all_to_all.20.got, s32[1,2048]{1,0:T(1,128)S(1)} %copy-done.9, s32[1,2048]{1,0:T(1,128)S(1)} %copy-done.11, f32[225,16,128]{2,1,0:T(8,128)S(1)} %bitcast.4, f32[1,64]{1,0:T(1,128)S(1)} %copy-done.14, ...), custom_call_target="tpu_custom_call" | custom-call | tf_op jit(solution)/shard_map/group/pallas_call | solution.py:329
  32.0 0.0 copy-start.1
  32.0 0.0 copy-start.10
  32.0 0.0 copy-start.12
  32.0 12.8 %all_to_all.21.got = f32[32,16,128]{2,1,0:T(8,128)S(1)} all-to-all(f32[32,16,128]{2,1,0:T(8,128)S(1)} %get-tuple-element.17), channel_id=1, replica_groups=mesh['tm'=8,'clus'=4] {'tm','clus'}, dimensions={0} | all-to-all | bytes 524288 | tf_op jit(solution)/shard_map/all_to_all | solution.py:326
  44.8 0.0 copy-done.3
  44.8 0.0 copy-done.6
  44.8 0.0 copy-done.8
  44.8 0.6 step.1
  45.5 12.8 %all_to_all.22.got = f32[32,16,128]{2,1,0:T(8,128)S(1)} all-to-all(f32[32,16,128]{2,1,0:T(8,128)S(1)} %bitcast.6), channel_id=1, replica_groups=mesh['tm'=8,'clus'=4] {'tm','clus'}, dimensions={0} | all-to-all | bytes 524288 | tf_op jit(solution)/shard_map/all_to_all | solution.py:326
  58.3 0.0 copy-done.1
  58.3 0.0 copy-done.10
  58.3 0.0 copy-done.12
  58.3 6.3 %group.3 = (f32[32,16,128]{2,1,0:T(8,128)S(1)}, f32[16,1024]{1,0:T(8,128)S(1)}, f32[1,128]{1,0:T(1,128)S(1)}) custom-call(f32[32,16,128]{2,1,0:T(8,128)S(1)} %all_to_all.22.got, s32[1,2048]{1,0:T(1,128)S(1)} %copy-done.10, s32[1,2048]{1,0:T(1,128)S(1)} %copy-done.12, f32[225,16,128]{2,1,0:T(8,128)S(1)} %bitcast.5, f32[1,64]{1,0:T(1,128)S(1)} %copy-done.14, ...), custom_call_target="tpu_custom_call" | custom-call | tf_op jit(solution)/shard_map/group/pallas_call | solution.py:329
  64.7 12.8 %all_to_all.23.got = f32[32,16,128]{2,1,0:T(8,128)S(1)} all-to-all(f32[32,16,128]{2,1,0:T(8,128)S(1)} %get-tuple-element.22), channel_id=1, replica_groups=mesh['tm'=8,'clus'=4] {'tm','clus'}, dimensions={0} | all-to-all | bytes 524288 | tf_op jit(solution)/shard_map/all_to_all | solution.py:326
  77.5 0.9 %end.1 = (f32[15,1024]{1,0:T(8,128)}, f32[15,1024]{1,0:T(8,128)}) custom-call(f32[32,16,128]{2,1,0:T(8,128)S(1)} %all_to_all.23.got, f32[15,1024]{1,0:T(8,128)S(1)} %get-tuple-element.23.residual, f32[16,1024]{1,0:T(8,128)S(1)} %get-tuple-element.24.inertial, s32[1,1024]{1,0:T(1,128)S(1)} %bitcast.10, f32[16,1024]{1,0:T(8,128)S(1)} %get-tuple-element.16.scaled.first, ...), custom_call_target="tpu_custom_call" | custom-call | tf_op jit(solution)/shard_map/end/pallas_call | solution.py:360
Async XLA Ops:
  0.6 1.2 %copy-start.2 = (f32[15,15,1024]{2,1,0:T(8,128)S(1)}, f32[15,15,1024]{2,1,0:T(8,128)}, u32[]{:S(2)}) copy-start(f32[15,15,1024]{2,1,0:T(8,128)} %precond.3) | copy-start | bytes 2764804
  1.8 0.8 %copy-start.5 = (f32[15,1024]{1,0:T(8,128)S(1)}, f32[15,1024]{1,0:T(8,128)}, u32[]{:S(2)}) copy-start(f32[15,1024]{1,0:T(8,128)} %right.3) | copy-start | bytes 184324
  2.7 0.7 copy-start.7
  3.4 18.1 %copy-start.4 = (f32[15,15,1024]{2,1,0:T(8,128)S(1)}, f32[15,15,1024]{2,1,0:T(8,128)}, u32[]{:S(2)}) copy-start(f32[15,15,1024]{2,1,0:T(8,128)} %transition.3) | copy-start | bytes 2764804
  21.4 1.5 %copy-start = (f32[15,15,1,2048]{3,2,1,0:T(1,128)S(1)}, f32[15,15,1,2048]{3,2,1,0:T(1,128)}, u32[]{:S(2)}) copy-start(f32[15,15,1,2048]{3,2,1,0:T(1,128)} %param.17) | copy-start | bytes 5529604
  22.9 0.7 copy-start.9
  23.6 0.7 copy-start.11
  24.3 0.7 copy-start.13
  25.0 0.7 copy-start.14
  25.7 19.1 %copy-start.3 = (f32[15,15,1024]{2,1,0:T(8,128)S(1)}, f32[15,15,1024]{2,1,0:T(8,128)}, u32[]{:S(2)}) copy-start(f32[15,15,1024]{2,1,0:T(8,128)} %precond.3) | copy-start | bytes 2764804
  25.7 19.1 %copy-start.6 = (f32[15,1024]{1,0:T(8,128)S(1)}, f32[15,1024]{1,0:T(8,128)}, u32[]{:S(2)}) copy-start(f32[15,1024]{1,0:T(8,128)} %right.3) | copy-start | bytes 184324
  25.7 19.1 %copy-start.8 = (s32[1024]{0:T(1024)S(1)}, s32[1024]{0:T(1024)}, u32[]{:S(2)}) copy-start(s32[1024]{0:T(1024)} %param.12) | copy-start | bytes 12292
  32.0 26.3 %copy-start.1 = (f32[15,15,1,2048]{3,2,1,0:T(1,128)S(1)}, f32[15,15,1,2048]{3,2,1,0:T(1,128)}, u32[]{:S(2)}) copy-start(f32[15,15,1,2048]{3,2,1,0:T(1,128)} %param.17) | copy-start | bytes 5529604
  32.0 26.3 %copy-start.10 = (s32[1,2048]{1,0:T(1,128)S(1)}, s32[1,2048]{1,0:T(1,128)}, u32[]{:S(2)}) copy-start(s32[1,2048]{1,0:T(1,128)} %heads.3) | copy-start | bytes 24580
  32.0 26.3 %copy-start.12 = (s32[1,2048]{1,0:T(1,128)S(1)}, s32[1,2048]{1,0:T(1,128)}, u32[]{:S(2)}) copy-start(s32[1,2048]{1,0:T(1,128)} %tails.3) | copy-start | bytes 24580
where the time goes:
time: 78.9 us; the launch traced here: 78.4 us
  blocking collectives  56.1 us (71%)
  Pallas kernels  14.5 us (18%)
  local copies, waits for them, and re-layouts  6.99 us (9%)
    all_to_all x4, blocking collectives, exchange(): lax.all_to_all(sent.reshape(devices, ROWS, share), axes, split_axis=0, co...  56.1 us
    pallas_call x2, Pallas kernels, grouped(): pl.pallas_call(functools.partial(group_kernel, n_time, n_clus, axes), out...  12.6 us
    unnamed x30, local copies, waits for them, and re-layouts  6.99 us

commit v1 on v0

--- a/solution.py
+++ b/solution.py
@@ -11,7 +11,7 @@
 ROWS = 16
 SUB = 256
 LANE = 128
-VMEM_LIMIT = 48 * 1024 * 1024
+VMEM_LIMIT = 16 * 1024 * 1024
 
 
 def iota(shape, axis):
@@ -19,19 +19,35 @@
 
 
 def halves(value):
-    high = value.astype(BF16).astype(F32)
-    return high, value - high
+    high = value.astype(BF16)
+    return high, (value - high.astype(F32)).astype(BF16)
 
 
 def join(pieces):
     return pieces[0] if len(pieces) == 1 else jnp.concatenate(pieces, axis=1)
 
 
+def spread_row(row, count):
+    return jnp.broadcast_to(row.astype(F32), (count, row.shape[1])).astype(BF16)
+
+
+def hot_tile(index):
+    rows = iota((SUB, index.shape[1]), 0).astype(F32).astype(BF16)
+    low = spread_row(index & (SUB - 1), SUB)
+    return jnp.where(rows == low, jnp.ones((), BF16), jnp.zeros((), BF16))
+
+
 def hot_table(hot, index_ref, width):
     for start in range(0, width, SUB):
-        low = index_ref[0:1, start : start + SUB] & (SUB - 1)
-        table = jnp.where(iota((SUB, SUB), 0) == low, 1.0, 0.0)
-        hot[:, start : start + SUB] = table.astype(BF16)
+        hot[:, start : start + SUB] = hot_tile(index_ref[0:1, start : start + SUB])
+
+
+def masked(part, k, value):
+    return jnp.where(part == jnp.asarray(k, BF16), value, jnp.zeros((), BF16))
+
+
+def both(left, right, contract):
+    return lax.dot_general(left, right, (contract, ((), ())), preferred_element_type=F32)
 
 
 def column_to_row(column, state, share):
@@ -76,25 +92,37 @@
     parts = width // SUB
     for start in range(0, width, SUB):
         at = slice(start, start + SUB)
+        also = slice(width + start, width + start + SUB)
         high, low = halves(scaled[:, at])
-        part = slot[0:1, at] >> 8
+        part = spread_row(slot[0:1, at] >> 8, ROWS)
         for k in range(parts):
-            left[k * 2 * ROWS : k * 2 * ROWS + ROWS, at] = jnp.where(part == k, high, 0.0).astype(BF16)
-            left[k * 2 * ROWS + ROWS : (k + 1) * 2 * ROWS, at] = jnp.where(part == k, low, 0.0).astype(BF16)
-    moved = lax.dot_general(left[...], hot[...], (((1,), (1,)), ((), ())), preferred_element_type=F32)
+            rows = slice(k * ROWS, (k + 1) * ROWS)
+            left[rows, at] = masked(part, k, high)
+            left[rows, also] = masked(part, k, low)
+    table = hot[...]
+    moved = both(left[:, :width], table, ((1,), (1,))) + both(left[:, width:], table, ((1,), (1,)))
     notes = note(scaled[:, 0:1], dot, state, share)
     sub = iota((ROWS, share), 0)
     for k in range(parts):
-        piece = moved[k * 2 * ROWS : k * 2 * ROWS + ROWS] + moved[k * 2 * ROWS + ROWS : (k + 1) * 2 * ROWS]
+        piece = moved[k * ROWS : (k + 1) * ROWS]
         for m in range(SUB // share):
             one = jnp.where(sub == state, notes[:, :share], piece[:, m * share : (m + 1) * share])
             for copy in range(copies):
                 send[k * (SUB // share) + m, copy] = one
 
 
-def begin_kernel(right, precond, slot, send, scaled, hot, left):
+def begin_kernel(right_in, precond_in, slot_in, send, scaled, hot, left, right, precond, slot, sems):
     state = right.shape[0]
+    copies = [
+        pltpu.make_async_copy(source, place, sems.at[i])
+        for i, (source, place) in enumerate(((precond_in, precond), (right_in, right), (slot_in, slot)))
+    ]
+    for copy in copies:
+        copy.start()
+    copies[2].wait()
     hot_table(hot, slot, right.shape[1])
+    copies[1].wait()
+    copies[0].wait()
     dot = apply_precond(precond, right, scaled)
     send_states(scaled, dot, slot, hot, left, send, state)
 
@@ -141,31 +169,25 @@
     product = total(energy)
 
     for k in range(parts):
-        high, low = halves(join([got[source(k * per_part + m)] for m in range(per_part)]))
-        field[k * 2 * ROWS : k * 2 * ROWS + ROWS, :] = high.astype(BF16)
-        field[k * 2 * ROWS + ROWS : (k + 1) * 2 * ROWS, :] = low.astype(BF16)
+        rows = slice(k * ROWS, (k + 1) * ROWS)
+        field[rows, 0:SUB], field[rows, SUB:] = halves(join([got[source(k * per_part + m)] for m in range(per_part)]))
 
     def pull(ends, base, n):
-        at = pl.ds(pl.multiple_of(n * SUB, SUB), SUB)
-        index = ends[0:1, at]
-        low, part = index & (SUB - 1), index >> 8
-        table = jnp.where(iota((SUB, SUB), 0) == low, 1.0, 0.0).astype(BF16)
-        hot[:, pl.ds(pl.multiple_of(base * LANE + n * SUB, SUB), SUB)] = table
-        found = jnp.dot(field[...], table, preferred_element_type=F32)
-        out = jnp.zeros((ROWS, SUB), F32)
-        for k in range(parts):
-            one = found[k * 2 * ROWS : k * 2 * ROWS + ROWS] + found[k * 2 * ROWS + ROWS : (k + 1) * 2 * ROWS]
-            out = jnp.where(part == k, one, out)
+        index = ends[0:1, n * SUB : (n + 1) * SUB]
+        part = index >> 8
+        table = hot_tile(index)
+        hot[:, base * LANE + n * SUB : base * LANE + (n + 1) * SUB] = table
+        found = both(field[:, 0:SUB], table, ((1,), (0,))) + both(field[:, SUB:], table, ((1,), (0,)))
+        out = found[0:ROWS]
+        for k in range(1, parts):
+            out = jnp.where(part == k, found[k * ROWS : (k + 1) * ROWS], out)
         for m in range(SUB // LANE):
             row = (base + n * (SUB // LANE) + m) * ROWS
-            pulled[pl.ds(pl.multiple_of(row, ROWS), ROWS), :] = out[:, m * LANE : (m + 1) * LANE]
-
-    def pull_both(n, carry):
+            pulled[row : row + ROWS, :] = out[:, m * LANE : (m + 1) * LANE]
+
+    for n in range(pairs // SUB):
         pull(heads, 0, n)
         pull(tails, chunks, n)
-        return carry
-
-    lax.fori_loop(0, pairs // SUB, pull_both, 0)
 
     squares = jnp.zeros((8, LANE), F32)
     for h in range(0, chunks, 8):
@@ -188,23 +210,21 @@
     product = product + total(squares)
 
     def spread(ends, base, n):
-        at = pl.ds(pl.multiple_of(base * LANE + n * SUB, SUB), SUB)
-        part = ends[0:1, pl.ds(pl.multiple_of(n * SUB, SUB), SUB)] >> 8
+        at = slice(base * LANE + n * SUB, base * LANE + (n + 1) * SUB)
+        also = slice(2 * pairs + at.start, 2 * pairs + at.stop)
+        part = spread_row(ends[0:1, n * SUB : (n + 1) * SUB] >> 8, ROWS)
         row = (base + n * (SUB // LANE)) * ROWS
-        high, low = halves(join([
-            values[pl.ds(pl.multiple_of(row + m * ROWS, ROWS), ROWS), :] for m in range(SUB // LANE)
-        ]))
+        high, low = halves(join([values[row + m * ROWS : row + (m + 1) * ROWS, :] for m in range(SUB // LANE)]))
         for k in range(parts):
-            left[k * 2 * ROWS : k * 2 * ROWS + ROWS, at] = jnp.where(part == k, high, 0.0).astype(BF16)
-            left[k * 2 * ROWS + ROWS : (k + 1) * 2 * ROWS, at] = jnp.where(part == k, low, 0.0).astype(BF16)
-
-    def spread_both(n, carry):
+            rows = slice(k * ROWS, (k + 1) * ROWS)
+            left[rows, at] = masked(part, k, high)
+            left[rows, also] = masked(part, k, low)
+
+    for n in range(pairs // SUB):
         spread(heads, 0, n)
         spread(tails, chunks, n)
-        return carry
-
-    lax.fori_loop(0, pairs // SUB, spread_both, 0)
-    summed = lax.dot_general(left[...], hot[...], (((1,), (1,)), ((), ())), preferred_element_type=F32)
+    table = hot[...]
+    summed = both(left[:, : 2 * pairs], table, ((1,), (1,))) + both(left[:, 2 * pairs :], table, ((1,), (1,)))
 
     lam = jnp.zeros((1, width), F32)
     for label in range(damping.shape[1]):
@@ -213,7 +233,7 @@
     damped = jnp.zeros((ROWS, share), F32)
     out = {}
     for k in range(parts):
-        one = summed[k * 2 * ROWS : k * 2 * ROWS + ROWS] + summed[k * 2 * ROWS + ROWS : (k + 1) * 2 * ROWS]
+        one = summed[k * ROWS : (k + 1) * ROWS]
         for m in range(per_part):
             piece = k * per_part + m
             c, t = piece // n_time, piece % n_time
@@ -242,19 +262,18 @@
             for c in range(1, n_clus):
                 one = one + got[t * n_clus + c]
             pieces.append(one)
-        high, low = halves(join(pieces))
-        field[k * 2 * ROWS : k * 2 * ROWS + ROWS, :] = high.astype(BF16)
-        field[k * 2 * ROWS + ROWS : (k + 1) * 2 * ROWS, :] = low.astype(BF16)
+        rows = slice(k * ROWS, (k + 1) * ROWS)
+        field[rows, 0:SUB], field[rows, SUB:] = halves(join(pieces))
     prior = row_to_column(got[jnp.maximum(flat - 1, 0), state : state + 1, :], state)
     prior = jnp.where(flat == 0, 0.0, prior)
     for start in range(0, width, SUB):
         at = slice(start, start + SUB)
-        found = jnp.dot(field[...], hot[:, at], preferred_element_type=F32)
+        table = hot[:, at]
+        found = both(field[:, 0:SUB], table, ((1,), (0,))) + both(field[:, SUB:], table, ((1,), (0,)))
         part = slot[0:1, at] >> 8
-        out = jnp.zeros((ROWS, SUB), F32)
-        for k in range(parts):
-            one = found[k * 2 * ROWS : k * 2 * ROWS + ROWS] + found[k * 2 * ROWS + ROWS : (k + 1) * 2 * ROWS]
-            out = jnp.where(part == k, one, out)
+        out = found[0:ROWS]
+        for k in range(1, parts):
+            out = jnp.where(part == k, found[k * ROWS : (k + 1) * ROWS], out)
         out = out + inertial[:, at]
         if start == 0:
             out = jnp.where(iota((ROWS, SUB), 1) == 0, out + prior, out)
@@ -319,8 +338,8 @@
     row = like(1, share)
     tile = like(ROWS, width)
     hot = pltpu.VMEM((SUB, width), BF16)
-    left = pltpu.VMEM((2 * ROWS * width // SUB, width), BF16)
-    field = pltpu.VMEM((2 * ROWS * width // SUB, SUB), BF16)
+    left = pltpu.VMEM((ROWS * width // SUB, 2 * width), BF16)
+    field = pltpu.VMEM((ROWS * width // SUB, 2 * SUB), BF16)
 
     def exchange(sent):
         return lax.all_to_all(sent.reshape(devices, ROWS, share), axes, split_axis=0, concat_axis=0, tiled=True)
@@ -330,11 +349,11 @@
             functools.partial(group_kernel, n_time, n_clus, axes),
             out_shape=(message, tile, row),
             scratch_shapes=[
-                pltpu.VMEM((2 * ROWS * positions // SUB, SUB), BF16),
+                pltpu.VMEM((ROWS * positions // SUB, 2 * SUB), BF16),
                 pltpu.VMEM((SUB, 2 * pairs), BF16),
                 pltpu.VMEM((2 * pairs // LANE * ROWS, LANE), F32),
                 pltpu.VMEM((2 * pairs // LANE * ROWS, LANE), F32),
-                pltpu.VMEM((2 * ROWS * positions // SUB, 2 * pairs), BF16),
+                pltpu.VMEM((ROWS * positions // SUB, 4 * pairs), BF16),
                 pltpu.VMEM((ROWS, width), F32),
             ],
             compiler_params=params,
@@ -344,7 +363,15 @@
     sent, first = pl.pallas_call(
         begin_kernel,
         out_shape=(outgoing, tile),
-        scratch_shapes=[hot, left],
+        in_specs=[pl.BlockSpec(memory_space=pltpu.HBM)] * 3,
+        scratch_shapes=[
+            hot,
+            left,
+            pltpu.VMEM(right_side.shape, F32),
+            pltpu.VMEM(precond.shape, F32),
+            pltpu.VMEM(slot.shape, jnp.int32),
+            pltpu.SemaphoreType.DMA((3,)),
+        ],
         compiler_params=params,
         name="begin",
     )(right_side, precond, slot)

time: 78.9 us -> 76.5 us (0.970)
  Pallas kernels: 14.5 us -> 12.2 us
    pallas_call x2, Pallas kernels: 12.6 us -> 9.62 us  [grouped(): pl.pallas_call(functools.partial(group_kernel, n_time, n_clus, axes), out...]
where the time goes in v1:
time: 76.5 us; the launch traced here: 76 us
  blocking collectives  56.1 us (73%)
  Pallas kernels  12.2 us (16%)
  local copies, waits for them, and re-layouts  6.99 us (9%)
    all_to_all x4, blocking collectives, exchange(): lax.all_to_all(sent.reshape(devices, ROWS, share), axes, split_axis=0, co...  56.1 us
    pallas_call x2, Pallas kernels, grouped(): pl.pallas_call(functools.partial(group_kernel, n_time, n_clus, axes), out...  9.62 us
    unnamed x30, local copies, waits for them, and re-layouts  6.99 us

profile of v1, /device:TPU:0, one launch (start us, length us, event | category | flops | bytes accessed | tf_op | source)
XLA Modules:
  0.0 76.0 jit_solution(7661436347656480105)
XLA Ops:
  0.6 0.0 copy-start.2
  0.6 1.2 %copy-done.2 = f32[15,15,1024]{2,1,0:T(8,128)S(1)} copy-done((f32[15,15,1024]{2,1,0:T(8,128)S(1)}, f32[15,15,1024]{2,1,0:T(8,128)}, u32[]{:S(2)}) %copy-start.2) | copy-done | bytes 921624
  1.8 0.0 copy-start.5
  1.8 0.8 %copy-done.5 = f32[15,1024]{1,0:T(8,128)S(1)} copy-done((f32[15,1024]{1,0:T(8,128)S(1)}, f32[15,1024]{1,0:T(8,128)}, u32[]{:S(2)}) %copy-start.5) | copy-done | bytes 61464
  2.7 0.0 copy-start.7
  2.7 0.7 copy-done.7
  3.4 0.0 copy-start.4
  3.4 0.9 %begin.1 = (f32[8,4,16,128]{3,2,1,0:T(8,128)S(1)}, f32[16,1024]{1,0:T(8,128)S(1)}) custom-call(f32[15,1024]{1,0:T(8,128)S(1)} %copy-done.5, f32[15,15,1024]{2,1,0:T(8,128)S(1)} %copy-done.2, s32[1,1024]{1,0:T(1,128)S(1)} %bitcast.8), custom_call_target="tpu_custom_call" | custom-call | tf_op jit(solution)/shard_map/begin/pallas_call | solution.py:363
  4.3 17.7 %all_to_all.20.got = f32[32,16,128]{2,1,0:T(8,128)S(1)} all-to-all(f32[32,16,128]{2,1,0:T(8,128)S(1)} %bitcast.7), channel_id=1, replica_groups=mesh['tm'=8,'clus'=4] {'tm','clus'}, dimensions={0} | all-to-all | bytes 524288 | tf_op jit(solution)/shard_map/all_to_all | solution.py:345
  22.0 0.0 copy-done.4
  22.0 0.0 copy-start
  22.0 1.5 %copy-done = f32[15,15,1,2048]{3,2,1,0:T(1,128)S(1)} copy-done((f32[15,15,1,2048]{3,2,1,0:T(1,128)S(1)}, f32[15,15,1,2048]{3,2,1,0:T(1,128)}, u32[]{:S(2)}) %copy-start) | copy-done | bytes 1843224
  23.5 0.0 copy-start.9
  23.5 0.7 copy-done.9
  24.2 0.0 copy-start.11
  24.2 0.7 copy-done.11
  24.9 0.0 copy-start.13
  24.9 0.7 copy-done.13
  25.6 0.0 copy-start.14
  25.6 0.7 copy-done.14
  26.2 0.0 copy-start.3
  26.2 0.0 copy-start.6
  26.2 0.0 copy-start.8
  26.2 4.8 %group.2 = (f32[32,16,128]{2,1,0:T(8,128)S(1)}, f32[16,1024]{1,0:T(8,128)S(1)}, f32[1,128]{1,0:T(1,128)S(1)}) custom-call(f32[32,16,128]{2,1,0:T(8,128)S(1)} %all_to_all.20.got, s32[1,2048]{1,0:T(1,128)S(1)} %copy-done.9, s32[1,2048]{1,0:T(1,128)S(1)} %copy-done.11, f32[225,16,128]{2,1,0:T(8,128)S(1)} %bitcast.4, f32[1,64]{1,0:T(1,128)S(1)} %copy-done.14, ...), custom_call_target="tpu_custom_call" | custom-call | tf_op jit(solution)/shard_map/group/pallas_call | solution.py:348
  31.0 0.0 copy-start.1
  31.1 0.0 copy-start.10
  31.1 0.0 copy-start.12
  31.1 12.8 %all_to_all.21.got = f32[32,16,128]{2,1,0:T(8,128)S(1)} all-to-all(f32[32,16,128]{2,1,0:T(8,128)S(1)} %get-tuple-element.17), channel_id=1, replica_groups=mesh['tm'=8,'clus'=4] {'tm','clus'}, dimensions={0} | all-to-all | bytes 524288 | tf_op jit(solution)/shard_map/all_to_all | solution.py:345
  43.9 0.0 copy-done.3
  43.9 0.0 copy-done.6
  43.9 0.0 copy-done.8
  43.9 0.7 step.1
  44.6 12.8 %all_to_all.22.got = f32[32,16,128]{2,1,0:T(8,128)S(1)} all-to-all(f32[32,16,128]{2,1,0:T(8,128)S(1)} %bitcast.6), channel_id=1, replica_groups=mesh['tm'=8,'clus'=4] {'tm','clus'}, dimensions={0} | all-to-all | bytes 524288 | tf_op jit(solution)/shard_map/all_to_all | solution.py:345
  57.4 0.0 copy-done.1
  57.4 0.0 copy-done.10
  57.4 0.0 copy-done.12
  57.4 4.8 %group.3 = (f32[32,16,128]{2,1,0:T(8,128)S(1)}, f32[16,1024]{1,0:T(8,128)S(1)}, f32[1,128]{1,0:T(1,128)S(1)}) custom-call(f32[32,16,128]{2,1,0:T(8,128)S(1)} %all_to_all.22.got, s32[1,2048]{1,0:T(1,128)S(1)} %copy-done.10, s32[1,2048]{1,0:T(1,128)S(1)} %copy-done.12, f32[225,16,128]{2,1,0:T(8,128)S(1)} %bitcast.5, f32[1,64]{1,0:T(1,128)S(1)} %copy-done.14, ...), custom_call_target="tpu_custom_call" | custom-call | tf_op jit(solution)/shard_map/group/pallas_call | solution.py:348
  62.3 12.8 %all_to_all.23.got = f32[32,16,128]{2,1,0:T(8,128)S(1)} all-to-all(f32[32,16,128]{2,1,0:T(8,128)S(1)} %get-tuple-element.22), channel_id=1, replica_groups=mesh['tm'=8,'clus'=4] {'tm','clus'}, dimensions={0} | all-to-all | bytes 524288 | tf_op jit(solution)/shard_map/all_to_all | solution.py:345
  75.1 0.9 %end.1 = (f32[15,1024]{1,0:T(8,128)}, f32[15,1024]{1,0:T(8,128)}) custom-call(f32[32,16,128]{2,1,0:T(8,128)S(1)} %all_to_all.23.got, f32[15,1024]{1,0:T(8,128)S(1)} %get-tuple-element.23.residual, f32[16,1024]{1,0:T(8,128)S(1)} %get-tuple-element.24.inertial, s32[1,1024]{1,0:T(1,128)S(1)} %bitcast.10, f32[16,1024]{1,0:T(8,128)S(1)} %get-tuple-element.16.scaled.first, ...), custom_call_target="tpu_custom_call" | custom-call | tf_op jit(solution)/shard_map/end/pallas_call | solution.py:387
Async XLA Ops:
  0.6 1.2 %copy-start.2 = (f32[15,15,1024]{2,1,0:T(8,128)S(1)}, f32[15,15,1024]{2,1,0:T(8,128)}, u32[]{:S(2)}) copy-start(f32[15,15,1024]{2,1,0:T(8,128)} %precond.1) | copy-start | bytes 2764804
  1.8 0.8 %copy-start.5 = (f32[15,1024]{1,0:T(8,128)S(1)}, f32[15,1024]{1,0:T(8,128)}, u32[]{:S(2)}) copy-start(f32[15,1024]{1,0:T(8,128)} %right.1) | copy-start | bytes 184324
  2.7 0.7 copy-start.7
  3.4 18.6 %copy-start.4 = (f32[15,15,1024]{2,1,0:T(8,128)S(1)}, f32[15,15,1024]{2,1,0:T(8,128)}, u32[]{:S(2)}) copy-start(f32[15,15,1024]{2,1,0:T(8,128)} %transition.3) | copy-start | bytes 2764804
  22.0 1.5 %copy-start = (f32[15,15,1,2048]{3,2,1,0:T(1,128)S(1)}, f32[15,15,1,2048]{3,2,1,0:T(1,128)}, u32[]{:S(2)}) copy-start(f32[15,15,1,2048]{3,2,1,0:T(1,128)} %param.17) | copy-start | bytes 5529604
  23.5 0.7 copy-start.9
  24.2 0.7 copy-start.11
  24.9 0.7 copy-start.13
  25.6 0.7 copy-start.14
  26.2 17.7 %copy-start.3 = (f32[15,15,1024]{2,1,0:T(8,128)S(1)}, f32[15,15,1024]{2,1,0:T(8,128)}, u32[]{:S(2)}) copy-start(f32[15,15,1024]{2,1,0:T(8,128)} %precond.1) | copy-start | bytes 2764804
  26.2 17.7 %copy-start.6 = (f32[15,1024]{1,0:T(8,128)S(1)}, f32[15,1024]{1,0:T(8,128)}, u32[]{:S(2)}) copy-start(f32[15,1024]{1,0:T(8,128)} %right.1) | copy-start | bytes 184324
  26.2 17.7 %copy-start.8 = (s32[1024]{0:T(1024)S(1)}, s32[1024]{0:T(1024)}, u32[]{:S(2)}) copy-start(s32[1024]{0:T(1024)} %param.12) | copy-start | bytes 12292
  31.0 26.4 %copy-start.1 = (f32[15,15,1,2048]{3,2,1,0:T(1,128)S(1)}, f32[15,15,1,2048]{3,2,1,0:T(1,128)}, u32[]{:S(2)}) copy-start(f32[15,15,1,2048]{3,2,1,0:T(1,128)} %param.17) | copy-start | bytes 5529604
  31.1 26.4 %copy-start.10 = (s32[1,2048]{1,0:T(1,128)S(1)}, s32[1,2048]{1,0:T(1,128)}, u32[]{:S(2)}) copy-start(s32[1,2048]{1,0:T(1,128)} %heads.3) | copy-start | bytes 24580
  31.1 26.3 %copy-start.12 = (s32[1,2048]{1,0:T(1,128)S(1)}, s32[1,2048]{1,0:T(1,128)}, u32[]{:S(2)}) copy-start(s32[1,2048]{1,0:T(1,128)} %tails.3) | copy-start | bytes 24580

commit v2 on v1

--- a/solution.py
+++ b/solution.py
@@ -113,12 +113,7 @@
 
 def begin_kernel(right_in, precond_in, slot_in, send, scaled, hot, left, right, precond, slot, sems):
     state = right.shape[0]
-    copies = [
-        pltpu.make_async_copy(source, place, sems.at[i])
-        for i, (source, place) in enumerate(((precond_in, precond), (right_in, right), (slot_in, slot)))
-    ]
-    for copy in copies:
-        copy.start()
+    copies = fetch(sems, (precond_in, precond), (right_in, right), (slot_in, slot))
     copies[2].wait()
     hot_table(hot, slot, right.shape[1])
     copies[1].wait()
@@ -127,10 +122,61 @@
     send_states(scaled, dot, slot, hot, left, send, state)
 
 
-def group_kernel(n_time, n_clus, axes, got, heads, tails, blocks, damping, cluster, scaled, transition,
-                 send, inertial, sums, field, hot, pulled, values, left, errors):
+def fetch(sems, *pairs):
+    copies = [pltpu.make_async_copy(source, place, sems.at[i]) for i, (source, place) in enumerate(pairs)]
+    for copy in copies:
+        copy.start()
+    return copies
+
+
+def tables_kernel(heads_in, tails_in, blocks_in, damping_in, cluster_in,
+                  hot, heads, tails, blocks, lam, damping, cluster, sems):
+    copies = fetch(sems, (heads_in, heads), (tails_in, tails), (damping_in, damping), (cluster_in, cluster),
+                   (blocks_in, blocks))
+    pairs = heads.shape[1]
+    copies[0].wait()
+    hot_table(hot.at[:, 0:pairs], heads, pairs)
+    copies[1].wait()
+    hot_table(hot.at[:, pairs:], tails, pairs)
+    copies[2].wait()
+    copies[3].wait()
+    row = jnp.zeros(lam.shape, F32)
+    for label in range(damping.shape[1]):
+        row = jnp.where(cluster[...] == label, damping[0:1, label : label + 1], row)
+    lam[...] = row
+    copies[4].wait()
+
+
+def inertial_kernel(scaled, transition_in, errors, inertial, ending, transition, sems):
     state = transition.shape[0]
     width = scaled.shape[1]
+    (copy,) = fetch(sems, (transition_in, transition))
+    lane = iota((ROWS, width), 1)
+    errors[...] = jnp.where(lane == width - 1, 0.0, pltpu.roll(scaled[...], width - 1, 1))
+    copy.wait()
+    for i in range(state):
+        moved = jnp.sum(transition[i] * scaled[0:state, :], axis=0, keepdims=True)
+        errors[i : i + 1, :] = errors[i : i + 1, :] - moved
+    prior = jnp.where(lane == 0, 0.0, pltpu.roll(errors[...], 1, 1))
+    inertial[state:ROWS, :] = jnp.zeros((ROWS - state, width), F32)
+    for start in range(0, width - LANE, LANE):
+        at = slice(start, start + LANE)
+        inertial[0:state, at] = prior[0:state, at] - back_product(transition, errors, at)
+    inertial[0:state, width - LANE :] = prior[0:state, width - LANE :]
+    ending[...] = transition[:, :, width - LANE :]
+
+
+def back_product(transition, errors, at):
+    back = transition[0, :, at] * errors[0:1, at]
+    for j in range(1, transition.shape[0]):
+        back = back + transition[j, :, at] * errors[j : j + 1, at]
+    return back
+
+
+def group_kernel(n_time, n_clus, axes, got, heads, tails, blocks, hot, lam, errors, partial, transition,
+                 send, inertial, sums, field, pulled, values, left, last):
+    state = transition.shape[0]
+    width = errors.shape[1]
     share = got.shape[2]
     pairs = heads.shape[1]
     parts = n_clus * width // SUB
@@ -146,37 +192,30 @@
     sums[...] = jnp.sum(got[:, state : state + 1, :], axis=0)
 
     following = row_to_column(got[jnp.minimum(flat + 1, devices - 1), state : state + 1, :], state)
-    own = scaled[...]
-    lane = iota((ROWS, width), 1)
-    ahead = jnp.where(lane == width - 1, following, pltpu.roll(own, width - 1, 1))
-    errors[...] = ahead
-    for i in range(state):
-        moved = jnp.sum(transition[i] * scaled[0:state, :], axis=0, keepdims=True)
-        errors[i : i + 1, :] = errors[i : i + 1, :] - moved
-    closed = (lane == width - 1) & (flat == devices - 1)
-    error = jnp.where(closed | (iota((ROWS, width), 0) >= state), 0.0, errors[...])
-    errors[...] = error
-    prior = jnp.where(lane == 0, 0.0, pltpu.roll(error, 1, 1))
-    inertial[state:ROWS, :] = jnp.zeros((ROWS - state, width), F32)
-    energy = jnp.zeros((ROWS, LANE), F32)
-    for start in range(0, width, LANE):
-        at = slice(start, start + LANE)
-        back = transition[0, :, at] * errors[0:1, at]
-        for j in range(1, state):
-            back = back + transition[j, :, at] * errors[j : j + 1, at]
-        inertial[0:state, at] = prior[0:state, at] - back
-        energy = energy + error[:, at] * error[:, at]
+    at = slice(width - LANE, width)
+    ending = iota((ROWS, LANE), 1) == LANE - 1
+    closed = ending & (flat == devices - 1)
+    ahead = jnp.where(ending, errors[:, at] + following, errors[:, at])
+    last[...] = jnp.where(closed | (iota((ROWS, LANE), 0) >= state), 0.0, ahead)
+    energy = last[...] * last[...]
+    for start in range(0, width - LANE, LANE):
+        block = errors[:, start : start + LANE]
+        energy = energy + jnp.where(iota((ROWS, LANE), 0) < state, block * block, 0.0)
     product = total(energy)
+    inertial[:, 0 : width - LANE] = partial[:, 0 : width - LANE]
+    inertial[state:ROWS, at] = partial[state:ROWS, at]
+    back = transition[0] * last[0:1, :]
+    for j in range(1, state):
+        back = back + transition[j] * last[j : j + 1, :]
+    inertial[0:state, at] = partial[0:state, at] - back
 
     for k in range(parts):
         rows = slice(k * ROWS, (k + 1) * ROWS)
         field[rows, 0:SUB], field[rows, SUB:] = halves(join([got[source(k * per_part + m)] for m in range(per_part)]))
 
     def pull(ends, base, n):
-        index = ends[0:1, n * SUB : (n + 1) * SUB]
-        part = index >> 8
-        table = hot_tile(index)
-        hot[:, base * LANE + n * SUB : base * LANE + (n + 1) * SUB] = table
+        part = ends[0:1, n * SUB : (n + 1) * SUB] >> 8
+        table = hot[:, base * LANE + n * SUB : base * LANE + (n + 1) * SUB]
         found = both(field[:, 0:SUB], table, ((1,), (0,))) + both(field[:, SUB:], table, ((1,), (0,)))
         out = found[0:ROWS]
         for k in range(1, parts):
@@ -226,12 +265,8 @@
     table = hot[...]
     summed = both(left[:, : 2 * pairs], table, ((1,), (1,))) + both(left[:, 2 * pairs :], table, ((1,), (1,)))
 
-    lam = jnp.zeros((1, width), F32)
-    for label in range(damping.shape[1]):
-        lam = jnp.where(cluster[...] == label, damping[0:1, label : label + 1], lam)
     sub = iota((ROWS, share), 0)
     damped = jnp.zeros((ROWS, share), F32)
-    out = {}
     for k in range(parts):
         one = summed[k * ROWS : (k + 1) * ROWS]
         for m in range(per_part):
@@ -243,7 +278,7 @@
             damped = damped + extra * states
             send[source(piece)] = one[:, m * share : (m + 1) * share] + extra
     product = product + total(damped)
-    notes = note(error[:, width - 1 : width], product, state, share)
+    notes = note(last[:, LANE - 1 : LANE], product, state, share)
     for d in range(devices):
         send[d, state : state + 1, :] = notes[:, :share]
 
@@ -344,26 +379,53 @@
     def exchange(sent):
         return lax.all_to_all(sent.reshape(devices, ROWS, share), axes, split_axis=0, concat_axis=0, tiled=True)
 
-    def grouped(got, scaled):
+    def held(*arrays):
+        return tuple(pltpu.with_memory_space_constraint(array, pltpu.HBM) for array in arrays)
+
+    in_hbm = pl.BlockSpec(memory_space=pltpu.HBM)
+    hot_pairs = jax.ShapeDtypeStruct((SUB, 2 * pairs), BF16)
+    ends = jax.ShapeDtypeStruct((1, pairs), jnp.int32)
+    tables = pl.pallas_call(
+        tables_kernel,
+        out_shape=(hot_pairs, ends, ends, like(*blocks.shape), like(1, width)),
+        in_specs=[in_hbm] * 5,
+        scratch_shapes=[
+            pltpu.VMEM(damping.shape, F32),
+            pltpu.VMEM(cluster_id.shape, jnp.int32),
+            pltpu.SemaphoreType.DMA((5,)),
+        ],
+        compiler_params=params,
+        name="tables",
+    )(*held(pair_first, pair_second, blocks, damping, cluster_id))
+    hot_of, heads, tails, blocks_of, lam = tables
+
+    def grouped(sent, scaled):
+        errors, partial, ending = pl.pallas_call(
+            inertial_kernel,
+            out_shape=(tile, tile, like(state, state, LANE)),
+            in_specs=[pl.BlockSpec(memory_space=pltpu.VMEM), in_hbm],
+            scratch_shapes=[pltpu.VMEM(transition.shape, F32), pltpu.SemaphoreType.DMA((1,))],
+            compiler_params=params,
+            name="inertial",
+        )(scaled, *held(transition))
         return pl.pallas_call(
             functools.partial(group_kernel, n_time, n_clus, axes),
             out_shape=(message, tile, row),
             scratch_shapes=[
                 pltpu.VMEM((ROWS * positions // SUB, 2 * SUB), BF16),
-                pltpu.VMEM((SUB, 2 * pairs), BF16),
                 pltpu.VMEM((2 * pairs // LANE * ROWS, LANE), F32),
                 pltpu.VMEM((2 * pairs // LANE * ROWS, LANE), F32),
                 pltpu.VMEM((ROWS * positions // SUB, 4 * pairs), BF16),
-                pltpu.VMEM((ROWS, width), F32),
+                pltpu.VMEM((ROWS, LANE), F32),
             ],
             compiler_params=params,
             name="group",
-        )(got, pair_first, pair_second, blocks, damping, cluster_id, scaled, transition)
+        )(exchange(sent), heads, tails, blocks_of, hot_of, lam, errors, partial, ending)
 
     sent, first = pl.pallas_call(
         begin_kernel,
         out_shape=(outgoing, tile),
-        in_specs=[pl.BlockSpec(memory_space=pltpu.HBM)] * 3,
+        in_specs=[in_hbm] * 3,
         scratch_shapes=[
             hot,
             left,
@@ -374,8 +436,8 @@
         ],
         compiler_params=params,
         name="begin",
-    )(right_side, precond, slot)
-    back, inertial, sums = grouped(exchange(sent), first)
+    )(*held(right_side, precond, slot))
+    back, inertial, sums = grouped(sent, first)
     sent, scaled, residual, along, scalars = pl.pallas_call(
         functools.partial(step_kernel, n_time, n_clus, axes),
         out_shape=(outgoing, tile, like(state, width), tile, like(1, LANE)),
@@ -383,7 +445,7 @@
         compiler_params=params,
         name="step",
     )(exchange(back), right_side, inertial, precond, slot, sums)
-    back, inertial, sums_next = grouped(exchange(sent), scaled)
+    back, inertial, sums_next = grouped(sent, scaled)
     return pl.pallas_call(
         functools.partial(end_kernel, n_time, n_clus, axes),
         out_shape=(like(state, width), like(state, width)),

time: 76.5 us -> 74.7 us (0.976)
  blocking collectives: 56.1 us -> 25.5 us
  waiting for transfers between devices: 0 us -> 15.3 us
  starting transfers between devices: 0 us -> 9.89 us
  Pallas kernels: 12.2 us -> 18.5 us
  local copies, waits for them, and re-layouts: 6.99 us -> 4.28 us
    all_to_all x4 -> x2, blocking collectives: 56.1 us -> 25.5 us  [exchange(): lax.all_to_all(sent.reshape(devices, ROWS, share), axes, split_axis=0, co...]
    all_to_all x0 -> x2, waiting for transfers between devices: none -> 15.3 us  [exchange(): lax.all_to_all(sent.reshape(devices, ROWS, share), axes, split_axis=0, co...]
    all_to_all x0 -> x2, starting transfers between devices: none -> 9.89 us  [exchange(): lax.all_to_all(sent.reshape(devices, ROWS, share), axes, split_axis=0, co...]
    pallas_call x1 -> x4, Pallas kernels: 0.92 us -> 7.05 us  [the longest x2 3.02 us: grouped(): pl.pallas_call(inertial_kernel, out_shape=(tile, tile, like(state, state,...]
    unnamed x30 -> x12, local copies, waits for them, and re-layouts: 6.99 us -> 4.28 us
  transfers between devices with their start and end apart: 0 -> 2, of which waited for: 0 -> 2; matrix products, arithmetic and copies ran while one was open for 0% -> 0% of each run, Pallas kernels for 0% -> 6%
where the time goes in v2:
time: 74.7 us; the launch traced here: 74.2 us
  blocking collectives  25.5 us (34%)
  Pallas kernels  18.5 us (25%)
  waiting for transfers between devices  15.3 us (20%)
  starting transfers between devices  9.89 us (13%)
  local copies, waits for them, and re-layouts  4.28 us (6%)
    all_to_all x2, blocking collectives, exchange(): lax.all_to_all(sent.reshape(devices, ROWS, share), axes, split_axis=0, co...  25.5 us
    all_to_all x2, waiting for transfers between devices, exchange(): lax.all_to_all(sent.reshape(devices, ROWS, share), axes, split_axis=0, co...  15.3 us
    all_to_all x2, starting transfers between devices, exchange(): lax.all_to_all(sent.reshape(devices, ROWS, share), axes, split_axis=0, co...  9.89 us
    pallas_call x2, Pallas kernels, grouped(): pl.pallas_call(functools.partial(group_kernel, n_time, n_clus, axes), out...  9.11 us
    unnamed x12, local copies, waits for them, and re-layouts  4.28 us
    pallas_call x2, Pallas kernels, grouped(): pl.pallas_call(inertial_kernel, out_shape=(tile, tile, like(state, state,...  3.02 us
    pallas_call x1, Pallas kernels, on_device(): pl.pallas_call(begin_kernel, out_shape=(outgoing, tile), in_specs=[in_hbm...  2.41 us
    pallas_call x1, Pallas kernels, on_device(): pl.pallas_call(tables_kernel, out_shape=(hot_pairs, ends, ends, like(*blo...  1.62 us
  transfers between devices with their start and end apart: 2, of which 2 were waited for; matrix products, arithmetic and copies ran while one was open for 0% of the time, Pallas kernels for 6%

profile of v2, /device:TPU:0, one launch (start us, length us, event | category | flops | bytes accessed | tf_op | source)
XLA Modules:
  0.0 74.2 jit_solution(15829474516748551543)
XLA Ops:
  0.6 2.4 %begin.1 = (f32[8,4,16,128]{3,2,1,0:T(8,128)}, f32[16,1024]{1,0:T(8,128)S(1)}) custom-call(f32[15,1024]{1,0:T(8,128)} %right.1, f32[15,15,1024]{2,1,0:T(8,128)} %precond.1, s32[1,1024]{1,0:T(1,128)} %bitcast.4), custom_call_target="tpu_custom_call" | custom-call | tf_op jit(solution)/shard_map/begin/pallas_call | solution.py:425
  3.0 7.3 %all-to-all-start = ((f32[32,16,128]{2,1,0:T(8,128)}), f32[32,16,128]{2,1,0:T(8,128)S(1)}, u32[]{:S(2)}, u32[]{:S(2)}) async-start(f32[32,16,128]{2,1,0:T(8,128)} %bitcast.1), calls=%async_computation | async-start | bytes 524288 | tf_op jit(solution)/shard_map/all_to_all | solution.py:380
  10.4 1.5 %inertial.2 = (f32[16,1024]{1,0:T(8,128)S(1)}, f32[16,1024]{1,0:T(8,128)S(1)}, f32[15,15,128]{2,1,0:T(8,128)S(1)}) custom-call(f32[16,1024]{1,0:T(8,128)S(1)} %get-tuple-element.32.scaled.first, f32[15,15,1024]{2,1,0:T(8,128)} %transition_in.3), custom_call_target="tpu_custom_call" | custom-call | tf_op jit(solution)/shard_map/inertial/pallas_call | solution.py:403
  11.9 1.6 %tables.1 = (bf16[256,4096]{1,0:T(8,128)(2,1)S(1)}, s32[1,2048]{1,0:T(1,128)S(1)}, s32[1,2048]{1,0:T(1,128)S(1)}, f32[225,16,128]{2,1,0:T(8,128)S(1)}, f32[1,1024]{1,0:T(1,128)S(1)}) custom-call(s32[1,2048]{1,0:T(1,128)} %heads_in.1, s32[1,2048]{1,0:T(1,128)} %tails_in.1, f32[225,16,128]{2,1,0:T(8,128)} %bitcast.7, f32[1,64]{1,0:T(1,128)} %damping_in.1, ...), custom_call_target="tpu_custom_call" | custom-call | tf_op jit(solution)/shard_map/tables/pallas_call | solution.py:388
  13.5 0.0 copy-start
  13.5 1.3 %copy-done = f32[225,16,128]{2,1,0:T(8,128)} copy-done((f32[225,16,128]{2,1,0:T(8,128)}, f32[225,16,128]{2,1,0:T(8,128)S(1)}, u32[]{:S(2)}) %copy-start) | copy-done | bytes 1843224
  14.8 6.2 %all-to-all-done.got = f32[32,16,128]{2,1,0:T(8,128)S(1)} async-done(((f32[32,16,128]{2,1,0:T(8,128)}), f32[32,16,128]{2,1,0:T(8,128)S(1)}, u32[]{:S(2)}, u32[]{:S(2)}) %all-to-all-start) | async-done | bytes 262176 | tf_op jit(solution)/shard_map/all_to_all | solution.py:380
  21.0 0.0 copy-start.1
  21.0 1.5 %copy-done.1 = f32[225,16,128]{2,1,0:T(8,128)S(1)} copy-done((f32[225,16,128]{2,1,0:T(8,128)S(1)}, f32[225,16,128]{2,1,0:T(8,128)}, u32[]{:S(2)}) %copy-start.1) | copy-done | bytes 1843224
  22.5 0.0 copy-start.3
  22.5 0.0 copy-start.4
  22.5 0.0 copy-start.5
  22.5 4.6 %group.2 = (f32[32,16,128]{2,1,0:T(8,128)S(1)}, f32[16,1024]{1,0:T(8,128)S(1)}, f32[1,128]{1,0:T(1,128)S(1)}) custom-call(f32[32,16,128]{2,1,0:T(8,128)S(1)} %all-to-all-done.got, s32[1,2048]{1,0:T(1,128)S(1)} %get-tuple-element.27.heads, s32[1,2048]{1,0:T(1,128)S(1)} %get-tuple-element.28.tails, f32[225,16,128]{2,1,0:T(8,128)S(1)} %copy-done.1, ...), custom_call_target="tpu_custom_call" | custom-call | tf_op jit(solution)/shard_map/group/pallas_call | solution.py:411
  27.0 12.8 %all_to_all.20.got = f32[32,16,128]{2,1,0:T(8,128)S(1)} all-to-all(f32[32,16,128]{2,1,0:T(8,128)S(1)} %get-tuple-element.36), channel_id=1, replica_groups=mesh['tm'=8,'clus'=4] {'tm','clus'}, dimensions={0} | all-to-all | bytes 524288 | tf_op jit(solution)/shard_map/all_to_all | solution.py:380
  39.8 0.0 copy-done.3
  39.8 0.0 copy-done.4
  39.8 0.0 copy-done.5
  39.8 1.4 %step.1 = (f32[8,4,16,128]{3,2,1,0:T(8,128)}, f32[16,1024]{1,0:T(8,128)S(1)}, f32[15,1024]{1,0:T(8,128)S(1)}, f32[16,1024]{1,0:T(8,128)S(1)}, f32[1,128]{1,0:T(1,128)S(1)}) custom-call(f32[32,16,128]{2,1,0:T(8,128)S(1)} %all_to_all.20.got, f32[15,1024]{1,0:T(8,128)S(1)} %copy-done.4, f32[16,1024]{1,0:T(8,128)S(1)} %get-tuple-element.37.inertial, ...), custom_call_target="tpu_custom_call" | custom-call | tf_op jit(solution)/shard_map/step/pallas_call | solution.py:441
  41.3 2.6 %all-to-all-start.2 = ((f32[32,16,128]{2,1,0:T(8,128)}), f32[32,16,128]{2,1,0:T(8,128)S(1)}, u32[]{:S(2)}, u32[]{:S(2)}) async-start(f32[32,16,128]{2,1,0:T(8,128)} %bitcast.3), calls=%async_computation.2 | async-start | bytes 524288 | tf_op jit(solution)/shard_map/all_to_all | solution.py:380
  43.9 1.5 %inertial.3 = (f32[16,1024]{1,0:T(8,128)S(1)}, f32[16,1024]{1,0:T(8,128)S(1)}, f32[15,15,128]{2,1,0:T(8,128)S(1)}) custom-call(f32[16,1024]{1,0:T(8,128)S(1)} %get-tuple-element.40.scaled, f32[15,15,1024]{2,1,0:T(8,128)} %transition_in.3), custom_call_target="tpu_custom_call" | custom-call | tf_op jit(solution)/shard_map/inertial/pallas_call | solution.py:403
  45.4 9.1 %all-to-all-done.2.got = f32[32,16,128]{2,1,0:T(8,128)S(1)} async-done(((f32[32,16,128]{2,1,0:T(8,128)}), f32[32,16,128]{2,1,0:T(8,128)S(1)}, u32[]{:S(2)}, u32[]{:S(2)}) %all-to-all-start.2) | async-done | bytes 262176 | tf_op jit(solution)/shard_map/all_to_all | solution.py:380
  54.5 0.0 copy-start.2
  54.5 1.5 %copy-done.2 = f32[225,16,128]{2,1,0:T(8,128)S(1)} copy-done((f32[225,16,128]{2,1,0:T(8,128)S(1)}, f32[225,16,128]{2,1,0:T(8,128)}, u32[]{:S(2)}) %copy-start.2) | copy-done | bytes 1843224
  56.0 4.6 %group.3 = (f32[32,16,128]{2,1,0:T(8,128)S(1)}, f32[16,1024]{1,0:T(8,128)S(1)}, f32[1,128]{1,0:T(1,128)S(1)}) custom-call(f32[32,16,128]{2,1,0:T(8,128)S(1)} %all-to-all-done.2.got, s32[1,2048]{1,0:T(1,128)S(1)} %get-tuple-element.27.heads, s32[1,2048]{1,0:T(1,128)S(1)} %get-tuple-element.28.tails, f32[225,16,128]{2,1,0:T(8,128)S(1)} %copy-done.2, ...), custom_call_target="tpu_custom_call" | custom-call | tf_op jit(solution)/shard_map/group/pallas_call | solution.py:411
  60.5 12.7 %all_to_all.21.got = f32[32,16,128]{2,1,0:T(8,128)S(1)} all-to-all(f32[32,16,128]{2,1,0:T(8,128)S(1)} %get-tuple-element.44), channel_id=1, replica_groups=mesh['tm'=8,'clus'=4] {'tm','clus'}, dimensions={0} | all-to-all | bytes 524288 | tf_op jit(solution)/shard_map/all_to_all | solution.py:380
  73.2 0.9 %end.1 = (f32[15,1024]{1,0:T(8,128)}, f32[15,1024]{1,0:T(8,128)}) custom-call(f32[32,16,128]{2,1,0:T(8,128)S(1)} %all_to_all.21.got, f32[15,1024]{1,0:T(8,128)S(1)} %get-tuple-element.45.residual, f32[16,1024]{1,0:T(8,128)S(1)} %get-tuple-element.46.inertial, s32[1,1024]{1,0:T(1,128)S(1)} %bitcast.6, f32[16,1024]{1,0:T(8,128)S(1)} %get-tuple-element.32.scaled.first, ...), custom_call_target="tpu_custom_call" | custom-call | tf_op jit(solution)/shard_map/end/pallas_call | solution.py:449
Async XLA Ops:
  3.0 17.9 %all-to-all-start = ((f32[32,16,128]{2,1,0:T(8,128)}), f32[32,16,128]{2,1,0:T(8,128)S(1)}, u32[]{:S(2)}, u32[]{:S(2)}) async-start(f32[32,16,128]{2,1,0:T(8,128)} %bitcast.1), calls=%async_computation | async-start | bytes 524288 | tf_op jit(solution)/shard_map/all_to_all | solution.py:380
  13.5 1.3 %copy-start = (f32[225,16,128]{2,1,0:T(8,128)}, f32[225,16,128]{2,1,0:T(8,128)S(1)}, u32[]{:S(2)}) copy-start(f32[225,16,128]{2,1,0:T(8,128)S(1)} %get-tuple-element.29.blocks) | copy-start | bytes 5529604
  21.0 1.5 %copy-start.1 = (f32[225,16,128]{2,1,0:T(8,128)S(1)}, f32[225,16,128]{2,1,0:T(8,128)}, u32[]{:S(2)}) copy-start(f32[225,16,128]{2,1,0:T(8,128)} %copy-done) | copy-start | bytes 5529604
  22.5 17.4 %copy-start.3 = (f32[15,15,1024]{2,1,0:T(8,128)S(1)}, f32[15,15,1024]{2,1,0:T(8,128)}, u32[]{:S(2)}) copy-start(f32[15,15,1024]{2,1,0:T(8,128)} %precond.1) | copy-start | bytes 2764804
  22.5 17.4 %copy-start.4 = (f32[15,1024]{1,0:T(8,128)S(1)}, f32[15,1024]{1,0:T(8,128)}, u32[]{:S(2)}) copy-start(f32[15,1024]{1,0:T(8,128)} %right.1) | copy-start | bytes 184324
  22.5 17.4 %copy-start.5 = (s32[1024]{0:T(1024)S(1)}, s32[1024]{0:T(1024)}, u32[]{:S(2)}) copy-start(s32[1024]{0:T(1024)} %param.12) | copy-start | bytes 12292
  41.3 13.2 %all-to-all-start.2 = ((f32[32,16,128]{2,1,0:T(8,128)}), f32[32,16,128]{2,1,0:T(8,128)S(1)}, u32[]{:S(2)}, u32[]{:S(2)}) async-start(f32[32,16,128]{2,1,0:T(8,128)} %bitcast.3), calls=%async_computation.2 | async-start | bytes 524288 | tf_op jit(solution)/shard_map/all_to_all | solution.py:380
  54.5 1.5 %copy-start.2 = (f32[225,16,128]{2,1,0:T(8,128)S(1)}, f32[225,16,128]{2,1,0:T(8,128)}, u32[]{:S(2)}) copy-start(f32[225,16,128]{2,1,0:T(8,128)} %copy-done) | copy-start | bytes 5529604

commit v3 on v1

--- a/solution.py
+++ b/solution.py
@@ -113,12 +113,7 @@
 
 def begin_kernel(right_in, precond_in, slot_in, send, scaled, hot, left, right, precond, slot, sems):
     state = right.shape[0]
-    copies = [
-        pltpu.make_async_copy(source, place, sems.at[i])
-        for i, (source, place) in enumerate(((precond_in, precond), (right_in, right), (slot_in, slot)))
-    ]
-    for copy in copies:
-        copy.start()
+    copies = fetch(sems, (precond_in, precond), (right_in, right), (slot_in, slot))
     copies[2].wait()
     hot_table(hot, slot, right.shape[1])
     copies[1].wait()
@@ -127,13 +122,40 @@
     send_states(scaled, dot, slot, hot, left, send, state)
 
 
-def group_kernel(n_time, n_clus, axes, got, heads, tails, blocks, damping, cluster, scaled, transition,
-                 send, inertial, sums, field, hot, pulled, values, left, errors):
+def fetch(sems, *pairs):
+    copies = [pltpu.make_async_copy(source, place, sems.at[i]) for i, (source, place) in enumerate(pairs)]
+    for copy in copies:
+        copy.start()
+    return copies
+
+
+def back_product(transition, errors, at):
+    back = transition[0, :, at] * errors[0:1, at]
+    for j in range(1, transition.shape[0]):
+        back = back + transition[j, :, at] * errors[j : j + 1, at]
+    return back
+
+
+def group_kernel(n_time, n_clus, axes, staged, got, scaled, *refs):
+    inputs, (send, inertial, sums), refs = refs[:8], refs[8:11], refs[11:]
+    field, hot, values, left, errors = refs[:5]
+    if staged:
+        places, sems = refs[5:13], refs[13]
+        copies = fetch(sems, *zip(inputs, places))
+        inputs = places
+
+    def arrived(*which):
+        if staged:
+            for i in which:
+                copies[i].wait()
+
+    heads, tails, heads_tile, tails_tile, cluster, damping, blocks, transition = inputs
     state = transition.shape[0]
     width = scaled.shape[1]
     share = got.shape[2]
     pairs = heads.shape[1]
     parts = n_clus * width // SUB
+    rows_of = n_clus * width // LANE
     per_part = SUB // share
     chunks = pairs // LANE
     time_at, clus_at = lax.axis_index(axes[0]), lax.axis_index(axes[1])
@@ -145,11 +167,64 @@
 
     sums[...] = jnp.sum(got[:, state : state + 1, :], axis=0)
 
+    for r in range(rows_of):
+        field[r] = join([got[source(r * (LANE // share) + m)] for m in range(LANE // share)])
+
+    def pull(ends, h):
+        index = ends[h : h + 8, :]
+        low, part = index & (LANE - 1), index >> 7
+        out = [None] * state
+        for r in range(rows_of):
+            here = part == r
+            for c in range(state):
+                from_row = jnp.broadcast_to(field[r, c : c + 1, :], (8, LANE))
+                found = jnp.take_along_axis(from_row, low, axis=1)
+                out[c] = found if r == 0 else jnp.where(here, found, out[c])
+        return out
+
+    arrived(0, 1, 2, 3)
+    squares = jnp.zeros((8, LANE), F32)
+    for h in range(0, chunks, 8):
+        far = pull(tails_tile, h)
+        near = pull(heads_tile, h)
+        if h == 0:
+            arrived(6)
+        back = [None] * state
+        for i in range(state):
+            row = [blocks[i * state + j, h : h + 8, :] for j in range(state)]
+            f = near[i]
+            for j in range(state):
+                f = f - row[j] * far[j]
+            squares = squares + f * f
+            values[pl.ds(h * ROWS + i, 8, stride=ROWS), :] = f
+            for j in range(state):
+                back[j] = row[j] * f if i == 0 else back[j] + row[j] * f
+        for j in range(state):
+            values[pl.ds((chunks + h) * ROWS + j, 8, stride=ROWS), :] = -back[j]
+        for j in range(state, ROWS):
+            values[pl.ds(h * ROWS + j, 8, stride=ROWS), :] = jnp.zeros((8, LANE), F32)
+            values[pl.ds((chunks + h) * ROWS + j, 8, stride=ROWS), :] = jnp.zeros((8, LANE), F32)
+
+    def spread(ends, base, n):
+        at = slice(base * LANE + n * SUB, base * LANE + (n + 1) * SUB)
+        index = ends[0:1, n * SUB : (n + 1) * SUB]
+        hot[:, at] = hot_tile(index)
+        part = spread_row(index >> 8, ROWS)
+        row = (base + n * (SUB // LANE)) * ROWS
+        high, low = halves(join([values[row + m * ROWS : row + (m + 1) * ROWS, :] for m in range(SUB // LANE)]))
+        for k in range(parts):
+            left[k * 2 * ROWS : k * 2 * ROWS + ROWS, at] = masked(part, k, high)
+            left[k * 2 * ROWS + ROWS : (k + 1) * 2 * ROWS, at] = masked(part, k, low)
+
+    for n in range(pairs // SUB):
+        spread(heads, 0, n)
+        spread(tails, chunks, n)
+    summed = both(left[...], hot[...], ((1,), (1,)))
+
+    arrived(7)
     following = row_to_column(got[jnp.minimum(flat + 1, devices - 1), state : state + 1, :], state)
-    own = scaled[...]
     lane = iota((ROWS, width), 1)
-    ahead = jnp.where(lane == width - 1, following, pltpu.roll(own, width - 1, 1))
-    errors[...] = ahead
+    errors[...] = jnp.where(lane == width - 1, following, pltpu.roll(scaled[...], width - 1, 1))
     for i in range(state):
         moved = jnp.sum(transition[i] * scaled[0:state, :], axis=0, keepdims=True)
         errors[i : i + 1, :] = errors[i : i + 1, :] - moved
@@ -161,79 +236,19 @@
     energy = jnp.zeros((ROWS, LANE), F32)
     for start in range(0, width, LANE):
         at = slice(start, start + LANE)
-        back = transition[0, :, at] * errors[0:1, at]
-        for j in range(1, state):
-            back = back + transition[j, :, at] * errors[j : j + 1, at]
-        inertial[0:state, at] = prior[0:state, at] - back
+        inertial[0:state, at] = prior[0:state, at] - back_product(transition, errors, at)
         energy = energy + error[:, at] * error[:, at]
-    product = total(energy)
-
-    for k in range(parts):
-        rows = slice(k * ROWS, (k + 1) * ROWS)
-        field[rows, 0:SUB], field[rows, SUB:] = halves(join([got[source(k * per_part + m)] for m in range(per_part)]))
-
-    def pull(ends, base, n):
-        index = ends[0:1, n * SUB : (n + 1) * SUB]
-        part = index >> 8
-        table = hot_tile(index)
-        hot[:, base * LANE + n * SUB : base * LANE + (n + 1) * SUB] = table
-        found = both(field[:, 0:SUB], table, ((1,), (0,))) + both(field[:, SUB:], table, ((1,), (0,)))
-        out = found[0:ROWS]
-        for k in range(1, parts):
-            out = jnp.where(part == k, found[k * ROWS : (k + 1) * ROWS], out)
-        for m in range(SUB // LANE):
-            row = (base + n * (SUB // LANE) + m) * ROWS
-            pulled[row : row + ROWS, :] = out[:, m * LANE : (m + 1) * LANE]
-
-    for n in range(pairs // SUB):
-        pull(heads, 0, n)
-        pull(tails, chunks, n)
-
-    squares = jnp.zeros((8, LANE), F32)
-    for h in range(0, chunks, 8):
-        far = [pulled[pl.ds((chunks + h) * ROWS + j, 8, stride=ROWS), :] for j in range(state)]
-        back = [None] * state
-        for i in range(state):
-            row = [blocks[i * state + j, h : h + 8, :] for j in range(state)]
-            f = pulled[pl.ds(h * ROWS + i, 8, stride=ROWS), :]
-            for j in range(state):
-                f = f - row[j] * far[j]
-            squares = squares + f * f
-            values[pl.ds(h * ROWS + i, 8, stride=ROWS), :] = f
-            for j in range(state):
-                back[j] = row[j] * f if i == 0 else back[j] + row[j] * f
-        for j in range(state):
-            values[pl.ds((chunks + h) * ROWS + j, 8, stride=ROWS), :] = -back[j]
-        for j in range(state, ROWS):
-            values[pl.ds(h * ROWS + j, 8, stride=ROWS), :] = jnp.zeros((8, LANE), F32)
-            values[pl.ds((chunks + h) * ROWS + j, 8, stride=ROWS), :] = jnp.zeros((8, LANE), F32)
-    product = product + total(squares)
-
-    def spread(ends, base, n):
-        at = slice(base * LANE + n * SUB, base * LANE + (n + 1) * SUB)
-        also = slice(2 * pairs + at.start, 2 * pairs + at.stop)
-        part = spread_row(ends[0:1, n * SUB : (n + 1) * SUB] >> 8, ROWS)
-        row = (base + n * (SUB // LANE)) * ROWS
-        high, low = halves(join([values[row + m * ROWS : row + (m + 1) * ROWS, :] for m in range(SUB // LANE)]))
-        for k in range(parts):
-            rows = slice(k * ROWS, (k + 1) * ROWS)
-            left[rows, at] = masked(part, k, high)
-            left[rows, also] = masked(part, k, low)
-
-    for n in range(pairs // SUB):
-        spread(heads, 0, n)
-        spread(tails, chunks, n)
-    table = hot[...]
-    summed = both(left[:, : 2 * pairs], table, ((1,), (1,))) + both(left[:, 2 * pairs :], table, ((1,), (1,)))
-
+    product = total(squares) + total(energy)
+
+    arrived(4, 5)
     lam = jnp.zeros((1, width), F32)
     for label in range(damping.shape[1]):
         lam = jnp.where(cluster[...] == label, damping[0:1, label : label + 1], lam)
+
     sub = iota((ROWS, share), 0)
     damped = jnp.zeros((ROWS, share), F32)
-    out = {}
     for k in range(parts):
-        one = summed[k * ROWS : (k + 1) * ROWS]
+        one = summed[k * 2 * ROWS : k * 2 * ROWS + ROWS] + summed[k * 2 * ROWS + ROWS : (k + 1) * 2 * ROWS]
         for m in range(per_part):
             piece = k * per_part + m
             c, t = piece // n_time, piece % n_time
@@ -344,26 +359,39 @@
     def exchange(sent):
         return lax.all_to_all(sent.reshape(devices, ROWS, share), axes, split_axis=0, concat_axis=0, tiled=True)
 
-    def grouped(got, scaled):
+    def held(*arrays):
+        return tuple(pltpu.with_memory_space_constraint(array, pltpu.HBM) for array in arrays)
+
+    in_hbm = pl.BlockSpec(memory_space=pltpu.HBM)
+    dense = (pairs // LANE, LANE)
+    own = (pair_first, pair_second, pair_first.reshape(dense), pair_second.reshape(dense),
+           cluster_id, damping, blocks, transition)
+
+    def grouped(got, scaled, staged):
+        in_vmem = pl.BlockSpec(memory_space=pltpu.VMEM)
+        scratch = [
+            pltpu.VMEM((positions // LANE, ROWS, LANE), F32),
+            pltpu.VMEM((SUB, 2 * pairs), BF16),
+            pltpu.VMEM((2 * pairs // LANE * ROWS, LANE), F32),
+            pltpu.VMEM((2 * ROWS * positions // SUB, 2 * pairs), BF16),
+            pltpu.VMEM((ROWS, width), F32),
+        ]
+        if staged:
+            scratch += [pltpu.VMEM(array.shape, array.dtype) for array in own]
+            scratch += [pltpu.SemaphoreType.DMA((len(own),))]
         return pl.pallas_call(
-            functools.partial(group_kernel, n_time, n_clus, axes),
+            functools.partial(group_kernel, n_time, n_clus, axes, staged),
             out_shape=(message, tile, row),
-            scratch_shapes=[
-                pltpu.VMEM((ROWS * positions // SUB, 2 * SUB), BF16),
-                pltpu.VMEM((SUB, 2 * pairs), BF16),
-                pltpu.VMEM((2 * pairs // LANE * ROWS, LANE), F32),
-                pltpu.VMEM((2 * pairs // LANE * ROWS, LANE), F32),
-                pltpu.VMEM((ROWS * positions // SUB, 4 * pairs), BF16),
-                pltpu.VMEM((ROWS, width), F32),
-            ],
+            in_specs=[in_vmem] * 2 + [in_hbm if staged else in_vmem] * len(own),
+            scratch_shapes=scratch,
             compiler_params=params,
             name="group",
-        )(got, pair_first, pair_second, blocks, damping, cluster_id, scaled, transition)
+        )(got, scaled, *(held(*own) if staged else own))
 
     sent, first = pl.pallas_call(
         begin_kernel,
         out_shape=(outgoing, tile),
-        in_specs=[pl.BlockSpec(memory_space=pltpu.HBM)] * 3,
+        in_specs=[in_hbm] * 3,
         scratch_shapes=[
             hot,
             left,
@@ -374,8 +402,8 @@
         ],
         compiler_params=params,
         name="begin",
-    )(right_side, precond, slot)
-    back, inertial, sums = grouped(exchange(sent), first)
+    )(*held(right_side, precond, slot))
+    back, inertial, sums = grouped(exchange(sent), first, True)
     sent, scaled, residual, along, scalars = pl.pallas_call(
         functools.partial(step_kernel, n_time, n_clus, axes),
         out_shape=(outgoing, tile, like(state, width), tile, like(1, LANE)),
@@ -383,7 +411,7 @@
         compiler_params=params,
         name="step",
     )(exchange(back), right_side, inertial, precond, slot, sums)
-    back, inertial, sums_next = grouped(exchange(sent), scaled)
+    back, inertial, sums_next = grouped(exchange(sent), scaled, False)
     return pl.pallas_call(
         functools.partial(end_kernel, n_time, n_clus, axes),
         out_shape=(like(state, width), like(state, width)),

time: 76.5 us -> 68.9 us (0.901)
  local copies, waits for them, and re-layouts: 6.99 us -> 0.05 us
    unnamed x30 -> x18, local copies, waits for them, and re-layouts: 6.99 us -> 0.05 us
where the time goes in v3:
time: 68.9 us; the launch traced here: 68.6 us
  blocking collectives  56.1 us (81%)
  Pallas kernels  11.7 us (17%)
  between operations  0.73 us (1%)
    all_to_all x4, blocking collectives, exchange(): lax.all_to_all(sent.reshape(devices, ROWS, share), axes, split_axis=0, co...  56.1 us
    pallas_call x2, Pallas kernels, grouped(): pl.pallas_call(functools.partial(group_kernel, n_time, n_clus, axes, stag...  8.41 us
    pallas_call x1, Pallas kernels, on_device(): pl.pallas_call(begin_kernel, out_shape=(outgoing, tile), in_specs=[in_hbm...  1.67 us

profile of v3, /device:TPU:0, one launch (start us, length us, event | category | flops | bytes accessed | tf_op | source)
XLA Modules:
  0.0 68.6 jit_solution(3499571450581011009)
XLA Ops:
  0.6 1.7 %begin.1 = (f32[8,4,16,128]{3,2,1,0:T(8,128)S(1)}, f32[16,1024]{1,0:T(8,128)S(1)}) custom-call(f32[15,1024]{1,0:T(8,128)} %right.1, f32[15,15,1024]{2,1,0:T(8,128)} %precond.1, s32[1,1024]{1,0:T(1,128)} %bitcast.14), custom_call_target="tpu_custom_call" | custom-call | tf_op jit(solution)/shard_map/begin/pallas_call | solution.py:391
  2.3 17.7 %all_to_all.20.got = f32[32,16,128]{2,1,0:T(8,128)S(1)} all-to-all(f32[32,16,128]{2,1,0:T(8,128)S(1)} %bitcast.9), channel_id=1, replica_groups=mesh['tm'=8,'clus'=4] {'tm','clus'}, dimensions={0} | all-to-all | bytes 524288 | tf_op jit(solution)/shard_map/all_to_all | solution.py:360
  20.0 0.0 copy-start.1
  20.0 0.0 copy-start.3
  20.0 0.0 copy-start.6
  20.0 0.0 copy-start.2
  20.0 4.9 %group.2 = (f32[32,16,128]{2,1,0:T(8,128)S(1)}, f32[16,1024]{1,0:T(8,128)S(1)}, f32[1,128]{1,0:T(1,128)S(1)}) custom-call(f32[32,16,128]{2,1,0:T(8,128)S(1)} %all_to_all.20.got, f32[16,1024]{1,0:T(8,128)S(1)} %get-tuple-element.16.scaled.first, s32[1,2048]{1,0:T(1,128)} %refs_0_.3, s32[1,2048]{1,0:T(1,128)} %refs_1_.3, s32[16,128]{1,0:T(8,128)} %bitcast.10, ...), custom_call_target="tpu_custom_call" | custom-call | tf_op jit(solution)/shard_map/group/pallas_call | solution.py:382
  24.9 0.0 copy-start
  24.9 0.0 copy-start.4
  24.9 0.0 copy-start.5
  24.9 0.0 copy-start.7
  24.9 0.0 copy-start.8
  25.0 12.8 %all_to_all.21.got = f32[32,16,128]{2,1,0:T(8,128)S(1)} all-to-all(f32[32,16,128]{2,1,0:T(8,128)S(1)} %get-tuple-element.17), channel_id=1, replica_groups=mesh['tm'=8,'clus'=4] {'tm','clus'}, dimensions={0} | all-to-all | bytes 524288 | tf_op jit(solution)/shard_map/all_to_all | solution.py:360
  37.8 0.0 copy-done.1
  37.8 0.0 copy-done.3
  37.8 0.0 copy-done.6
  37.8 0.7 %step.1 = (f32[8,4,16,128]{3,2,1,0:T(8,128)S(1)}, f32[16,1024]{1,0:T(8,128)S(1)}, f32[15,1024]{1,0:T(8,128)S(1)}, f32[16,1024]{1,0:T(8,128)S(1)}, f32[1,128]{1,0:T(1,128)S(1)}) custom-call(f32[32,16,128]{2,1,0:T(8,128)S(1)} %all_to_all.21.got, f32[15,1024]{1,0:T(8,128)S(1)} %copy-done.3, f32[16,1024]{1,0:T(8,128)S(1)} %get-tuple-element.18.inertial, ...), custom_call_target="tpu_custom_call" | custom-call | tf_op jit(solution)/shard_map/step/pallas_call | solution.py:407
  38.5 12.8 %all_to_all.22.got = f32[32,16,128]{2,1,0:T(8,128)S(1)} all-to-all(f32[32,16,128]{2,1,0:T(8,128)S(1)} %bitcast.8), channel_id=1, replica_groups=mesh['tm'=8,'clus'=4] {'tm','clus'}, dimensions={0} | all-to-all | bytes 524288 | tf_op jit(solution)/shard_map/all_to_all | solution.py:360
  51.3 0.0 copy-done.2
  51.3 0.0 copy-done
  51.3 0.0 copy-done.4
  51.3 0.0 copy-done.5
  51.3 0.0 copy-done.7
  51.3 0.0 copy-done.8
  51.3 3.6 %group.3 = (f32[32,16,128]{2,1,0:T(8,128)S(1)}, f32[16,1024]{1,0:T(8,128)S(1)}, f32[1,128]{1,0:T(1,128)S(1)}) custom-call(f32[32,16,128]{2,1,0:T(8,128)S(1)} %all_to_all.22.got, f32[16,1024]{1,0:T(8,128)S(1)} %get-tuple-element.21.scaled, s32[1,2048]{1,0:T(1,128)S(1)} %copy-done.4, s32[1,2048]{1,0:T(1,128)S(1)} %copy-done.5, s32[16,128]{1,0:T(8,128)S(1)} %bitcast.11, ...), custom_call_target="tpu_custom_call" | custom-call | tf_op jit(solution)/shard_map/group/pallas_call | solution.py:382
  54.9 12.8 %all_to_all.23.got = f32[32,16,128]{2,1,0:T(8,128)S(1)} all-to-all(f32[32,16,128]{2,1,0:T(8,128)S(1)} %get-tuple-element.22), channel_id=1, replica_groups=mesh['tm'=8,'clus'=4] {'tm','clus'}, dimensions={0} | all-to-all | bytes 524288 | tf_op jit(solution)/shard_map/all_to_all | solution.py:360
  67.7 0.9 %end.1 = (f32[15,1024]{1,0:T(8,128)}, f32[15,1024]{1,0:T(8,128)}) custom-call(f32[32,16,128]{2,1,0:T(8,128)S(1)} %all_to_all.23.got, f32[15,1024]{1,0:T(8,128)S(1)} %get-tuple-element.23.residual, f32[16,1024]{1,0:T(8,128)S(1)} %get-tuple-element.24.inertial, s32[1,1024]{1,0:T(1,128)S(1)} %bitcast.16, f32[16,1024]{1,0:T(8,128)S(1)} %get-tuple-element.16.scaled.first, ...), custom_call_target="tpu_custom_call" | custom-call | tf_op jit(solution)/shard_map/end/pallas_call | solution.py:415
Async XLA Ops:
  20.0 17.8 %copy-start.1 = (f32[15,15,1024]{2,1,0:T(8,128)S(1)}, f32[15,15,1024]{2,1,0:T(8,128)}, u32[]{:S(2)}) copy-start(f32[15,15,1024]{2,1,0:T(8,128)} %precond.1) | copy-start | bytes 2764804
  20.0 17.8 %copy-start.3 = (f32[15,1024]{1,0:T(8,128)S(1)}, f32[15,1024]{1,0:T(8,128)}, u32[]{:S(2)}) copy-start(f32[15,1024]{1,0:T(8,128)} %right.1) | copy-start | bytes 184324
  20.0 17.8 %copy-start.6 = (s32[1024]{0:T(1024)S(1)}, s32[1024]{0:T(1024)}, u32[]{:S(2)}) copy-start(s32[1024]{0:T(1024)} %param.12) | copy-start | bytes 12292
  20.0 31.3 %copy-start.2 = (f32[15,15,1024]{2,1,0:T(8,128)S(1)}, f32[15,15,1024]{2,1,0:T(8,128)}, u32[]{:S(2)}) copy-start(f32[15,15,1024]{2,1,0:T(8,128)} %refs_7_.3) | copy-start | bytes 2764804
  24.9 26.4 %copy-start = (f32[15,15,1,2048]{3,2,1,0:T(1,128)S(1)}, f32[15,15,1,2048]{3,2,1,0:T(1,128)}, u32[]{:S(2)}) copy-start(f32[15,15,1,2048]{3,2,1,0:T(1,128)} %param.17) | copy-start | bytes 5529604
  24.9 26.4 %copy-start.4 = (s32[1,2048]{1,0:T(1,128)S(1)}, s32[1,2048]{1,0:T(1,128)}, u32[]{:S(2)}) copy-start(s32[1,2048]{1,0:T(1,128)} %refs_0_.3) | copy-start | bytes 24580
  24.9 26.4 %copy-start.5 = (s32[1,2048]{1,0:T(1,128)S(1)}, s32[1,2048]{1,0:T(1,128)}, u32[]{:S(2)}) copy-start(s32[1,2048]{1,0:T(1,128)} %refs_1_.3) | copy-start | bytes 24580
  24.9 26.4 %copy-start.7 = (s32[1,1024]{1,0:T(1,128)S(1)}, s32[1,1024]{1,0:T(1,128)}, u32[]{:S(2)}) copy-start(s32[1,1024]{1,0:T(1,128)} %refs_4_.3) | copy-start | bytes 12292
  24.9 26.4 %copy-start.8 = (f32[1,64]{1,0:T(1,128)S(1)}, f32[1,64]{1,0:T(1,128)}, u32[]{:S(2)}) copy-start(f32[1,64]{1,0:T(1,128)} %refs_5_.3) | copy-start | bytes 772

commit v4 on v3

--- a/solution.py
+++ b/solution.py
@@ -111,15 +111,20 @@
                 send[k * (SUB // share) + m, copy] = one
 
 
-def begin_kernel(right_in, precond_in, slot_in, send, scaled, hot, left, right, precond, slot, sems):
+def begin_kernel(right_in, precond_in, slot_in, *refs):
+    carried = len(refs) // 2 - 4
+    (send, scaled), (hot, left, right, precond, slot, sems) = refs[carried : carried + 2], refs[2 * carried + 2 :]
     state = right.shape[0]
-    copies = fetch(sems, (precond_in, precond), (right_in, right), (slot_in, slot))
+    copies = fetch(sems, (precond_in, precond), (right_in, right), (slot_in, slot),
+                   *zip(refs[:carried], refs[carried + 2 : 2 * carried + 2]))
     copies[2].wait()
     hot_table(hot, slot, right.shape[1])
     copies[1].wait()
     copies[0].wait()
     dot = apply_precond(precond, right, scaled)
     send_states(scaled, dot, slot, hot, left, send, state)
+    for copy in copies[3:]:
+        copy.wait()
 
 
 def fetch(sems, *pairs):
@@ -140,14 +145,13 @@
     inputs, (send, inertial, sums), refs = refs[:8], refs[8:11], refs[11:]
     field, hot, values, left, errors = refs[:5]
     if staged:
-        places, sems = refs[5:13], refs[13]
-        copies = fetch(sems, *zip(inputs, places))
-        inputs = places
-
-    def arrived(*which):
+        places, sems = refs[5:7], refs[7]
+        copies = fetch(sems, *zip(inputs[6:], places))
+        inputs = inputs[:6] + places
+
+    def arrived(which):
         if staged:
-            for i in which:
-                copies[i].wait()
+            copies[which].wait()
 
     heads, tails, heads_tile, tails_tile, cluster, damping, blocks, transition = inputs
     state = transition.shape[0]
@@ -182,13 +186,24 @@
                 out[c] = found if r == 0 else jnp.where(here, found, out[c])
         return out
 
-    arrived(0, 1, 2, 3)
+    def spread(ends, base, n):
+        at = slice(base * LANE + n * SUB, base * LANE + (n + 1) * SUB)
+        index = ends[0:1, n * SUB : (n + 1) * SUB]
+        hot[:, at] = hot_tile(index)
+        part = spread_row(index >> 8, ROWS)
+        row = (base + n * (SUB // LANE)) * ROWS
+        high, low = halves(join([values[row + m * ROWS : row + (m + 1) * ROWS, :] for m in range(SUB // LANE)]))
+        for k in range(parts):
+            left[k * 2 * ROWS : k * 2 * ROWS + ROWS, at] = masked(part, k, high)
+            left[k * 2 * ROWS + ROWS : (k + 1) * 2 * ROWS, at] = masked(part, k, low)
+
     squares = jnp.zeros((8, LANE), F32)
+    summed = []
     for h in range(0, chunks, 8):
         far = pull(tails_tile, h)
         near = pull(heads_tile, h)
         if h == 0:
-            arrived(6)
+            arrived(0)
         back = [None] * state
         for i in range(state):
             row = [blocks[i * state + j, h : h + 8, :] for j in range(state)]
@@ -204,24 +219,15 @@
         for j in range(state, ROWS):
             values[pl.ds(h * ROWS + j, 8, stride=ROWS), :] = jnp.zeros((8, LANE), F32)
             values[pl.ds((chunks + h) * ROWS + j, 8, stride=ROWS), :] = jnp.zeros((8, LANE), F32)
-
-    def spread(ends, base, n):
-        at = slice(base * LANE + n * SUB, base * LANE + (n + 1) * SUB)
-        index = ends[0:1, n * SUB : (n + 1) * SUB]
-        hot[:, at] = hot_tile(index)
-        part = spread_row(index >> 8, ROWS)
-        row = (base + n * (SUB // LANE)) * ROWS
-        high, low = halves(join([values[row + m * ROWS : row + (m + 1) * ROWS, :] for m in range(SUB // LANE)]))
-        for k in range(parts):
-            left[k * 2 * ROWS : k * 2 * ROWS + ROWS, at] = masked(part, k, high)
-            left[k * 2 * ROWS + ROWS : (k + 1) * 2 * ROWS, at] = masked(part, k, low)
-
-    for n in range(pairs // SUB):
-        spread(heads, 0, n)
-        spread(tails, chunks, n)
-    summed = both(left[...], hot[...], ((1,), (1,)))
-
-    arrived(7)
+        first, final = h * LANE // SUB, (h + 8) * LANE // SUB
+        for base, ends in ((0, heads), (chunks, tails)):
+            for n in range(first, final):
+                spread(ends, base, n)
+            at = slice(base * LANE + first * SUB, base * LANE + final * SUB)
+            summed.append(both(left[:, at], hot[:, at], ((1,), (1,))))
+    summed = functools.reduce(lambda one, other: one + other, summed)
+
+    arrived(1)
     following = row_to_column(got[jnp.minimum(flat + 1, devices - 1), state : state + 1, :], state)
     lane = iota((ROWS, width), 1)
     errors[...] = jnp.where(lane == width - 1, following, pltpu.roll(scaled[...], width - 1, 1))
@@ -240,7 +246,6 @@
         energy = energy + error[:, at] * error[:, at]
     product = total(squares) + total(energy)
 
-    arrived(4, 5)
     lam = jnp.zeros((1, width), F32)
     for label in range(damping.shape[1]):
         lam = jnp.where(cluster[...] == label, damping[0:1, label : label + 1], lam)
@@ -364,8 +369,8 @@
 
     in_hbm = pl.BlockSpec(memory_space=pltpu.HBM)
     dense = (pairs // LANE, LANE)
-    own = (pair_first, pair_second, pair_first.reshape(dense), pair_second.reshape(dense),
-           cluster_id, damping, blocks, transition)
+    small = (pair_first, pair_second, pair_first.reshape(dense), pair_second.reshape(dense), cluster_id, damping)
+    large = (blocks, transition)
 
     def grouped(got, scaled, staged):
         in_vmem = pl.BlockSpec(memory_space=pltpu.VMEM)
@@ -377,32 +382,32 @@
             pltpu.VMEM((ROWS, width), F32),
         ]
         if staged:
-            scratch += [pltpu.VMEM(array.shape, array.dtype) for array in own]
-            scratch += [pltpu.SemaphoreType.DMA((len(own),))]
+            scratch += [pltpu.VMEM(array.shape, array.dtype) for array in large]
+            scratch += [pltpu.SemaphoreType.DMA((len(large),))]
         return pl.pallas_call(
             functools.partial(group_kernel, n_time, n_clus, axes, staged),
             out_shape=(message, tile, row),
-            in_specs=[in_vmem] * 2 + [in_hbm if staged else in_vmem] * len(own),
+            in_specs=[in_vmem] * (2 + len(small)) + [in_hbm if staged else in_vmem] * len(large),
             scratch_shapes=scratch,
             compiler_params=params,
             name="group",
-        )(got, scaled, *(held(*own) if staged else own))
-
-    sent, first = pl.pallas_call(
+        )(got, scaled, *carried, *(held(*large) if staged else large))
+
+    sent, first, *carried = pl.pallas_call(
         begin_kernel,
-        out_shape=(outgoing, tile),
-        in_specs=[in_hbm] * 3,
+        out_shape=(outgoing, tile, *(jax.ShapeDtypeStruct(array.shape, array.dtype) for array in small)),
+        in_specs=[in_hbm] * (3 + len(small)),
         scratch_shapes=[
             hot,
             left,
             pltpu.VMEM(right_side.shape, F32),
             pltpu.VMEM(precond.shape, F32),
             pltpu.VMEM(slot.shape, jnp.int32),
-            pltpu.SemaphoreType.DMA((3,)),
+            pltpu.SemaphoreType.DMA((3 + len(small),)),
         ],
         compiler_params=params,
         name="begin",
-    )(*held(right_side, precond, slot))
+    )(*held(right_side, precond, slot, *small))
     back, inertial, sums = grouped(exchange(sent), first, True)
     sent, scaled, residual, along, scalars = pl.pallas_call(
         functools.partial(step_kernel, n_time, n_clus, axes),

time: 68.9 us -> 70.3 us (1.020)
  Pallas kernels: 11.7 us -> 13.3 us
    pallas_call x2, Pallas kernels: 8.41 us -> 9.89 us  [grouped(): pl.pallas_call(functools.partial(group_kernel, n_time, n_clus, axes, stag...]
where the time goes in v4:
time: 70.3 us; the launch traced here: 70.1 us
  blocking collectives  56.1 us (80%)
  Pallas kernels  13.3 us (19%)
    all_to_all x4, blocking collectives, exchange(): lax.all_to_all(sent.reshape(devices, ROWS, share), axes, split_axis=0, co...  56.1 us
    pallas_call x2, Pallas kernels, grouped(): pl.pallas_call(functools.partial(group_kernel, n_time, n_clus, axes, stag...  9.89 us
    pallas_call x1, Pallas kernels, on_device(): pl.pallas_call(begin_kernel, out_shape=(outgoing, tile, *(jax.ShapeDtypeS...  1.75 us

profile of v4, /device:TPU:0, one launch (start us, length us, event | category | flops | bytes accessed | tf_op | source)
XLA Modules:
  0.0 70.1 jit_solution(1871666041005686606)
XLA Ops:
  0.6 1.8 %begin.1 = (f32[8,4,16,128]{3,2,1,0:T(8,128)S(1)}, f32[16,1024]{1,0:T(8,128)S(1)}, s32[1,2048]{1,0:T(1,128)S(1)}, s32[1,2048]{1,0:T(1,128)S(1)}, s32[16,128]{1,0...) custom-call(f32[15,1024]{1,0:T(8,128)} %right.1, f32[15,15,1024]{2,1,0:T(8,128)} %precond.1, ...), custom_call_target="tpu_custom_call" | custom-call | tf_op jit(solution)/shard_map/begin/pallas_call | solution.py:396
  2.4 17.7 %all_to_all.20.got = f32[32,16,128]{2,1,0:T(8,128)S(1)} all-to-all(f32[32,16,128]{2,1,0:T(8,128)S(1)} %bitcast.8), channel_id=1, replica_groups=mesh['tm'=8,'clus'=4] {'tm','clus'}, dimensions={0} | all-to-all | bytes 524288 | tf_op jit(solution)/shard_map/all_to_all | solution.py:365
  20.1 0.0 copy-start.1
  20.1 0.0 copy-start.3
  20.1 0.0 copy-start.4
  20.1 0.0 copy-start.2
  20.1 5.3 %group.2 = (f32[32,16,128]{2,1,0:T(8,128)S(1)}, f32[16,1024]{1,0:T(8,128)S(1)}, f32[1,128]{1,0:T(1,128)S(1)}) custom-call(f32[32,16,128]{2,1,0:T(8,128)S(1)} %all_to_all.20.got, f32[16,1024]{1,0:T(8,128)S(1)} %get-tuple-element.22.scaled.first, s32[1,2048]{1,0:T(1,128)S(1)} %get-tuple-element.23.refs_0_, s32[1,2048]{1,0:T(1,128)S(1)} %get-tuple-element.24.refs_1_, ...), custom_call_target="tpu_custom_call" | custom-call | tf_op jit(solution)/shard_map/group/pallas_call | solution.py:387
  25.5 0.0 copy-start
  25.5 12.8 %all_to_all.21.got = f32[32,16,128]{2,1,0:T(8,128)S(1)} all-to-all(f32[32,16,128]{2,1,0:T(8,128)S(1)} %get-tuple-element.29), channel_id=1, replica_groups=mesh['tm'=8,'clus'=4] {'tm','clus'}, dimensions={0} | all-to-all | bytes 524288 | tf_op jit(solution)/shard_map/all_to_all | solution.py:365
  38.3 0.0 copy-done.1
  38.3 0.0 copy-done.3
  38.3 0.0 copy-done.4
  38.3 0.7 step.1
  39.0 12.8 %all_to_all.22.got = f32[32,16,128]{2,1,0:T(8,128)S(1)} all-to-all(f32[32,16,128]{2,1,0:T(8,128)S(1)} %bitcast.9), channel_id=1, replica_groups=mesh['tm'=8,'clus'=4] {'tm','clus'}, dimensions={0} | all-to-all | bytes 524288 | tf_op jit(solution)/shard_map/all_to_all | solution.py:365
  51.8 0.0 copy-done.2
  51.8 0.0 copy-done
  51.8 4.5 %group.3 = (f32[32,16,128]{2,1,0:T(8,128)S(1)}, f32[16,1024]{1,0:T(8,128)S(1)}, f32[1,128]{1,0:T(1,128)S(1)}) custom-call(f32[32,16,128]{2,1,0:T(8,128)S(1)} %all_to_all.22.got, f32[16,1024]{1,0:T(8,128)S(1)} %get-tuple-element.33.scaled, s32[1,2048]{1,0:T(1,128)S(1)} %get-tuple-element.23.refs_0_, s32[1,2048]{1,0:T(1,128)S(1)} %get-tuple-element.24.refs_1_, ...), custom_call_target="tpu_custom_call" | custom-call | tf_op jit(solution)/shard_map/group/pallas_call | solution.py:387
  56.4 12.8 %all_to_all.23.got = f32[32,16,128]{2,1,0:T(8,128)S(1)} all-to-all(f32[32,16,128]{2,1,0:T(8,128)S(1)} %get-tuple-element.34), channel_id=1, replica_groups=mesh['tm'=8,'clus'=4] {'tm','clus'}, dimensions={0} | all-to-all | bytes 524288 | tf_op jit(solution)/shard_map/all_to_all | solution.py:365
  69.2 0.9 %end.1 = (f32[15,1024]{1,0:T(8,128)}, f32[15,1024]{1,0:T(8,128)}) custom-call(f32[32,16,128]{2,1,0:T(8,128)S(1)} %all_to_all.23.got, f32[15,1024]{1,0:T(8,128)S(1)} %get-tuple-element.35.residual, f32[16,1024]{1,0:T(8,128)S(1)} %get-tuple-element.36.inertial, s32[1,1024]{1,0:T(1,128)S(1)} %bitcast.12, f32[16,1024]{1,0:T(8,128)S(1)} %get-tuple-element.22.scaled.first, ...), custom_call_target="tpu_custom_call" | custom-call | tf_op jit(solution)/shard_map/end/pallas_call | solution.py:420
Async XLA Ops:
  20.1 18.2 %copy-start.1 = (f32[15,15,1024]{2,1,0:T(8,128)S(1)}, f32[15,15,1024]{2,1,0:T(8,128)}, u32[]{:S(2)}) copy-start(f32[15,15,1024]{2,1,0:T(8,128)} %precond.1) | copy-start | bytes 2764804
  20.1 18.2 %copy-start.3 = (f32[15,1024]{1,0:T(8,128)S(1)}, f32[15,1024]{1,0:T(8,128)}, u32[]{:S(2)}) copy-start(f32[15,1024]{1,0:T(8,128)} %right.1) | copy-start | bytes 184324
  20.1 18.2 %copy-start.4 = (s32[1024]{0:T(1024)S(1)}, s32[1024]{0:T(1024)}, u32[]{:S(2)}) copy-start(s32[1024]{0:T(1024)} %param.12) | copy-start | bytes 12292
  20.1 31.7 %copy-start.2 = (f32[15,15,1024]{2,1,0:T(8,128)S(1)}, f32[15,15,1024]{2,1,0:T(8,128)}, u32[]{:S(2)}) copy-start(f32[15,15,1024]{2,1,0:T(8,128)} %refs_7_.3) | copy-start | bytes 2764804
  25.5 26.3 %copy-start = (f32[15,15,1,2048]{3,2,1,0:T(1,128)S(1)}, f32[15,15,1,2048]{3,2,1,0:T(1,128)}, u32[]{:S(2)}) copy-start(f32[15,15,1,2048]{3,2,1,0:T(1,128)} %param.17) | copy-start | bytes 5529604

commit v5 on v4

--- a/solution.py
+++ b/solution.py
@@ -88,7 +88,7 @@
 
 def send_states(scaled, dot, slot, hot, left, send, state):
     width = scaled.shape[1]
-    groups, copies, _, share = send.shape
+    share = send.shape[2]
     parts = width // SUB
     for start in range(0, width, SUB):
         at = slice(start, start + SUB)
@@ -107,8 +107,7 @@
         piece = moved[k * ROWS : (k + 1) * ROWS]
         for m in range(SUB // share):
             one = jnp.where(sub == state, notes[:, :share], piece[:, m * share : (m + 1) * share])
-            for copy in range(copies):
-                send[k * (SUB // share) + m, copy] = one
+            send[k * (SUB // share) + m] = one
 
 
 def begin_kernel(right_in, precond_in, slot_in, *refs):
@@ -145,15 +144,9 @@
     inputs, (send, inertial, sums), refs = refs[:8], refs[8:11], refs[11:]
     field, hot, values, left, errors = refs[:5]
     if staged:
-        places, sems = refs[5:7], refs[7]
-        copies = fetch(sems, *zip(inputs[6:], places))
-        inputs = inputs[:6] + places
-
-    def arrived(which):
-        if staged:
-            copies[which].wait()
-
-    heads, tails, heads_tile, tails_tile, cluster, damping, blocks, transition = inputs
+        (copy,) = fetch(refs[6], (inputs[7], refs[5]))
+        inputs = inputs[:7] + (refs[5],)
+    heads, tails, heads_tile, tails_tile, cluster, damping, transition, blocks = inputs
     state = transition.shape[0]
     width = scaled.shape[1]
     share = got.shape[2]
@@ -172,7 +165,7 @@
     sums[...] = jnp.sum(got[:, state : state + 1, :], axis=0)
 
     for r in range(rows_of):
-        field[r] = join([got[source(r * (LANE // share) + m)] for m in range(LANE // share)])
+        field[r] = join([got[r * (LANE // share) + m] for m in range(LANE // share)])
 
     def pull(ends, h):
         index = ends[h : h + 8, :]
@@ -198,12 +191,11 @@
             left[k * 2 * ROWS + ROWS : (k + 1) * 2 * ROWS, at] = masked(part, k, low)
 
     squares = jnp.zeros((8, LANE), F32)
-    summed = []
     for h in range(0, chunks, 8):
         far = pull(tails_tile, h)
         near = pull(heads_tile, h)
-        if h == 0:
-            arrived(0)
+        if staged and h == 0:
+            copy.wait()
         back = [None] * state
         for i in range(state):
             row = [blocks[i * state + j, h : h + 8, :] for j in range(state)]
@@ -219,16 +211,13 @@
         for j in range(state, ROWS):
             values[pl.ds(h * ROWS + j, 8, stride=ROWS), :] = jnp.zeros((8, LANE), F32)
             values[pl.ds((chunks + h) * ROWS + j, 8, stride=ROWS), :] = jnp.zeros((8, LANE), F32)
-        first, final = h * LANE // SUB, (h + 8) * LANE // SUB
-        for base, ends in ((0, heads), (chunks, tails)):
-            for n in range(first, final):
-                spread(ends, base, n)
-            at = slice(base * LANE + first * SUB, base * LANE + final * SUB)
-            summed.append(both(left[:, at], hot[:, at], ((1,), (1,))))
-    summed = functools.reduce(lambda one, other: one + other, summed)
-
-    arrived(1)
-    following = row_to_column(got[jnp.minimum(flat + 1, devices - 1), state : state + 1, :], state)
+    for n in range(pairs // SUB):
+        spread(heads, 0, n)
+        spread(tails, chunks, n)
+    summed = both(left[...], hot[...], ((1,), (1,)))
+
+    after = jnp.minimum(flat + 1, devices - 1)
+    following = row_to_column(got[(after % n_clus) * n_time + after // n_clus, state : state + 1, :], state)
     lane = iota((ROWS, width), 1)
     errors[...] = jnp.where(lane == width - 1, following, pltpu.roll(scaled[...], width - 1, 1))
     for i in range(state):
@@ -258,7 +247,7 @@
             piece = k * per_part + m
             c, t = piece // n_time, piece % n_time
             here = jnp.where(clus_at == c, lam[:, t * share : (t + 1) * share], 0.0)
-            states = jnp.where(sub < state, got[source(piece)], 0.0)
+            states = jnp.where(sub < state, got[piece], 0.0)
             extra = here * states
             damped = damped + extra * states
             send[source(piece)] = one[:, m * share : (m + 1) * share] + extra
@@ -354,7 +343,7 @@
         return jax.ShapeDtypeStruct(shape, F32)
 
     message = like(devices, ROWS, share)
-    outgoing = like(n_time, n_clus, ROWS, share)
+    outgoing = like(n_time, ROWS, share)
     row = like(1, share)
     tile = like(ROWS, width)
     hot = pltpu.VMEM((SUB, width), BF16)
@@ -370,7 +359,10 @@
     in_hbm = pl.BlockSpec(memory_space=pltpu.HBM)
     dense = (pairs // LANE, LANE)
     small = (pair_first, pair_second, pair_first.reshape(dense), pair_second.reshape(dense), cluster_id, damping)
-    large = (blocks, transition)
+
+    def collect(sent):
+        own = lax.all_to_all(sent, "tm", split_axis=0, concat_axis=0, tiled=True)
+        return lax.all_gather(own, "clus", axis=0, tiled=True)
 
     def grouped(got, scaled, staged):
         in_vmem = pl.BlockSpec(memory_space=pltpu.VMEM)
@@ -382,16 +374,15 @@
             pltpu.VMEM((ROWS, width), F32),
         ]
         if staged:
-            scratch += [pltpu.VMEM(array.shape, array.dtype) for array in large]
-            scratch += [pltpu.SemaphoreType.DMA((len(large),))]
+            scratch += [pltpu.VMEM(blocks.shape, F32), pltpu.SemaphoreType.DMA((1,))]
         return pl.pallas_call(
             functools.partial(group_kernel, n_time, n_clus, axes, staged),
             out_shape=(message, tile, row),
-            in_specs=[in_vmem] * (2 + len(small)) + [in_hbm if staged else in_vmem] * len(large),
+            in_specs=[in_vmem] * (3 + len(small)) + [in_hbm if staged else in_vmem],
             scratch_shapes=scratch,
             compiler_params=params,
             name="group",
-        )(got, scaled, *carried, *(held(*large) if staged else large))
+        )(got, scaled, *carried, transition, *(held(blocks) if staged else [blocks]))
 
     sent, first, *carried = pl.pallas_call(
         begin_kernel,
@@ -408,7 +399,7 @@
         compiler_params=params,
         name="begin",
     )(*held(right_side, precond, slot, *small))
-    back, inertial, sums = grouped(exchange(sent), first, True)
+    back, inertial, sums = grouped(collect(sent), first, True)
     sent, scaled, residual, along, scalars = pl.pallas_call(
         functools.partial(step_kernel, n_time, n_clus, axes),
         out_shape=(outgoing, tile, like(state, width), tile, like(1, LANE)),
@@ -416,7 +407,7 @@
         compiler_params=params,
         name="step",
     )(exchange(back), right_side, inertial, precond, slot, sums)
-    back, inertial, sums_next = grouped(exchange(sent), scaled, False)
+    back, inertial, sums_next = grouped(collect(sent), scaled, False)
     return pl.pallas_call(
         functools.partial(end_kernel, n_time, n_clus, axes),
         out_shape=(like(state, width), like(state, width)),

time: 70.3 us -> 71.9 us (1.023)
  blocking collectives: 56.1 us -> 59.9 us
  Pallas kernels: 13.3 us -> 11 us
    all_to_all x4 -> x2, blocking collectives: 56.1 us -> 24.8 us  [exchange(): lax.all_to_all(sent.reshape(devices, ROWS, share), axes, split_axis=0, co...]
    all_to_all x0 -> x2, blocking collectives: none -> 23.5 us  [collect(): own = lax.all_to_all(sent, 'tm', split_axis=0, concat_axis=0, tiled=True)]
    all_gather x0 -> x2, blocking collectives: none -> 11.5 us  [collect(): return lax.all_gather(own, 'clus', axis=0, tiled=True)]
    pallas_call x2, Pallas kernels: 9.89 us -> 7.52 us  [grouped(): pl.pallas_call(functools.partial(group_kernel, n_time, n_clus, axes, stag...]
where the time goes in v5:
time: 71.9 us; the launch traced here: 71.6 us
  blocking collectives  59.9 us (83%)
  Pallas kernels  11 us (15%)
    all_to_all x2, blocking collectives, exchange(): lax.all_to_all(sent.reshape(devices, ROWS, share), axes, split_axis=0, co...  24.8 us
    all_to_all x2, blocking collectives, collect(): own = lax.all_to_all(sent, 'tm', split_axis=0, concat_axis=0, tiled=True)  23.5 us
    all_gather x2, blocking collectives, collect(): return lax.all_gather(own, 'clus', axis=0, tiled=True)  11.5 us
    pallas_call x2, Pallas kernels, grouped(): pl.pallas_call(functools.partial(group_kernel, n_time, n_clus, axes, stag...  7.52 us
    pallas_call x1, Pallas kernels, on_device(): pl.pallas_call(begin_kernel, out_shape=(outgoing, tile, *(jax.ShapeDtypeS...  1.83 us

profile of v5, /device:TPU:0, one launch (start us, length us, event | category | flops | bytes accessed | tf_op | source)
XLA Modules:
  0.0 71.6 jit_solution(5513232793236216415)
XLA Ops:
  0.6 0.0 copy-start.2
  0.6 1.8 %begin.1 = (f32[8,16,128]{2,1,0:T(8,128)S(1)}, f32[16,1024]{1,0:T(8,128)S(1)}, s32[1,2048]{1,0:T(1,128)S(1)}, s32[1,2048]{1,0:T(1,128)S(1)}, s32[16,128]{1,0:T(8...) custom-call(f32[15,1024]{1,0:T(8,128)} %right.1, f32[15,15,1024]{2,1,0:T(8,128)} %precond.1, ...), custom_call_target="tpu_custom_call" | custom-call | tf_op jit(solution)/shard_map/begin/pallas_call | solution.py:387
  2.5 14.0 %all_to_all.20 = f32[8,16,128]{2,1,0:T(8,128)S(1)} all-to-all(f32[8,16,128]{2,1,0:T(8,128)S(1)} %get-tuple-element.21), channel_id=1, replica_groups=mesh['tm'=8,'clus'=4] {'tm'}, dimensions={0} | all-to-all | bytes 131072 | tf_op jit(solution)/shard_map/all_to_all | solution.py:364
  16.5 5.8 %all_gather.6.got = f32[32,16,128]{2,1,0:T(8,128)S(1)} all-gather(f32[8,16,128]{2,1,0:T(8,128)S(1)} %all_to_all.20), channel_id=1, replica_groups=mesh['tm'=8,'clus'=4] {'clus'}, dimensions={0}, use_global_device_ids=true | all-gather | bytes 327680 | tf_op jit(solution)/shard_map/all_gather | solution.py:365
  22.2 0.0 copy-done.2
  22.2 0.0 copy-start.1
  22.2 0.0 copy-start.3
  22.2 0.0 copy-start.4
  22.3 4.0 %group.2 = (f32[32,16,128]{2,1,0:T(8,128)S(1)}, f32[16,1024]{1,0:T(8,128)S(1)}, f32[1,128]{1,0:T(1,128)S(1)}) custom-call(f32[32,16,128]{2,1,0:T(8,128)S(1)} %all_gather.6.got, f32[16,1024]{1,0:T(8,128)S(1)} %get-tuple-element.22.scaled.first, s32[1,2048]{1,0:T(1,128)S(1)} %get-tuple-element.23.refs_0_, s32[1,2048]{1,0:T(1,128)S(1)} %get-tuple-element.24.refs_1_, ...), custom_call_target="tpu_custom_call" | custom-call | tf_op jit(solution)/shard_map/group/pallas_call | solution.py:378
  26.2 0.0 copy-start
  26.2 12.5 %all_to_all.21.got = f32[32,16,128]{2,1,0:T(8,128)S(1)} all-to-all(f32[32,16,128]{2,1,0:T(8,128)S(1)} %get-tuple-element.29), channel_id=1, replica_groups=mesh['tm'=8,'clus'=4] {'tm','clus'}, dimensions={0} | all-to-all | bytes 524288 | tf_op jit(solution)/shard_map/all_to_all | solution.py:354
  38.8 0.0 copy-done.1
  38.8 0.0 copy-done.3
  38.8 0.0 copy-done.4
  38.8 0.7 step.1
  39.5 9.5 %all_to_all.22 = f32[8,16,128]{2,1,0:T(8,128)S(1)} all-to-all(f32[8,16,128]{2,1,0:T(8,128)S(1)} %get-tuple-element.32), channel_id=1, replica_groups=mesh['tm'=8,'clus'=4] {'tm'}, dimensions={0} | all-to-all | bytes 131072 | tf_op jit(solution)/shard_map/all_to_all | solution.py:364
  49.0 5.8 %all_gather.7.got = f32[32,16,128]{2,1,0:T(8,128)S(1)} all-gather(f32[8,16,128]{2,1,0:T(8,128)S(1)} %all_to_all.22), channel_id=1, replica_groups=mesh['tm'=8,'clus'=4] {'clus'}, dimensions={0}, use_global_device_ids=true | all-gather | bytes 327680 | tf_op jit(solution)/shard_map/all_gather | solution.py:365
  54.7 0.0 copy-done
  54.7 3.6 %group.3 = (f32[32,16,128]{2,1,0:T(8,128)S(1)}, f32[16,1024]{1,0:T(8,128)S(1)}, f32[1,128]{1,0:T(1,128)S(1)}) custom-call(f32[32,16,128]{2,1,0:T(8,128)S(1)} %all_gather.7.got, f32[16,1024]{1,0:T(8,128)S(1)} %get-tuple-element.33.scaled, s32[1,2048]{1,0:T(1,128)S(1)} %get-tuple-element.23.refs_0_, s32[1,2048]{1,0:T(1,128)S(1)} %get-tuple-element.24.refs_1_, ...), custom_call_target="tpu_custom_call" | custom-call | tf_op jit(solution)/shard_map/group/pallas_call | solution.py:378
  58.3 12.3 %all_to_all.23.got = f32[32,16,128]{2,1,0:T(8,128)S(1)} all-to-all(f32[32,16,128]{2,1,0:T(8,128)S(1)} %get-tuple-element.34), channel_id=1, replica_groups=mesh['tm'=8,'clus'=4] {'tm','clus'}, dimensions={0} | all-to-all | bytes 524288 | tf_op jit(solution)/shard_map/all_to_all | solution.py:354
  70.6 0.9 %end.1 = (f32[15,1024]{1,0:T(8,128)}, f32[15,1024]{1,0:T(8,128)}) custom-call(f32[32,16,128]{2,1,0:T(8,128)S(1)} %all_to_all.23.got, f32[15,1024]{1,0:T(8,128)S(1)} %get-tuple-element.35.residual, f32[16,1024]{1,0:T(8,128)S(1)} %get-tuple-element.36.inertial, s32[1,1024]{1,0:T(1,128)S(1)} %bitcast.8, f32[16,1024]{1,0:T(8,128)S(1)} %get-tuple-element.22.scaled.first, ...), custom_call_target="tpu_custom_call" | custom-call | tf_op jit(solution)/shard_map/end/pallas_call | solution.py:411
Async XLA Ops:
  0.6 21.6 %copy-start.2 = (f32[15,15,1024]{2,1,0:T(8,128)S(1)}, f32[15,15,1024]{2,1,0:T(8,128)}, u32[]{:S(2)}) copy-start(f32[15,15,1024]{2,1,0:T(8,128)} %refs_6_.3) | copy-start | bytes 2764804
  22.2 16.5 %copy-start.1 = (f32[15,15,1024]{2,1,0:T(8,128)S(1)}, f32[15,15,1024]{2,1,0:T(8,128)}, u32[]{:S(2)}) copy-start(f32[15,15,1024]{2,1,0:T(8,128)} %precond.1) | copy-start | bytes 2764804
  22.2 16.5 %copy-start.3 = (f32[15,1024]{1,0:T(8,128)S(1)}, f32[15,1024]{1,0:T(8,128)}, u32[]{:S(2)}) copy-start(f32[15,1024]{1,0:T(8,128)} %right.1) | copy-start | bytes 184324
  22.2 16.5 %copy-start.4 = (s32[1024]{0:T(1024)S(1)}, s32[1024]{0:T(1024)}, u32[]{:S(2)}) copy-start(s32[1024]{0:T(1024)} %param.12) | copy-start | bytes 12292
  26.2 28.5 %copy-start = (f32[15,15,1,2048]{3,2,1,0:T(1,128)S(1)}, f32[15,15,1,2048]{3,2,1,0:T(1,128)}, u32[]{:S(2)}) copy-start(f32[15,15,1,2048]{3,2,1,0:T(1,128)} %param.17) | copy-start | bytes 5529604

commit v6 on v5

--- a/solution.py
+++ b/solution.py
@@ -88,7 +88,7 @@
 
 def send_states(scaled, dot, slot, hot, left, send, state):
     width = scaled.shape[1]
-    share = send.shape[2]
+    groups, copies, _, share = send.shape
     parts = width // SUB
     for start in range(0, width, SUB):
         at = slice(start, start + SUB)
@@ -107,7 +107,8 @@
         piece = moved[k * ROWS : (k + 1) * ROWS]
         for m in range(SUB // share):
             one = jnp.where(sub == state, notes[:, :share], piece[:, m * share : (m + 1) * share])
-            send[k * (SUB // share) + m] = one
+            for copy in range(copies):
+                send[k * (SUB // share) + m, copy] = one
 
 
 def begin_kernel(right_in, precond_in, slot_in, *refs):
@@ -140,21 +141,77 @@
     return back
 
 
-def group_kernel(n_time, n_clus, axes, staged, got, scaled, *refs):
-    inputs, (send, inertial, sums), refs = refs[:8], refs[8:11], refs[11:]
-    field, hot, values, left, errors = refs[:5]
-    if staged:
-        (copy,) = fetch(refs[6], (inputs[7], refs[5]))
-        inputs = inputs[:7] + (refs[5],)
-    heads, tails, heads_tile, tails_tile, cluster, damping, transition, blocks = inputs
+def pull(ends, h, field, parity, state, found_before):
+    index = ends[h : h + 8, :]
+    low, part = index & (LANE - 1), index >> 7
+    out = list(found_before)
+    half, tiles = field.shape[0], field.shape[1]
+    for i in range(half):
+        for r in range(tiles):
+            here = part == (2 * i + parity) * tiles + r
+            for c in range(state):
+                from_row = jnp.broadcast_to(field[i, r, c : c + 1, :], (8, LANE))
+                out[c] = jnp.where(here, jnp.take_along_axis(from_row, low, axis=1), out[c])
+    return out
+
+
+def fill(field, got):
+    half, tiles = field.shape[0], field.shape[1]
+    per = LANE // got.shape[2]
+    for i in range(half):
+        for r in range(tiles):
+            field[i, r] = join([got[(r * per + m) * half + i] for m in range(per)])
+
+
+def half_kernel(axes, once, got, heads_tile, tails_tile, scaled, transition, *refs):
     state = transition.shape[0]
     width = scaled.shape[1]
+    chunks = heads_tile.shape[0]
+    if once:
+        heads, tails, cluster, damping, blocks_in = refs[:5]
+        pulled, errors, inertial, hot, lam, blocks, field, sems = refs[5:]
+        (copy,) = fetch(sems, (blocks_in, blocks))
+    else:
+        pulled, errors, inertial, field = refs
+    fill(field, got)
+    parity = lax.axis_index(axes[1]) % 2
+    zero = [jnp.zeros((8, LANE), F32)] * state
+    for h in range(0, chunks, 8):
+        for which, ends in enumerate((heads_tile, tails_tile)):
+            for c, value in enumerate(pull(ends, h, field, parity, state, zero)):
+                pulled[which * state + c, h : h + 8, :] = value
+    lane = iota((ROWS, width), 1)
+    errors[...] = jnp.where(lane == width - 1, 0.0, pltpu.roll(scaled[...], width - 1, 1))
+    for i in range(state):
+        moved = jnp.sum(transition[i] * scaled[0:state, :], axis=0, keepdims=True)
+        errors[i : i + 1, :] = errors[i : i + 1, :] - moved
+    prior = jnp.where(lane == 0, 0.0, pltpu.roll(errors[...], 1, 1))
+    inertial[state:ROWS, :] = jnp.zeros((ROWS - state, width), F32)
+    for start in range(0, width - LANE, LANE):
+        at = slice(start, start + LANE)
+        inertial[0:state, at] = prior[0:state, at] - back_product(transition, errors, at)
+    inertial[0:state, width - LANE :] = prior[0:state, width - LANE :]
+    if once:
+        pairs = heads.shape[1]
+        hot_table(hot.at[:, 0:pairs], heads, pairs)
+        hot_table(hot.at[:, pairs:], tails, pairs)
+        row = jnp.zeros(lam.shape, F32)
+        for label in range(damping.shape[1]):
+            row = jnp.where(cluster[...] == label, damping[0:1, label : label + 1], row)
+        lam[...] = row
+        copy.wait()
+
+
+def group_kernel(n_time, n_clus, axes, got, other, pulled, heads, tails, heads_tile, tails_tile, hot, lam, blocks,
+                 errors, partial, transition, send, inertial, sums, field, values, left, last):
+    state = transition.shape[0]
+    width = errors.shape[1]
     share = got.shape[2]
     pairs = heads.shape[1]
     parts = n_clus * width // SUB
-    rows_of = n_clus * width // LANE
     per_part = SUB // share
     chunks = pairs // LANE
+    half = n_clus // 2
     time_at, clus_at = lax.axis_index(axes[0]), lax.axis_index(axes[1])
     flat = time_at * n_clus + clus_at
     devices = n_time * n_clus
@@ -162,28 +219,13 @@
     def source(piece):
         return (piece % n_time) * n_clus + piece // n_time
 
-    sums[...] = jnp.sum(got[:, state : state + 1, :], axis=0)
-
-    for r in range(rows_of):
-        field[r] = join([got[r * (LANE // share) + m] for m in range(LANE // share)])
-
-    def pull(ends, h):
-        index = ends[h : h + 8, :]
-        low, part = index & (LANE - 1), index >> 7
-        out = [None] * state
-        for r in range(rows_of):
-            here = part == r
-            for c in range(state):
-                from_row = jnp.broadcast_to(field[r, c : c + 1, :], (8, LANE))
-                found = jnp.take_along_axis(from_row, low, axis=1)
-                out[c] = found if r == 0 else jnp.where(here, found, out[c])
-        return out
+    sums[...] = jnp.sum(got[:, state : state + 1, :], axis=0) + jnp.sum(other[:, state : state + 1, :], axis=0)
+    fill(field, other)
+    parity = 1 - clus_at % 2
 
     def spread(ends, base, n):
         at = slice(base * LANE + n * SUB, base * LANE + (n + 1) * SUB)
-        index = ends[0:1, n * SUB : (n + 1) * SUB]
-        hot[:, at] = hot_tile(index)
-        part = spread_row(index >> 8, ROWS)
+        part = spread_row(ends[0:1, n * SUB : (n + 1) * SUB] >> 8, ROWS)
         row = (base + n * (SUB // LANE)) * ROWS
         high, low = halves(join([values[row + m * ROWS : row + (m + 1) * ROWS, :] for m in range(SUB // LANE)]))
         for k in range(parts):
@@ -192,10 +234,10 @@
 
     squares = jnp.zeros((8, LANE), F32)
     for h in range(0, chunks, 8):
-        far = pull(tails_tile, h)
-        near = pull(heads_tile, h)
-        if staged and h == 0:
-            copy.wait()
+        near, far = (
+            pull(ends, h, field, parity, state, [pulled[which * state + c, h : h + 8, :] for c in range(state)])
+            for which, ends in enumerate((heads_tile, tails_tile))
+        )
         back = [None] * state
         for i in range(state):
             row = [blocks[i * state + j, h : h + 8, :] for j in range(state)]
@@ -217,27 +259,22 @@
     summed = both(left[...], hot[...], ((1,), (1,)))
 
     after = jnp.minimum(flat + 1, devices - 1)
-    following = row_to_column(got[(after % n_clus) * n_time + after // n_clus, state : state + 1, :], state)
-    lane = iota((ROWS, width), 1)
-    errors[...] = jnp.where(lane == width - 1, following, pltpu.roll(scaled[...], width - 1, 1))
-    for i in range(state):
-        moved = jnp.sum(transition[i] * scaled[0:state, :], axis=0, keepdims=True)
-        errors[i : i + 1, :] = errors[i : i + 1, :] - moved
-    closed = (lane == width - 1) & (flat == devices - 1)
-    error = jnp.where(closed | (iota((ROWS, width), 0) >= state), 0.0, errors[...])
-    errors[...] = error
-    prior = jnp.where(lane == 0, 0.0, pltpu.roll(error, 1, 1))
-    inertial[state:ROWS, :] = jnp.zeros((ROWS - state, width), F32)
-    energy = jnp.zeros((ROWS, LANE), F32)
-    for start in range(0, width, LANE):
-        at = slice(start, start + LANE)
-        inertial[0:state, at] = prior[0:state, at] - back_product(transition, errors, at)
-        energy = energy + error[:, at] * error[:, at]
+    following = row_to_column(other[after // n_clus * half + after % n_clus // 2, state : state + 1, :], state)
+    at = slice(width - LANE, width)
+    ending = iota((ROWS, LANE), 1) == LANE - 1
+    closed = ending & (flat == devices - 1)
+    ahead = jnp.where(ending, errors[:, at] + following, errors[:, at])
+    last[...] = jnp.where(closed | (iota((ROWS, LANE), 0) >= state), 0.0, ahead)
+    energy = last[...] * last[...]
+    for start in range(0, width - LANE, LANE):
+        block = errors[:, start : start + LANE]
+        energy = energy + jnp.where(iota((ROWS, LANE), 0) < state, block * block, 0.0)
     product = total(squares) + total(energy)
-
-    lam = jnp.zeros((1, width), F32)
-    for label in range(damping.shape[1]):
-        lam = jnp.where(cluster[...] == label, damping[0:1, label : label + 1], lam)
+    inertial[...] = partial[...]
+    back = transition[0, :, at] * last[0:1, :]
+    for j in range(1, state):
+        back = back + transition[j, :, at] * last[j : j + 1, :]
+    inertial[0:state, at] = partial[0:state, at] - back
 
     sub = iota((ROWS, share), 0)
     damped = jnp.zeros((ROWS, share), F32)
@@ -247,12 +284,12 @@
             piece = k * per_part + m
             c, t = piece // n_time, piece % n_time
             here = jnp.where(clus_at == c, lam[:, t * share : (t + 1) * share], 0.0)
-            states = jnp.where(sub < state, got[piece], 0.0)
+            states = jnp.where(sub < state, got[t * half + c // 2], 0.0)
             extra = here * states
             damped = damped + extra * states
             send[source(piece)] = one[:, m * share : (m + 1) * share] + extra
     product = product + total(damped)
-    notes = note(error[:, width - 1 : width], product, state, share)
+    notes = note(last[:, LANE - 1 : LANE], product, state, share)
     for d in range(devices):
         send[d, state : state + 1, :] = notes[:, :share]
 
@@ -343,12 +380,12 @@
         return jax.ShapeDtypeStruct(shape, F32)
 
     message = like(devices, ROWS, share)
-    outgoing = like(n_time, ROWS, share)
+    outgoing = like(n_time, n_clus // 2, ROWS, share)
     row = like(1, share)
     tile = like(ROWS, width)
     hot = pltpu.VMEM((SUB, width), BF16)
     left = pltpu.VMEM((ROWS * width // SUB, 2 * width), BF16)
-    field = pltpu.VMEM((ROWS * width // SUB, 2 * SUB), BF16)
+    terms = pltpu.VMEM((ROWS * width // SUB, 2 * SUB), BF16)
 
     def exchange(sent):
         return lax.all_to_all(sent.reshape(devices, ROWS, share), axes, split_axis=0, concat_axis=0, tiled=True)
@@ -357,32 +394,48 @@
         return tuple(pltpu.with_memory_space_constraint(array, pltpu.HBM) for array in arrays)
 
     in_hbm = pl.BlockSpec(memory_space=pltpu.HBM)
+    in_vmem = pl.BlockSpec(memory_space=pltpu.VMEM)
     dense = (pairs // LANE, LANE)
     small = (pair_first, pair_second, pair_first.reshape(dense), pair_second.reshape(dense), cluster_id, damping)
+    same = [[t * n_clus + c for t in range(n_time) for c in range(q, n_clus, 2)] for q in range(2)]
+    field = pltpu.VMEM((n_clus // 2, width // LANE, ROWS, LANE), F32)
 
     def collect(sent):
-        own = lax.all_to_all(sent, "tm", split_axis=0, concat_axis=0, tiled=True)
-        return lax.all_gather(own, "clus", axis=0, tiled=True)
-
-    def grouped(got, scaled, staged):
-        in_vmem = pl.BlockSpec(memory_space=pltpu.VMEM)
-        scratch = [
-            pltpu.VMEM((positions // LANE, ROWS, LANE), F32),
-            pltpu.VMEM((SUB, 2 * pairs), BF16),
-            pltpu.VMEM((2 * pairs // LANE * ROWS, LANE), F32),
-            pltpu.VMEM((2 * ROWS * positions // SUB, 2 * pairs), BF16),
-            pltpu.VMEM((ROWS, width), F32),
-        ]
-        if staged:
-            scratch += [pltpu.VMEM(blocks.shape, F32), pltpu.SemaphoreType.DMA((1,))]
-        return pl.pallas_call(
-            functools.partial(group_kernel, n_time, n_clus, axes, staged),
-            out_shape=(message, tile, row),
-            in_specs=[in_vmem] * (3 + len(small)) + [in_hbm if staged else in_vmem],
+        sent = sent.reshape(devices // 2, ROWS, share)
+        got = lax.all_to_all(sent, axes, split_axis=0, concat_axis=0, tiled=True, axis_index_groups=same)
+        return got, lax.ppermute(got, "clus", [(c, c ^ 1) for c in range(n_clus)])
+
+    def grouped(sent, scaled, carried, tables):
+        got, other = collect(sent)
+        heads, tails, heads_tile, tails_tile, cluster, lam_of = carried
+        shapes = (like(2 * state, *dense), tile, tile)
+        operands = (got, heads_tile, tails_tile, scaled, transition)
+        scratch = [field]
+        if not tables:
+            shapes += (jax.ShapeDtypeStruct((SUB, 2 * pairs), BF16), like(1, width), like(*blocks.shape))
+            operands += (heads, tails, cluster, lam_of, *held(blocks))
+            scratch += [pltpu.SemaphoreType.DMA((1,))]
+        pulled, errors, partial, *fresh = pl.pallas_call(
+            functools.partial(half_kernel, axes, not tables),
+            out_shape=shapes,
+            in_specs=[in_vmem] * (len(operands) - 1) + [in_vmem if tables else in_hbm],
             scratch_shapes=scratch,
             compiler_params=params,
+            name="half",
+        )(*operands)
+        tables = tables or fresh
+        return tables, pl.pallas_call(
+            functools.partial(group_kernel, n_time, n_clus, axes),
+            out_shape=(message, tile, row),
+            scratch_shapes=[
+                field,
+                pltpu.VMEM((2 * pairs // LANE * ROWS, LANE), F32),
+                pltpu.VMEM((2 * ROWS * positions // SUB, 2 * pairs), BF16),
+                pltpu.VMEM((ROWS, LANE), F32),
+            ],
+            compiler_params=params,
             name="group",
-        )(got, scaled, *carried, transition, *(held(blocks) if staged else [blocks]))
+        )(got, other, pulled, heads, tails, heads_tile, tails_tile, *tables, errors, partial, transition)
 
     sent, first, *carried = pl.pallas_call(
         begin_kernel,
@@ -399,19 +452,19 @@
         compiler_params=params,
         name="begin",
     )(*held(right_side, precond, slot, *small))
-    back, inertial, sums = grouped(collect(sent), first, True)
+    tables, (back, inertial, sums) = grouped(sent, first, carried, None)
     sent, scaled, residual, along, scalars = pl.pallas_call(
         functools.partial(step_kernel, n_time, n_clus, axes),
         out_shape=(outgoing, tile, like(state, width), tile, like(1, LANE)),
-        scratch_shapes=[hot, field, left],
+        scratch_shapes=[hot, terms, left],
         compiler_params=params,
         name="step",
     )(exchange(back), right_side, inertial, precond, slot, sums)
-    back, inertial, sums_next = grouped(collect(sent), scaled, False)
+    _, (back, inertial, sums_next) = grouped(sent, scaled, carried, tables)
     return pl.pallas_call(
         functools.partial(end_kernel, n_time, n_clus, axes),
         out_shape=(like(state, width), like(state, width)),
-        scratch_shapes=[hot, field, pltpu.VMEM((ROWS, width), F32)],
+        scratch_shapes=[hot, terms, pltpu.VMEM((ROWS, width), F32)],
         compiler_params=params,
         name="end",
     )(exchange(back), residual, inertial, slot, first, scaled, along, sums, sums_next, scalars)

time: 71.9 us -> 65.8 us (0.915)
  blocking collectives: 59.9 us -> 51.6 us
  Pallas kernels: 11 us -> 13.2 us
    all_gather x2 -> x0, blocking collectives: 11.5 us -> none  [collect(): return lax.all_gather(own, 'clus', axis=0, tiled=True)]
    all_to_all x2, blocking collectives: 23.5 us -> 26.9 us  [collect(): lax.all_to_all(sent, axes, split_axis=0, concat_axis=0, tiled=True, axis_...]
    pallas_call x2 -> x4, Pallas kernels: 7.52 us -> 9.75 us  [the longest x2 5.2 us: grouped(): pl.pallas_call(functools.partial(group_kernel, n_time, n_clus, axes), out...]
  transfers between devices with their start and end apart: 0 -> 2, of which waited for: 0 -> 0; matrix products, arithmetic and copies ran while one was open for 0% -> 0% of each run, Pallas kernels for 0% -> 7%
where the time goes in v6:
time: 65.8 us; the launch traced here: 65.5 us
  blocking collectives  51.6 us (78%)
  Pallas kernels  13.2 us (20%)
  between operations  0.72 us (1%)
    all_to_all x2, blocking collectives, collect(): lax.all_to_all(sent, axes, split_axis=0, concat_axis=0, tiled=True, axis_...  26.9 us
    all_to_all x2, blocking collectives, exchange(): lax.all_to_all(sent.reshape(devices, ROWS, share), axes, split_axis=0, co...  24.6 us
    pallas_call x2, Pallas kernels, grouped(): pl.pallas_call(functools.partial(group_kernel, n_time, n_clus, axes), out...  5.2 us
    pallas_call x2, Pallas kernels, grouped(): pl.pallas_call(functools.partial(half_kernel, axes, not tables), out_shap...  4.55 us
    pallas_call x1, Pallas kernels, on_device(): pl.pallas_call(begin_kernel, out_shape=(outgoing, tile, *(jax.ShapeDtypeS...  1.82 us
  transfers between devices with their start and end apart: 2, of which 0 were waited for; matrix products, arithmetic and copies ran while one was open for 0% of the time, Pallas kernels for 7%

profile of v6, /device:TPU:0, one launch (start us, length us, event | category | flops | bytes accessed | tf_op | source)
XLA Modules:
  0.0 65.5 jit_solution(11421170252412708480)
XLA Ops:
  0.6 0.0 copy-start
  0.6 1.8 %begin.1 = (f32[8,2,16,128]{3,2,1,0:T(8,128)S(1)}, f32[16,1024]{1,0:T(8,128)S(1)}, s32[1,2048]{1,0:T(1,128)S(1)}, s32[1,2048]{1,0:T(1,128)S(1)}, s32[16,128]{1,0...) custom-call(f32[15,1024]{1,0:T(8,128)} %right.1, f32[15,15,1024]{2,1,0:T(8,128)} %precond.1, ...), custom_call_target="tpu_custom_call" | custom-call | tf_op jit(solution)/shard_map/begin/pallas_call | solution.py:440
  2.5 15.9 %all_to_all.20.got = f32[16,16,128]{2,1,0:T(8,128)S(1)} all-to-all(f32[16,16,128]{2,1,0:T(8,128)S(1)} %bitcast.6), channel_id=1, replica_groups={{0,2,4,6,8,10,12,14,16,18,20,22,24,26,28,30},{1,3,5,7,9,11,13,15,17,19,..., dimensions={0} | all-to-all | bytes 262144 | tf_op jit(solution)/shard_map/all_to_all | solution.py:405
  18.4 0.0 collective-permute-start
  18.4 0.0 copy-done
  18.4 3.2 %half.2 = (f32[30,16,128]{2,1,0:T(8,128)S(1)}, f32[16,1024]{1,0:T(8,128)S(1)}, f32[16,1024]{1,0:T(8,128)S(1)}, bf16[256,4096]{1,0:T(8,128)(2,1)S(1)}, f32[1,1024...) custom-call(f32[16,16,128]{2,1,0:T(8,128)S(1)} %all_to_all.20.got, s32[16,128]{1,0:T(8,128)S(1)} %get-tuple-element.31.heads_tile, ...), custom_call_target="tpu_custom_call" | custom-call | tf_op jit(solution)/shard_map/half/pallas_call | solution.py:418
  21.6 0.0 collective-permute-done.other
  21.6 0.0 copy-start.1
  21.6 0.0 copy-start.2
  21.6 0.0 copy-start.3
  21.6 2.6 %group.2 = (f32[32,16,128]{2,1,0:T(8,128)S(1)}, f32[16,1024]{1,0:T(8,128)S(1)}, f32[1,128]{1,0:T(1,128)S(1)}) custom-call(f32[16,16,128]{2,1,0:T(8,128)S(1)} %all_to_all.20.got, f32[16,16,128]{2,1,0:T(8,128)S(1)} %collective-permute-done.other, f32[30,16,128]{2,1,0:T(8,128)S(1)} %get-tuple-element.38.pulled, s32[1,2048]{1,0:T(1,128)S(1)} %get-tuple-element.34.refs_0_.heads, ...), custom_call_target="tpu_custom_call" | custom-call | tf_op jit(solution)/shard_map/group/pallas_call | solution.py:427
  24.2 12.3 %all_to_all.21.got = f32[32,16,128]{2,1,0:T(8,128)S(1)} all-to-all(f32[32,16,128]{2,1,0:T(8,128)S(1)} %get-tuple-element.44), channel_id=1, replica_groups=mesh['tm'=8,'clus'=4] {'tm','clus'}, dimensions={0} | all-to-all | bytes 524288 | tf_op jit(solution)/shard_map/all_to_all | solution.py:391
  36.6 0.0 copy-done.1
  36.6 0.0 copy-done.2
  36.6 0.0 copy-done.3
  36.6 0.7 %step.1 = (f32[8,2,16,128]{3,2,1,0:T(8,128)S(1)}, f32[16,1024]{1,0:T(8,128)S(1)}, f32[15,1024]{1,0:T(8,128)S(1)}, f32[16,1024]{1,0:T(8,128)S(1)}, f32[1,128]{1,0:T(1,128)S(1)}) custom-call(f32[32,16,128]{2,1,0:T(8,128)S(1)} %all_to_all.21.got, f32[15,1024]{1,0:T(8,128)S(1)} %copy-done.2, f32[16,1024]{1,0:T(8,128)S(1)} %get-tuple-element.45.inertial, ...), custom_call_target="tpu_custom_call" | custom-call | tf_op jit(solution)/shard_map/step/pallas_call | solution.py:456
  37.3 11.0 %all_to_all.22.got = f32[16,16,128]{2,1,0:T(8,128)S(1)} all-to-all(f32[16,16,128]{2,1,0:T(8,128)S(1)} %bitcast.7), channel_id=1, replica_groups={{0,2,4,6,8,10,12,14,16,18,20,22,24,26,28,30},{1,3,5,7,9,11,13,15,17,19,..., dimensions={0} | all-to-all | bytes 262144 | tf_op jit(solution)/shard_map/all_to_all | solution.py:405
  48.3 0.0 collective-permute-start.1
  48.3 1.4 %half.3 = (f32[30,16,128]{2,1,0:T(8,128)S(1)}, f32[16,1024]{1,0:T(8,128)S(1)}, f32[16,1024]{1,0:T(8,128)S(1)}) custom-call(f32[16,16,128]{2,1,0:T(8,128)S(1)} %all_to_all.22.got, s32[16,128]{1,0:T(8,128)S(1)} %get-tuple-element.31.heads_tile, s32[16,128]{1,0:T(8,128)S(1)} %get-tuple-element.32.tails_tile, f32[16,1024]{1,0:T(8,128)S(1)} %get-tuple-element.48.scaled, ...), custom_call_target="tpu_custom_call" | custom-call | tf_op jit(solution)/shard_map/half/pallas_call | solution.py:418
  49.6 0.0 collective-permute-done.1.other
  49.6 2.6 %group.3 = (f32[32,16,128]{2,1,0:T(8,128)S(1)}, f32[16,1024]{1,0:T(8,128)S(1)}, f32[1,128]{1,0:T(1,128)S(1)}) custom-call(f32[16,16,128]{2,1,0:T(8,128)S(1)} %all_to_all.22.got, f32[16,16,128]{2,1,0:T(8,128)S(1)} %collective-permute-done.1.other, f32[30,16,128]{2,1,0:T(8,128)S(1)} %get-tuple-element.49.pulled, ...), custom_call_target="tpu_custom_call" | custom-call | tf_op jit(solution)/shard_map/group/pallas_call | solution.py:427
  52.3 12.3 %all_to_all.23.got = f32[32,16,128]{2,1,0:T(8,128)S(1)} all-to-all(f32[32,16,128]{2,1,0:T(8,128)S(1)} %get-tuple-element.52), channel_id=1, replica_groups=mesh['tm'=8,'clus'=4] {'tm','clus'}, dimensions={0} | all-to-all | bytes 524288 | tf_op jit(solution)/shard_map/all_to_all | solution.py:391
  64.6 0.9 %end.1 = (f32[15,1024]{1,0:T(8,128)}, f32[15,1024]{1,0:T(8,128)}) custom-call(f32[32,16,128]{2,1,0:T(8,128)S(1)} %all_to_all.23.got, f32[15,1024]{1,0:T(8,128)S(1)} %get-tuple-element.53.residual, f32[16,1024]{1,0:T(8,128)S(1)} %get-tuple-element.54.inertial, s32[1,1024]{1,0:T(1,128)S(1)} %bitcast.10, f32[16,1024]{1,0:T(8,128)S(1)} %get-tuple-element.33.scaled.first, ...), custom_call_target="tpu_custom_call" | custom-call | tf_op jit(solution)/shard_map/end/pallas_call | solution.py:464
Async XLA Ops:
  0.6 17.8 %copy-start = (f32[15,15,1024]{2,1,0:T(8,128)S(1)}, f32[15,15,1024]{2,1,0:T(8,128)}, u32[]{:S(2)}) copy-start(f32[15,15,1024]{2,1,0:T(8,128)} %transition.7) | copy-start | bytes 2764804
  18.4 3.2 %collective-permute-start = (f32[16,16,128]{2,1,0:T(8,128)S(1)}, f32[16,16,128]{2,1,0:T(8,128)S(1)}, u32[]{:S(2)}, u32[]{:S(2)}) collective-permute-start(f32[16,16,128]{2,1,0:T(8,128)S(1)} %all_to_all.20.got), channel_id=1, source_target_pairs={{0,1},{1,0},{2,3},{3,2},{4,5},{5,4},{6,7},{7,6},{8,9},{9,8},{10,11... | collective-permute-start | bytes 393224 | tf_op jit(solution)/shard_map/ppermute | solution.py:406
  21.6 15.0 %copy-start.1 = (f32[15,15,1024]{2,1,0:T(8,128)S(1)}, f32[15,15,1024]{2,1,0:T(8,128)}, u32[]{:S(2)}) copy-start(f32[15,15,1024]{2,1,0:T(8,128)} %precond.1) | copy-start | bytes 2764804
  21.6 15.0 %copy-start.2 = (f32[15,1024]{1,0:T(8,128)S(1)}, f32[15,1024]{1,0:T(8,128)}, u32[]{:S(2)}) copy-start(f32[15,1024]{1,0:T(8,128)} %right.1) | copy-start | bytes 184324
  21.6 15.0 %copy-start.3 = (s32[1024]{0:T(1024)S(1)}, s32[1024]{0:T(1024)}, u32[]{:S(2)}) copy-start(s32[1024]{0:T(1024)} %param.12) | copy-start | bytes 12292
  48.3 1.4 %collective-permute-start.1 = (f32[16,16,128]{2,1,0:T(8,128)S(1)}, f32[16,16,128]{2,1,0:T(8,128)S(1)}, u32[]{:S(2)}, u32[]{:S(2)}) collective-permute-start(f32[16,16,128]{2,1,0:T(8,128)S(1)} %all_to_all.22.got), channel_id=1, source_target_pairs={{0,1},{1,0},{2,3},{3,2},{4,5},{5,4},{6,7},{7,6},{8,9},{9,8},{10,11... | collective-permute-start | bytes 393224 | tf_op jit(solution)/shard_map/ppermute | solution.py:406

commit v7 on v6

--- a/solution.py
+++ b/solution.py
@@ -111,20 +111,31 @@
                 send[k * (SUB // share) + m, copy] = one
 
 
-def begin_kernel(right_in, precond_in, slot_in, *refs):
-    carried = len(refs) // 2 - 4
-    (send, scaled), (hot, left, right, precond, slot, sems) = refs[carried : carried + 2], refs[2 * carried + 2 :]
+def begin_kernel(right_in, precond_in, slot_in, heads_in, tails_in, heads_tile_in, tails_tile_in, cluster_in, damping_in,
+                 send, scaled, heads, tails, heads_tile, tails_tile, hot_pairs, lam,
+                 hot, left, right, precond, slot, cluster, damping, sems):
     state = right.shape[0]
-    copies = fetch(sems, (precond_in, precond), (right_in, right), (slot_in, slot),
-                   *zip(refs[:carried], refs[carried + 2 : 2 * carried + 2]))
+    copies = fetch(sems, (precond_in, precond), (heads_in, heads), (tails_in, tails), (slot_in, slot), (right_in, right),
+                   (cluster_in, cluster), (damping_in, damping), (heads_tile_in, heads_tile), (tails_tile_in, tails_tile))
+    pairs = heads.shape[1]
+    copies[1].wait()
+    hot_table(hot_pairs.at[:, 0:pairs], heads, pairs)
     copies[2].wait()
+    hot_table(hot_pairs.at[:, pairs:], tails, pairs)
+    copies[3].wait()
     hot_table(hot, slot, right.shape[1])
-    copies[1].wait()
+    copies[5].wait()
+    copies[6].wait()
+    row = jnp.zeros(lam.shape, F32)
+    for label in range(damping.shape[1]):
+        row = jnp.where(cluster[...] == label, damping[0:1, label : label + 1], row)
+    lam[...] = row
+    copies[4].wait()
     copies[0].wait()
     dot = apply_precond(precond, right, scaled)
     send_states(scaled, dot, slot, hot, left, send, state)
-    for copy in copies[3:]:
-        copy.wait()
+    copies[7].wait()
+    copies[8].wait()
 
 
 def fetch(sems, *pairs):
@@ -168,8 +179,7 @@
     width = scaled.shape[1]
     chunks = heads_tile.shape[0]
     if once:
-        heads, tails, cluster, damping, blocks_in = refs[:5]
-        pulled, errors, inertial, hot, lam, blocks, field, sems = refs[5:]
+        blocks_in, pulled, errors, inertial, blocks, field, sems = refs
         (copy,) = fetch(sems, (blocks_in, blocks))
     else:
         pulled, errors, inertial, field = refs
@@ -192,13 +202,6 @@
         inertial[0:state, at] = prior[0:state, at] - back_product(transition, errors, at)
     inertial[0:state, width - LANE :] = prior[0:state, width - LANE :]
     if once:
-        pairs = heads.shape[1]
-        hot_table(hot.at[:, 0:pairs], heads, pairs)
-        hot_table(hot.at[:, pairs:], tails, pairs)
-        row = jnp.zeros(lam.shape, F32)
-        for label in range(damping.shape[1]):
-            row = jnp.where(cluster[...] == label, damping[0:1, label : label + 1], row)
-        lam[...] = row
         copy.wait()
 
 
@@ -407,13 +410,13 @@
 
     def grouped(sent, scaled, carried, tables):
         got, other = collect(sent)
-        heads, tails, heads_tile, tails_tile, cluster, lam_of = carried
+        heads, tails, heads_tile, tails_tile, hot_of, lam = carried
         shapes = (like(2 * state, *dense), tile, tile)
         operands = (got, heads_tile, tails_tile, scaled, transition)
         scratch = [field]
         if not tables:
-            shapes += (jax.ShapeDtypeStruct((SUB, 2 * pairs), BF16), like(1, width), like(*blocks.shape))
-            operands += (heads, tails, cluster, lam_of, *held(blocks))
+            shapes += (like(*blocks.shape),)
+            operands += held(blocks)
             scratch += [pltpu.SemaphoreType.DMA((1,))]
         pulled, errors, partial, *fresh = pl.pallas_call(
             functools.partial(half_kernel, axes, not tables),
@@ -435,11 +438,17 @@
             ],
             compiler_params=params,
             name="group",
-        )(got, other, pulled, heads, tails, heads_tile, tails_tile, *tables, errors, partial, transition)
+        )(got, other, pulled, heads, tails, heads_tile, tails_tile, hot_of, lam, *tables, errors, partial, transition)
 
     sent, first, *carried = pl.pallas_call(
         begin_kernel,
-        out_shape=(outgoing, tile, *(jax.ShapeDtypeStruct(array.shape, array.dtype) for array in small)),
+        out_shape=(
+            outgoing,
+            tile,
+            *(jax.ShapeDtypeStruct(array.shape, array.dtype) for array in small[:4]),
+            jax.ShapeDtypeStruct((SUB, 2 * pairs), BF16),
+            like(1, width),
+        ),
         in_specs=[in_hbm] * (3 + len(small)),
         scratch_shapes=[
             hot,
@@ -447,6 +456,8 @@
             pltpu.VMEM(right_side.shape, F32),
             pltpu.VMEM(precond.shape, F32),
             pltpu.VMEM(slot.shape, jnp.int32),
+            pltpu.VMEM(cluster_id.shape, jnp.int32),
+            pltpu.VMEM(damping.shape, F32),
             pltpu.SemaphoreType.DMA((3 + len(small),)),
         ],
         compiler_params=params,

time: 65.8 us -> 64.4 us (0.979)
  Pallas kernels: 13.2 us -> 11.8 us
    pallas_call x2, Pallas kernels: 4.55 us -> 2.89 us  [grouped(): pl.pallas_call(functools.partial(half_kernel, axes, not tables), out_shap...]
  transfers between devices with their start and end apart: 2 -> 2, of which waited for: 0 -> 0; matrix products, arithmetic and copies ran while one was open for 0% -> 0% of each run, Pallas kernels for 7% -> 5%
where the time goes in v7:
time: 64.4 us; the launch traced here: 64.2 us
  blocking collectives  51.6 us (80%)
  Pallas kernels  11.8 us (18%)
  between operations  0.73 us (1%)
    all_to_all x2, blocking collectives, collect(): lax.all_to_all(sent, axes, split_axis=0, concat_axis=0, tiled=True, axis_...  26.9 us
    all_to_all x2, blocking collectives, exchange(): lax.all_to_all(sent.reshape(devices, ROWS, share), axes, split_axis=0, co...  24.6 us
    pallas_call x2, Pallas kernels, grouped(): pl.pallas_call(functools.partial(group_kernel, n_time, n_clus, axes), out...  5.19 us
    pallas_call x2, Pallas kernels, grouped(): pl.pallas_call(functools.partial(half_kernel, axes, not tables), out_shap...  2.89 us
    pallas_call x1, Pallas kernels, on_device(): pl.pallas_call(begin_kernel, out_shape=(outgoing, tile, *(jax.ShapeDtypeS...  2.12 us
  transfers between devices with their start and end apart: 2, of which 0 were waited for; matrix products, arithmetic and copies ran while one was open for 0% of the time, Pallas kernels for 5%

profile of v7, /device:TPU:0, one launch (start us, length us, event | category | flops | bytes accessed | tf_op | source)
XLA Modules:
  0.0 64.2 jit_solution(13897947932667856609)
XLA Ops:
  0.6 0.0 copy-start
  0.6 2.1 %begin.1 = (f32[8,2,16,128]{3,2,1,0:T(8,128)S(1)}, f32[16,1024]{1,0:T(8,128)S(1)}, s32[1,2048]{1,0:T(1,128)S(1)}, s32[1,2048]{1,0:T(1,128)S(1)}, s32[16,128]{1,0...) custom-call(f32[15,1024]{1,0:T(8,128)} %right.1, ...), custom_call_target="tpu_custom_call" | custom-call | tf_op jit(solution)/shard_map/begin/pallas_call | solution.py:443
  2.8 15.9 %all_to_all.20.got = f32[16,16,128]{2,1,0:T(8,128)S(1)} all-to-all(f32[16,16,128]{2,1,0:T(8,128)S(1)} %bitcast.6), channel_id=1, replica_groups={{0,2,4,6,8,10,12,14,16,18,20,22,24,26,28,30},{1,3,5,7,9,11,13,15,17,19,..., dimensions={0} | all-to-all | bytes 262144 | tf_op jit(solution)/shard_map/all_to_all | solution.py:408
  18.7 0.0 collective-permute-start
  18.7 0.0 copy-done
  18.7 1.5 %half.2 = (f32[30,16,128]{2,1,0:T(8,128)S(1)}, f32[16,1024]{1,0:T(8,128)S(1)}, f32[16,1024]{1,0:T(8,128)S(1)}, f32[225,16,128]{2,1,0:T(8,128)S(1)}) custom-call(f32[16,16,128]{2,1,0:T(8,128)S(1)} %all_to_all.20.got, s32[16,128]{1,0:T(8,128)S(1)} %get-tuple-element.29.heads_tile, s32[16,128]{1,0:T(8,128)S(1)} %get-tuple-element.30.tails_tile, ...), custom_call_target="tpu_custom_call" | custom-call | tf_op jit(solution)/shard_map/half/pallas_call | solution.py:421
  20.2 0.0 collective-permute-done.other
  20.3 0.0 copy-start.1
  20.3 0.0 copy-start.2
  20.3 0.0 copy-start.3
  20.3 2.6 %group.2 = (f32[32,16,128]{2,1,0:T(8,128)S(1)}, f32[16,1024]{1,0:T(8,128)S(1)}, f32[1,128]{1,0:T(1,128)S(1)}) custom-call(f32[16,16,128]{2,1,0:T(8,128)S(1)} %all_to_all.20.got, f32[16,16,128]{2,1,0:T(8,128)S(1)} %collective-permute-done.other, f32[30,16,128]{2,1,0:T(8,128)S(1)} %get-tuple-element.32.pulled, s32[1,2048]{1,0:T(1,128)S(1)} %get-tuple-element.33.heads, ...), custom_call_target="tpu_custom_call" | custom-call | tf_op jit(solution)/shard_map/group/pallas_call | solution.py:430
  22.9 12.3 %all_to_all.21.got = f32[32,16,128]{2,1,0:T(8,128)S(1)} all-to-all(f32[32,16,128]{2,1,0:T(8,128)S(1)} %get-tuple-element.40), channel_id=1, replica_groups=mesh['tm'=8,'clus'=4] {'tm','clus'}, dimensions={0} | all-to-all | bytes 524288 | tf_op jit(solution)/shard_map/all_to_all | solution.py:394
  35.2 0.0 copy-done.1
  35.2 0.0 copy-done.2
  35.2 0.0 copy-done.3
  35.2 0.7 %step.1 = (f32[8,2,16,128]{3,2,1,0:T(8,128)S(1)}, f32[16,1024]{1,0:T(8,128)S(1)}, f32[15,1024]{1,0:T(8,128)S(1)}, f32[16,1024]{1,0:T(8,128)S(1)}, f32[1,128]{1,0:T(1,128)S(1)}) custom-call(f32[32,16,128]{2,1,0:T(8,128)S(1)} %all_to_all.21.got, f32[15,1024]{1,0:T(8,128)S(1)} %copy-done.2, f32[16,1024]{1,0:T(8,128)S(1)} %get-tuple-element.41.inertial, ...), custom_call_target="tpu_custom_call" | custom-call | tf_op jit(solution)/shard_map/step/pallas_call | solution.py:467
  35.9 11.0 %all_to_all.22.got = f32[16,16,128]{2,1,0:T(8,128)S(1)} all-to-all(f32[16,16,128]{2,1,0:T(8,128)S(1)} %bitcast.7), channel_id=1, replica_groups={{0,2,4,6,8,10,12,14,16,18,20,22,24,26,28,30},{1,3,5,7,9,11,13,15,17,19,..., dimensions={0} | all-to-all | bytes 262144 | tf_op jit(solution)/shard_map/all_to_all | solution.py:408
  46.9 0.0 collective-permute-start.1
  46.9 1.4 %half.3 = (f32[30,16,128]{2,1,0:T(8,128)S(1)}, f32[16,1024]{1,0:T(8,128)S(1)}, f32[16,1024]{1,0:T(8,128)S(1)}) custom-call(f32[16,16,128]{2,1,0:T(8,128)S(1)} %all_to_all.22.got, s32[16,128]{1,0:T(8,128)S(1)} %get-tuple-element.29.heads_tile, s32[16,128]{1,0:T(8,128)S(1)} %get-tuple-element.30.tails_tile, f32[16,1024]{1,0:T(8,128)S(1)} %get-tuple-element.44.scaled, ...), custom_call_target="tpu_custom_call" | custom-call | tf_op jit(solution)/shard_map/half/pallas_call | solution.py:421
  48.3 0.0 collective-permute-done.1.other
  48.3 2.6 %group.3 = (f32[32,16,128]{2,1,0:T(8,128)S(1)}, f32[16,1024]{1,0:T(8,128)S(1)}, f32[1,128]{1,0:T(1,128)S(1)}) custom-call(f32[16,16,128]{2,1,0:T(8,128)S(1)} %all_to_all.22.got, f32[16,16,128]{2,1,0:T(8,128)S(1)} %collective-permute-done.1.other, f32[30,16,128]{2,1,0:T(8,128)S(1)} %get-tuple-element.45.pulled, s32[1,2048]{1,0:T(1,128)S(1)} %get-tuple-element.33.heads, ...), custom_call_target="tpu_custom_call" | custom-call | tf_op jit(solution)/shard_map/group/pallas_call | solution.py:430
  50.9 12.3 %all_to_all.23.got = f32[32,16,128]{2,1,0:T(8,128)S(1)} all-to-all(f32[32,16,128]{2,1,0:T(8,128)S(1)} %get-tuple-element.48), channel_id=1, replica_groups=mesh['tm'=8,'clus'=4] {'tm','clus'}, dimensions={0} | all-to-all | bytes 524288 | tf_op jit(solution)/shard_map/all_to_all | solution.py:394
  63.2 0.9 %end.1 = (f32[15,1024]{1,0:T(8,128)}, f32[15,1024]{1,0:T(8,128)}) custom-call(f32[32,16,128]{2,1,0:T(8,128)S(1)} %all_to_all.23.got, f32[15,1024]{1,0:T(8,128)S(1)} %get-tuple-element.49.residual, f32[16,1024]{1,0:T(8,128)S(1)} %get-tuple-element.50.inertial, s32[1,1024]{1,0:T(1,128)S(1)} %bitcast.10, f32[16,1024]{1,0:T(8,128)S(1)} %get-tuple-element.31.scaled.first, ...), custom_call_target="tpu_custom_call" | custom-call | tf_op jit(solution)/shard_map/end/pallas_call | solution.py:475
Async XLA Ops:
  0.6 18.1 %copy-start = (f32[15,15,1024]{2,1,0:T(8,128)S(1)}, f32[15,15,1024]{2,1,0:T(8,128)}, u32[]{:S(2)}) copy-start(f32[15,15,1024]{2,1,0:T(8,128)} %transition.7) | copy-start | bytes 2764804
  18.7 1.6 %collective-permute-start = (f32[16,16,128]{2,1,0:T(8,128)S(1)}, f32[16,16,128]{2,1,0:T(8,128)S(1)}, u32[]{:S(2)}, u32[]{:S(2)}) collective-permute-start(f32[16,16,128]{2,1,0:T(8,128)S(1)} %all_to_all.20.got), channel_id=1, source_target_pairs={{0,1},{1,0},{2,3},{3,2},{4,5},{5,4},{6,7},{7,6},{8,9},{9,8},{10,11... | collective-permute-start | bytes 393224 | tf_op jit(solution)/shard_map/ppermute | solution.py:409
  20.3 15.0 %copy-start.1 = (f32[15,15,1024]{2,1,0:T(8,128)S(1)}, f32[15,15,1024]{2,1,0:T(8,128)}, u32[]{:S(2)}) copy-start(f32[15,15,1024]{2,1,0:T(8,128)} %precond.1) | copy-start | bytes 2764804
  20.3 15.0 %copy-start.2 = (f32[15,1024]{1,0:T(8,128)S(1)}, f32[15,1024]{1,0:T(8,128)}, u32[]{:S(2)}) copy-start(f32[15,1024]{1,0:T(8,128)} %right.1) | copy-start | bytes 184324
  20.3 14.9 %copy-start.3 = (s32[1024]{0:T(1024)S(1)}, s32[1024]{0:T(1024)}, u32[]{:S(2)}) copy-start(s32[1024]{0:T(1024)} %param.12) | copy-start | bytes 12292
  46.9 1.4 %collective-permute-start.1 = (f32[16,16,128]{2,1,0:T(8,128)S(1)}, f32[16,16,128]{2,1,0:T(8,128)S(1)}, u32[]{:S(2)}, u32[]{:S(2)}) collective-permute-start(f32[16,16,128]{2,1,0:T(8,128)S(1)} %all_to_all.22.got), channel_id=1, source_target_pairs={{0,1},{1,0},{2,3},{3,2},{4,5},{5,4},{6,7},{7,6},{8,9},{9,8},{10,11... | collective-permute-start | bytes 393224 | tf_op jit(solution)/shard_map/ppermute | solution.py:409

commit v8 on v7

--- a/solution.py
+++ b/solution.py
@@ -86,44 +86,58 @@
     return total(dot)
 
 
-def send_states(scaled, dot, slot, hot, left, send, state):
+def reorder(tiles, index):
+    low = jnp.broadcast_to(index & (LANE - 1), (ROWS, LANE))
+    part = jnp.broadcast_to(index >> 7, (ROWS, LANE))
+    out = jnp.zeros((ROWS, LANE), F32)
+    for k, one in enumerate(tiles):
+        out = jnp.where(part == k, jnp.take_along_axis(one, low, axis=1), out)
+    return out
+
+
+def send_states(scaled, dot, origin, send, state):
     width = scaled.shape[1]
-    groups, copies, _, share = send.shape
-    parts = width // SUB
-    for start in range(0, width, SUB):
-        at = slice(start, start + SUB)
-        also = slice(width + start, width + start + SUB)
-        high, low = halves(scaled[:, at])
-        part = spread_row(slot[0:1, at] >> 8, ROWS)
-        for k in range(parts):
-            rows = slice(k * ROWS, (k + 1) * ROWS)
-            left[rows, at] = masked(part, k, high)
-            left[rows, also] = masked(part, k, low)
-    table = hot[...]
-    moved = both(left[:, :width], table, ((1,), (1,))) + both(left[:, width:], table, ((1,), (1,)))
+    copies, _, share = send.shape[1:]
     notes = note(scaled[:, 0:1], dot, state, share)
+    tiles = [scaled[:, start : start + LANE] for start in range(0, width, LANE)]
     sub = iota((ROWS, share), 0)
-    for k in range(parts):
-        piece = moved[k * ROWS : (k + 1) * ROWS]
-        for m in range(SUB // share):
+    for k in range(width // LANE):
+        piece = reorder(tiles, origin[0:1, k * LANE : (k + 1) * LANE])
+        for m in range(LANE // share):
             one = jnp.where(sub == state, notes[:, :share], piece[:, m * share : (m + 1) * share])
             for copy in range(copies):
-                send[k * (SUB // share) + m, copy] = one
+                send[k * (LANE // share) + m, copy] = one
+
+
+def invert(slot, hot, left, origin):
+    width = slot.shape[1]
+    hot_table(hot, slot, width)
+    sub = iota((ROWS, SUB), 0)
+    for start in range(0, width, SUB):
+        number = iota((ROWS, SUB), 1) + start
+        digits = jnp.where(sub == 0, number >> 5, jnp.where(sub == 1, number & 31, 0)).astype(F32).astype(BF16)
+        part = spread_row(slot[0:1, start : start + SUB] >> 8, ROWS)
+        for k in range(width // SUB):
+            left[k * ROWS : (k + 1) * ROWS, start : start + SUB] = masked(part, k, digits)
+    found = both(left[...], hot[...], ((1,), (1,)))
+    for k in range(width // SUB):
+        row = 32.0 * found[k * ROWS : k * ROWS + 1] + found[k * ROWS + 1 : k * ROWS + 2]
+        origin[0:1, k * SUB : (k + 1) * SUB] = row.astype(jnp.int32)
 
 
 def begin_kernel(right_in, precond_in, slot_in, heads_in, tails_in, heads_tile_in, tails_tile_in, cluster_in, damping_in,
-                 send, scaled, heads, tails, heads_tile, tails_tile, hot_pairs, lam,
+                 send, scaled, origin, heads, tails, heads_tile, tails_tile, hot_pairs, lam,
                  hot, left, right, precond, slot, cluster, damping, sems):
     state = right.shape[0]
     copies = fetch(sems, (precond_in, precond), (heads_in, heads), (tails_in, tails), (slot_in, slot), (right_in, right),
                    (cluster_in, cluster), (damping_in, damping), (heads_tile_in, heads_tile), (tails_tile_in, tails_tile))
     pairs = heads.shape[1]
+    copies[3].wait()
+    invert(slot, hot, left, origin)
     copies[1].wait()
     hot_table(hot_pairs.at[:, 0:pairs], heads, pairs)
     copies[2].wait()
     hot_table(hot_pairs.at[:, pairs:], tails, pairs)
-    copies[3].wait()
-    hot_table(hot, slot, right.shape[1])
     copies[5].wait()
     copies[6].wait()
     row = jnp.zeros(lam.shape, F32)
@@ -133,7 +147,7 @@
     copies[4].wait()
     copies[0].wait()
     dot = apply_precond(precond, right, scaled)
-    send_states(scaled, dot, slot, hot, left, send, state)
+    send_states(scaled, dot, origin, send, state)
     copies[7].wait()
     copies[8].wait()
 
@@ -297,56 +311,45 @@
         send[d, state : state + 1, :] = notes[:, :share]
 
 
-def image_of(n_time, n_clus, axes, got, inertial, slot, hot, field, image, state):
+def image_of(n_time, n_clus, axes, got, inertial, slot, image, state):
     width = image.shape[1]
-    share = got.shape[2]
-    per_part = SUB // share
-    parts = width // SUB
+    per = LANE // got.shape[2]
     flat = lax.axis_index(axes[0]) * n_clus + lax.axis_index(axes[1])
-    for k in range(parts):
+    tiles = []
+    for r in range(width // LANE):
         pieces = []
-        for m in range(per_part):
-            t = k * per_part + m
+        for t in range(r * per, (r + 1) * per):
             one = got[t * n_clus]
             for c in range(1, n_clus):
                 one = one + got[t * n_clus + c]
             pieces.append(one)
-        rows = slice(k * ROWS, (k + 1) * ROWS)
-        field[rows, 0:SUB], field[rows, SUB:] = halves(join(pieces))
+        tiles.append(join(pieces))
     prior = row_to_column(got[jnp.maximum(flat - 1, 0), state : state + 1, :], state)
     prior = jnp.where(flat == 0, 0.0, prior)
-    for start in range(0, width, SUB):
-        at = slice(start, start + SUB)
-        table = hot[:, at]
-        found = both(field[:, 0:SUB], table, ((1,), (0,))) + both(field[:, SUB:], table, ((1,), (0,)))
-        part = slot[0:1, at] >> 8
-        out = found[0:ROWS]
-        for k in range(1, parts):
-            out = jnp.where(part == k, found[k * ROWS : (k + 1) * ROWS], out)
-        out = out + inertial[:, at]
+    for start in range(0, width, LANE):
+        at = slice(start, start + LANE)
+        out = reorder(tiles, slot[0:1, at]) + inertial[:, at]
         if start == 0:
-            out = jnp.where(iota((ROWS, SUB), 1) == 0, out + prior, out)
+            out = jnp.where(iota((ROWS, LANE), 1) == 0, out + prior, out)
         image[:, at] = out
     return jnp.sum(got[:, state : state + 1, :], axis=0)[:, state : state + 1]
 
 
-def step_kernel(n_time, n_clus, axes, got, right, inertial, precond, slot, sums,
-                send, scaled, residual, image, scalars, hot, field, left):
+def step_kernel(n_time, n_clus, axes, got, right, inertial, precond, slot, origin, sums,
+                send, scaled, residual, image, scalars):
     state, width = right.shape
-    hot_table(hot, slot, width)
-    product = image_of(n_time, n_clus, axes, got, inertial, slot, hot, field, image, state)
+    product = image_of(n_time, n_clus, axes, got, inertial, slot, image, state)
     alpha = sums[0:1, state : state + 1] / product
     residual[...] = right[...] - alpha * image[0:state, :]
     dot = apply_precond(precond, residual, scaled)
-    send_states(scaled, dot, slot, hot, left, send, state)
+    send_states(scaled, dot, origin, send, state)
     scalars[...] = jnp.broadcast_to(alpha, scalars.shape)
 
 
 def end_kernel(n_time, n_clus, axes, got, residual, inertial, slot, first, scaled, along, sums, sums_next, scalars,
-               solution_field, residual_out, hot, field, image):
+               solution_field, residual_out, image):
     state, width = residual.shape
-    hot_table(hot, slot, width)
-    product = image_of(n_time, n_clus, axes, got, inertial, slot, hot, field, image, state)
+    product = image_of(n_time, n_clus, axes, got, inertial, slot, image, state)
     alpha = scalars[0:1, 0:1]
     rz, rz_next = sums[0:1, state : state + 1], sums_next[0:1, state : state + 1]
     ratio = rz_next / rz
@@ -387,8 +390,7 @@
     row = like(1, share)
     tile = like(ROWS, width)
     hot = pltpu.VMEM((SUB, width), BF16)
-    left = pltpu.VMEM((ROWS * width // SUB, 2 * width), BF16)
-    terms = pltpu.VMEM((ROWS * width // SUB, 2 * SUB), BF16)
+    left = pltpu.VMEM((ROWS * width // SUB, width), BF16)
 
     def exchange(sent):
         return lax.all_to_all(sent.reshape(devices, ROWS, share), axes, split_axis=0, concat_axis=0, tiled=True)
@@ -440,11 +442,12 @@
             name="group",
         )(got, other, pulled, heads, tails, heads_tile, tails_tile, hot_of, lam, *tables, errors, partial, transition)
 
-    sent, first, *carried = pl.pallas_call(
+    sent, first, origin, *carried = pl.pallas_call(
         begin_kernel,
         out_shape=(
             outgoing,
             tile,
+            jax.ShapeDtypeStruct((1, width), jnp.int32),
             *(jax.ShapeDtypeStruct(array.shape, array.dtype) for array in small[:4]),
             jax.ShapeDtypeStruct((SUB, 2 * pairs), BF16),
             like(1, width),
@@ -467,15 +470,14 @@
     sent, scaled, residual, along, scalars = pl.pallas_call(
         functools.partial(step_kernel, n_time, n_clus, axes),
         out_shape=(outgoing, tile, like(state, width), tile, like(1, LANE)),
-        scratch_shapes=[hot, terms, left],
         compiler_params=params,
         name="step",
-    )(exchange(back), right_side, inertial, precond, slot, sums)
+    )(exchange(back), right_side, inertial, precond, slot, origin, sums)
     _, (back, inertial, sums_next) = grouped(sent, scaled, carried, tables)
     return pl.pallas_call(
         functools.partial(end_kernel, n_time, n_clus, axes),
         out_shape=(like(state, width), like(state, width)),
-        scratch_shapes=[hot, terms, pltpu.VMEM((ROWS, width), F32)],
+        scratch_shapes=[pltpu.VMEM((ROWS, width), F32)],
         compiler_params=params,
         name="end",
     )(exchange(back), residual, inertial, slot, first, scaled, along, sums, sums_next, scalars)

time: 64.4 us -> 64.4 us (level)
  transfers between devices with their start and end apart: 2 -> 2, of which waited for: 0 -> 0; matrix products, arithmetic and copies ran while one was open for 0% -> 0% of each run, Pallas kernels for 5% -> 4%
where the time goes in v8:
time: 64.4 us; the launch traced here: 64.1 us
  blocking collectives  51.6 us (80%)
  Pallas kernels  11.8 us (18%)
  between operations  0.72 us (1%)
    all_to_all x2, blocking collectives, collect(): lax.all_to_all(sent, axes, split_axis=0, concat_axis=0, tiled=True, axis_...  26.9 us
    all_to_all x2, blocking collectives, exchange(): lax.all_to_all(sent.reshape(devices, ROWS, share), axes, split_axis=0, co...  24.6 us
    pallas_call x2, Pallas kernels, grouped(): pl.pallas_call(functools.partial(group_kernel, n_time, n_clus, axes), out...  5.17 us
    pallas_call x2, Pallas kernels, grouped(): pl.pallas_call(functools.partial(half_kernel, axes, not tables), out_shap...  2.86 us
    pallas_call x1, Pallas kernels, on_device(): pl.pallas_call(begin_kernel, out_shape=(outgoing, tile, jax.ShapeDtypeStr...  2.26 us
  transfers between devices with their start and end apart: 2, of which 0 were waited for; matrix products, arithmetic and copies ran while one was open for 0% of the time, Pallas kernels for 4%

profile of v8, /device:TPU:0, one launch (start us, length us, event | category | flops | bytes accessed | tf_op | source)
XLA Modules:
  0.0 64.1 jit_solution(2240393208825900689)
XLA Ops:
  0.6 0.0 copy-start
  0.6 2.3 %begin.1 = (f32[8,2,16,128]{3,2,1,0:T(8,128)S(1)}, f32[16,1024]{1,0:T(8,128)S(1)}, s32[1,1024]{1,0:T(1,128)S(1)}, s32[1,2048]{1,0:T(1,128)S(1)}, s32[1,2048]{1,0...) custom-call(f32[15,1024]{1,0:T(8,128)} %right.1, ...), custom_call_target="tpu_custom_call" | custom-call | tf_op jit(solution)/shard_map/begin/pallas_call | solution.py:445
  2.9 15.9 %all_to_all.20.got = f32[16,16,128]{2,1,0:T(8,128)S(1)} all-to-all(f32[16,16,128]{2,1,0:T(8,128)S(1)} %bitcast.6), channel_id=1, replica_groups={{0,2,4,6,8,10,12,14,16,18,20,22,24,26,28,30},{1,3,5,7,9,11,13,15,17,19,..., dimensions={0} | all-to-all | bytes 262144 | tf_op jit(solution)/shard_map/all_to_all | solution.py:410
  18.8 0.0 collective-permute-start
  18.8 0.0 copy-done
  18.8 1.5 %half.2 = (f32[30,16,128]{2,1,0:T(8,128)S(1)}, f32[16,1024]{1,0:T(8,128)S(1)}, f32[16,1024]{1,0:T(8,128)S(1)}, f32[225,16,128]{2,1,0:T(8,128)S(1)}) custom-call(f32[16,16,128]{2,1,0:T(8,128)S(1)} %all_to_all.20.got, s32[16,128]{1,0:T(8,128)S(1)} %get-tuple-element.30.heads_tile, s32[16,128]{1,0:T(8,128)S(1)} %get-tuple-element.31.tails_tile, ...), custom_call_target="tpu_custom_call" | custom-call | tf_op jit(solution)/shard_map/half/pallas_call | solution.py:423
  20.4 0.0 collective-permute-done.other
  20.4 0.0 copy-start.1
  20.4 0.0 copy-start.2
  20.4 0.0 copy-start.3
  20.4 2.6 %group.2 = (f32[32,16,128]{2,1,0:T(8,128)S(1)}, f32[16,1024]{1,0:T(8,128)S(1)}, f32[1,128]{1,0:T(1,128)S(1)}) custom-call(f32[16,16,128]{2,1,0:T(8,128)S(1)} %all_to_all.20.got, f32[16,16,128]{2,1,0:T(8,128)S(1)} %collective-permute-done.other, f32[30,16,128]{2,1,0:T(8,128)S(1)} %get-tuple-element.33.pulled, s32[1,2048]{1,0:T(1,128)S(1)} %get-tuple-element.34.heads, ...), custom_call_target="tpu_custom_call" | custom-call | tf_op jit(solution)/shard_map/group/pallas_call | solution.py:432
  23.0 12.3 %all_to_all.21.got = f32[32,16,128]{2,1,0:T(8,128)S(1)} all-to-all(f32[32,16,128]{2,1,0:T(8,128)S(1)} %get-tuple-element.41), channel_id=1, replica_groups=mesh['tm'=8,'clus'=4] {'tm','clus'}, dimensions={0} | all-to-all | bytes 524288 | tf_op jit(solution)/shard_map/all_to_all | solution.py:396
  35.3 0.0 copy-done.1
  35.3 0.0 copy-done.2
  35.3 0.0 copy-done.3
  35.3 0.6 step.1
  35.9 11.0 %all_to_all.22.got = f32[16,16,128]{2,1,0:T(8,128)S(1)} all-to-all(f32[16,16,128]{2,1,0:T(8,128)S(1)} %bitcast.7), channel_id=1, replica_groups={{0,2,4,6,8,10,12,14,16,18,20,22,24,26,28,30},{1,3,5,7,9,11,13,15,17,19,..., dimensions={0} | all-to-all | bytes 262144 | tf_op jit(solution)/shard_map/all_to_all | solution.py:410
  46.9 0.0 collective-permute-start.1
  46.9 1.3 %half.3 = (f32[30,16,128]{2,1,0:T(8,128)S(1)}, f32[16,1024]{1,0:T(8,128)S(1)}, f32[16,1024]{1,0:T(8,128)S(1)}) custom-call(f32[16,16,128]{2,1,0:T(8,128)S(1)} %all_to_all.22.got, s32[16,128]{1,0:T(8,128)S(1)} %get-tuple-element.30.heads_tile, s32[16,128]{1,0:T(8,128)S(1)} %get-tuple-element.31.tails_tile, f32[16,1024]{1,0:T(8,128)S(1)} %get-tuple-element.46.scaled, ...), custom_call_target="tpu_custom_call" | custom-call | tf_op jit(solution)/shard_map/half/pallas_call | solution.py:423
  48.3 0.0 collective-permute-done.1.other
  48.3 2.6 %group.3 = (f32[32,16,128]{2,1,0:T(8,128)S(1)}, f32[16,1024]{1,0:T(8,128)S(1)}, f32[1,128]{1,0:T(1,128)S(1)}) custom-call(f32[16,16,128]{2,1,0:T(8,128)S(1)} %all_to_all.22.got, f32[16,16,128]{2,1,0:T(8,128)S(1)} %collective-permute-done.1.other, f32[30,16,128]{2,1,0:T(8,128)S(1)} %get-tuple-element.47.pulled, s32[1,2048]{1,0:T(1,128)S(1)} %get-tuple-element.34.heads, ...), custom_call_target="tpu_custom_call" | custom-call | tf_op jit(solution)/shard_map/group/pallas_call | solution.py:432
  50.9 12.3 %all_to_all.23.got = f32[32,16,128]{2,1,0:T(8,128)S(1)} all-to-all(f32[32,16,128]{2,1,0:T(8,128)S(1)} %get-tuple-element.50), channel_id=1, replica_groups=mesh['tm'=8,'clus'=4] {'tm','clus'}, dimensions={0} | all-to-all | bytes 524288 | tf_op jit(solution)/shard_map/all_to_all | solution.py:396
  63.2 0.9 %end.1 = (f32[15,1024]{1,0:T(8,128)}, f32[15,1024]{1,0:T(8,128)}) custom-call(f32[32,16,128]{2,1,0:T(8,128)S(1)} %all_to_all.23.got, f32[15,1024]{1,0:T(8,128)S(1)} %get-tuple-element.51.residual, f32[16,1024]{1,0:T(8,128)S(1)} %get-tuple-element.52.inertial, s32[1,1024]{1,0:T(1,128)S(1)} %bitcast.10, f32[16,1024]{1,0:T(8,128)S(1)} %get-tuple-element.32.scaled.first, ...), custom_call_target="tpu_custom_call" | custom-call | tf_op jit(solution)/shard_map/end/pallas_call | solution.py:477
Async XLA Ops:
  0.6 18.2 %copy-start = (f32[15,15,1024]{2,1,0:T(8,128)S(1)}, f32[15,15,1024]{2,1,0:T(8,128)}, u32[]{:S(2)}) copy-start(f32[15,15,1024]{2,1,0:T(8,128)} %transition.7) | copy-start | bytes 2764804
  18.8 1.6 %collective-permute-start = (f32[16,16,128]{2,1,0:T(8,128)S(1)}, f32[16,16,128]{2,1,0:T(8,128)S(1)}, u32[]{:S(2)}, u32[]{:S(2)}) collective-permute-start(f32[16,16,128]{2,1,0:T(8,128)S(1)} %all_to_all.20.got), channel_id=1, source_target_pairs={{0,1},{1,0},{2,3},{3,2},{4,5},{5,4},{6,7},{7,6},{8,9},{9,8},{10,11... | collective-permute-start | bytes 393224 | tf_op jit(solution)/shard_map/ppermute | solution.py:411
  20.4 15.0 %copy-start.1 = (f32[15,15,1024]{2,1,0:T(8,128)S(1)}, f32[15,15,1024]{2,1,0:T(8,128)}, u32[]{:S(2)}) copy-start(f32[15,15,1024]{2,1,0:T(8,128)} %precond.1) | copy-start | bytes 2764804
  20.4 14.9 %copy-start.2 = (f32[15,1024]{1,0:T(8,128)S(1)}, f32[15,1024]{1,0:T(8,128)}, u32[]{:S(2)}) copy-start(f32[15,1024]{1,0:T(8,128)} %right.1) | copy-start | bytes 184324
  20.4 14.9 %copy-start.3 = (s32[1024]{0:T(1024)S(1)}, s32[1024]{0:T(1024)}, u32[]{:S(2)}) copy-start(s32[1024]{0:T(1024)} %param.12) | copy-start | bytes 12292
  46.9 1.3 %collective-permute-start.1 = (f32[16,16,128]{2,1,0:T(8,128)S(1)}, f32[16,16,128]{2,1,0:T(8,128)S(1)}, u32[]{:S(2)}, u32[]{:S(2)}) collective-permute-start(f32[16,16,128]{2,1,0:T(8,128)S(1)} %all_to_all.22.got), channel_id=1, source_target_pairs={{0,1},{1,0},{2,3},{3,2},{4,5},{5,4},{6,7},{7,6},{8,9},{9,8},{10,11... | collective-permute-start | bytes 393224 | tf_op jit(solution)/shard_map/ppermute | solution.py:411

commit v9 on v8

--- a/solution.py
+++ b/solution.py
@@ -11,6 +11,7 @@
 ROWS = 16
 SUB = 256
 LANE = 128
+WIDE = 512
 VMEM_LIMIT = 16 * 1024 * 1024
 
 
@@ -27,19 +28,28 @@
     return pieces[0] if len(pieces) == 1 else jnp.concatenate(pieces, axis=1)
 
 
+def spread_rows(numbers):
+    return numbers.astype(F32).astype(BF16)
+
+
 def spread_row(row, count):
     return jnp.broadcast_to(row.astype(F32), (count, row.shape[1])).astype(BF16)
 
 
-def hot_tile(index):
-    rows = iota((SUB, index.shape[1]), 0).astype(F32).astype(BF16)
-    low = spread_row(index & (SUB - 1), SUB)
-    return jnp.where(rows == low, jnp.ones((), BF16), jnp.zeros((), BF16))
-
-
 def hot_table(hot, index_ref, width):
+    size = hot.shape[0]
+    ones, zeros = jnp.ones((), BF16), jnp.zeros((), BF16)
+    rows = [spread_rows(iota((ROWS, SUB), 0) + r) for r in range(0, SUB, ROWS)]
     for start in range(0, width, SUB):
-        hot[:, start : start + SUB] = hot_tile(index_ref[0:1, start : start + SUB])
+        at = slice(start, start + SUB)
+        index = index_ref[0:1, at]
+        for b in range(size // SUB):
+            low = index & (SUB - 1)
+            if size > SUB:
+                low = jnp.where((index & (size - 1)) >> 8 == b, low, WIDE)
+            low = spread_row(low, ROWS)
+            for r, row in enumerate(rows):
+                hot[b * SUB + r * ROWS : b * SUB + (r + 1) * ROWS, at] = jnp.where(row == low, ones, zeros)
 
 
 def masked(part, k, value):
@@ -140,9 +150,9 @@
     hot_table(hot_pairs.at[:, pairs:], tails, pairs)
     copies[5].wait()
     copies[6].wait()
-    row = jnp.zeros(lam.shape, F32)
-    for label in range(damping.shape[1]):
-        row = jnp.where(cluster[...] == label, damping[0:1, label : label + 1], row)
+    spare = jnp.zeros((1, LANE - damping.shape[1]), F32)
+    row = jnp.broadcast_to(jnp.concatenate([damping[...], spare], axis=1), lam.shape)
+    row = jnp.take_along_axis(row, cluster[...], axis=1)
     lam[...] = row
     copies[4].wait()
     copies[0].wait()
@@ -186,6 +196,16 @@
     for i in range(half):
         for r in range(tiles):
             field[i, r] = join([got[(r * per + m) * half + i] for m in range(per)])
+
+
+def row_sums(tiles):
+    row = iota((8, LANE), 0)
+    for step in (4, 2, 1):
+        tiles = [
+            jnp.where(row & step == 0, one + pltpu.roll(one, 8 - step, 0), other + pltpu.roll(other, step, 0))
+            for one, other in zip(tiles[:step], tiles[step:])
+        ]
+    return tiles[0]
 
 
 def half_kernel(axes, once, got, heads_tile, tails_tile, scaled, transition, *refs):
@@ -205,10 +225,18 @@
             for c, value in enumerate(pull(ends, h, field, parity, state, zero)):
                 pulled[which * state + c, h : h + 8, :] = value
     lane = iota((ROWS, width), 1)
-    errors[...] = jnp.where(lane == width - 1, 0.0, pltpu.roll(scaled[...], width - 1, 1))
-    for i in range(state):
-        moved = jnp.sum(transition[i] * scaled[0:state, :], axis=0, keepdims=True)
-        errors[i : i + 1, :] = errors[i : i + 1, :] - moved
+    ahead = jnp.where(lane == width - 1, 0.0, pltpu.roll(scaled[...], width - 1, 1))
+    empty = jnp.zeros((ROWS - state, LANE), F32)
+    for start in range(0, width, LANE):
+        at = slice(start, start + LANE)
+        low, high = scaled[0:8, at], scaled[8:state, at]
+        for first in range(0, ROWS, 8):
+            moved = [
+                transition[i, 0:8, at] * low + jnp.concatenate([transition[i, 8:state, at] * high, empty], axis=0)
+                for i in range(first, min(first + 8, state))
+            ]
+            moved += [jnp.zeros((8, LANE), F32)] * (8 - len(moved))
+            errors[first : first + 8, at] = ahead[first : first + 8, at] - row_sums(moved)
     prior = jnp.where(lane == 0, 0.0, pltpu.roll(errors[...], 1, 1))
     inertial[state:ROWS, :] = jnp.zeros((ROWS - state, width), F32)
     for start in range(0, width - LANE, LANE):
@@ -225,8 +253,8 @@
     width = errors.shape[1]
     share = got.shape[2]
     pairs = heads.shape[1]
-    parts = n_clus * width // SUB
-    per_part = SUB // share
+    parts = n_clus * width // WIDE
+    per_part = WIDE // share
     chunks = pairs // LANE
     half = n_clus // 2
     time_at, clus_at = lax.axis_index(axes[0]), lax.axis_index(axes[1])
@@ -242,7 +270,7 @@
 
     def spread(ends, base, n):
         at = slice(base * LANE + n * SUB, base * LANE + (n + 1) * SUB)
-        part = spread_row(ends[0:1, n * SUB : (n + 1) * SUB] >> 8, ROWS)
+        part = spread_row(ends[0:1, n * SUB : (n + 1) * SUB] >> 9, ROWS)
         row = (base + n * (SUB // LANE)) * ROWS
         high, low = halves(join([values[row + m * ROWS : row + (m + 1) * ROWS, :] for m in range(SUB // LANE)]))
         for k in range(parts):
@@ -300,7 +328,8 @@
         for m in range(per_part):
             piece = k * per_part + m
             c, t = piece // n_time, piece % n_time
-            here = jnp.where(clus_at == c, lam[:, t * share : (t + 1) * share], 0.0)
+            r, l = t * share // LANE, t * share % LANE
+            here = jnp.where(clus_at == c, lam[r : r + 1, l : l + share], 0.0)
             states = jnp.where(sub < state, got[t * half + c // 2], 0.0)
             extra = here * states
             damped = damped + extra * states
@@ -401,7 +430,8 @@
     in_hbm = pl.BlockSpec(memory_space=pltpu.HBM)
     in_vmem = pl.BlockSpec(memory_space=pltpu.VMEM)
     dense = (pairs // LANE, LANE)
-    small = (pair_first, pair_second, pair_first.reshape(dense), pair_second.reshape(dense), cluster_id, damping)
+    small = (pair_first, pair_second, pair_first.reshape(dense), pair_second.reshape(dense),
+             cluster_id.reshape(width // LANE, LANE), damping)
     same = [[t * n_clus + c for t in range(n_time) for c in range(q, n_clus, 2)] for q in range(2)]
     field = pltpu.VMEM((n_clus // 2, width // LANE, ROWS, LANE), F32)
 
@@ -435,7 +465,7 @@
             scratch_shapes=[
                 field,
                 pltpu.VMEM((2 * pairs // LANE * ROWS, LANE), F32),
-                pltpu.VMEM((2 * ROWS * positions // SUB, 2 * pairs), BF16),
+                pltpu.VMEM((2 * ROWS * positions // WIDE, 2 * pairs), BF16),
                 pltpu.VMEM((ROWS, LANE), F32),
             ],
             compiler_params=params,
@@ -449,8 +479,8 @@
             tile,
             jax.ShapeDtypeStruct((1, width), jnp.int32),
             *(jax.ShapeDtypeStruct(array.shape, array.dtype) for array in small[:4]),
-            jax.ShapeDtypeStruct((SUB, 2 * pairs), BF16),
-            like(1, width),
+            jax.ShapeDtypeStruct((WIDE, 2 * pairs), BF16),
+            like(width // LANE, LANE),
         ),
         in_specs=[in_hbm] * (3 + len(small)),
         scratch_shapes=[
@@ -459,7 +489,7 @@
             pltpu.VMEM(right_side.shape, F32),
             pltpu.VMEM(precond.shape, F32),
             pltpu.VMEM(slot.shape, jnp.int32),
-            pltpu.VMEM(cluster_id.shape, jnp.int32),
+            pltpu.VMEM((width // LANE, LANE), jnp.int32),
             pltpu.VMEM(damping.shape, F32),
             pltpu.SemaphoreType.DMA((3 + len(small),)),
         ],

time: 64.4 us -> 65.6 us (1.019)
  Pallas kernels: 11.8 us -> 13 us
    pallas_call x2, Pallas kernels: 2.86 us -> 3.61 us  [grouped(): pl.pallas_call(functools.partial(half_kernel, axes, not tables), out_shap...]
  transfers between devices with their start and end apart: 2 -> 2, of which waited for: 0 -> 1; matrix products, arithmetic and copies ran while one was open for 0% -> 0% of each run, Pallas kernels for 4% -> 6%
where the time goes in v9:
time: 65.6 us; the launch traced here: 65.4 us
  blocking collectives  51.6 us (79%)
  Pallas kernels  13 us (20%)
  between operations  0.72 us (1%)
    all_to_all x2, blocking collectives, collect(): lax.all_to_all(sent, axes, split_axis=0, concat_axis=0, tiled=True, axis_...  26.9 us
    all_to_all x2, blocking collectives, exchange(): lax.all_to_all(sent.reshape(devices, ROWS, share), axes, split_axis=0, co...  24.6 us
    pallas_call x2, Pallas kernels, grouped(): pl.pallas_call(functools.partial(group_kernel, n_time, n_clus, axes), out...  5.39 us
    pallas_call x2, Pallas kernels, grouped(): pl.pallas_call(functools.partial(half_kernel, axes, not tables), out_shap...  3.61 us
    pallas_call x1, Pallas kernels, on_device(): pl.pallas_call(begin_kernel, out_shape=(outgoing, tile, jax.ShapeDtypeStr...  2.45 us
  transfers between devices with their start and end apart: 2, of which 1 were waited for; matrix products, arithmetic and copies ran while one was open for 0% of the time, Pallas kernels for 6%

profile of v9, /device:TPU:0, one launch (start us, length us, event | category | flops | bytes accessed | tf_op | source)
XLA Modules:
  0.0 65.4 jit_solution(1043288183498702576)
XLA Ops:
  0.6 0.0 copy-start
  0.6 2.5 %begin.1 = (f32[8,2,16,128]{3,2,1,0:T(8,128)S(1)}, f32[16,1024]{1,0:T(8,128)S(1)}, s32[1,1024]{1,0:T(1,128)S(1)}, s32[1,2048]{1,0:T(1,128)S(1)}, s32[1,2048]{1,0...) custom-call(f32[15,1024]{1,0:T(8,128)} %right.1, ...), custom_call_target="tpu_custom_call" | custom-call | tf_op jit(solution)/shard_map/begin/pallas_call | solution.py:475
  3.1 15.9 %all_to_all.20.got = f32[16,16,128]{2,1,0:T(8,128)S(1)} all-to-all(f32[16,16,128]{2,1,0:T(8,128)S(1)} %bitcast.7), channel_id=1, replica_groups={{0,2,4,6,8,10,12,14,16,18,20,22,24,26,28,30},{1,3,5,7,9,11,13,15,17,19,..., dimensions={0} | all-to-all | bytes 262144 | tf_op jit(solution)/shard_map/all_to_all | solution.py:440
  19.0 0.0 collective-permute-start
  19.0 0.0 copy-done
  19.0 2.4 %half.2 = (f32[30,16,128]{2,1,0:T(8,128)S(1)}, f32[16,1024]{1,0:T(8,128)S(1)}, f32[16,1024]{1,0:T(8,128)S(1)}, f32[225,16,128]{2,1,0:T(8,128)S(1)}) custom-call(f32[16,16,128]{2,1,0:T(8,128)S(1)} %all_to_all.20.got, s32[16,128]{1,0:T(8,128)S(1)} %get-tuple-element.30.heads_tile, s32[16,128]{1,0:T(8,128)S(1)} %get-tuple-element.31.tails_tile, ...), custom_call_target="tpu_custom_call" | custom-call | tf_op jit(solution)/shard_map/half/pallas_call | solution.py:453
  21.4 0.0 collective-permute-done.other
  21.4 0.0 copy-start.1
  21.4 0.0 copy-start.2
  21.4 0.0 copy-start.3
  21.4 2.7 %group.2 = (f32[32,16,128]{2,1,0:T(8,128)S(1)}, f32[16,1024]{1,0:T(8,128)S(1)}, f32[1,128]{1,0:T(1,128)S(1)}) custom-call(f32[16,16,128]{2,1,0:T(8,128)S(1)} %all_to_all.20.got, f32[16,16,128]{2,1,0:T(8,128)S(1)} %collective-permute-done.other, f32[30,16,128]{2,1,0:T(8,128)S(1)} %get-tuple-element.33.pulled, s32[1,2048]{1,0:T(1,128)S(1)} %get-tuple-element.34.heads, ...), custom_call_target="tpu_custom_call" | custom-call | tf_op jit(solution)/shard_map/group/pallas_call | solution.py:462
  24.1 12.3 %all_to_all.21.got = f32[32,16,128]{2,1,0:T(8,128)S(1)} all-to-all(f32[32,16,128]{2,1,0:T(8,128)S(1)} %get-tuple-element.41), channel_id=1, replica_groups=mesh['tm'=8,'clus'=4] {'tm','clus'}, dimensions={0} | all-to-all | bytes 524288 | tf_op jit(solution)/shard_map/all_to_all | solution.py:425
  36.5 0.0 copy-done.1
  36.5 0.0 copy-done.2
  36.5 0.0 copy-done.3
  36.5 0.6 step.1
  37.1 11.0 %all_to_all.22.got = f32[16,16,128]{2,1,0:T(8,128)S(1)} all-to-all(f32[16,16,128]{2,1,0:T(8,128)S(1)} %bitcast.8), channel_id=1, replica_groups={{0,2,4,6,8,10,12,14,16,18,20,22,24,26,28,30},{1,3,5,7,9,11,13,15,17,19,..., dimensions={0} | all-to-all | bytes 262144 | tf_op jit(solution)/shard_map/all_to_all | solution.py:440
  48.1 0.0 collective-permute-start.1
  48.1 1.3 %half.3 = (f32[30,16,128]{2,1,0:T(8,128)S(1)}, f32[16,1024]{1,0:T(8,128)S(1)}, f32[16,1024]{1,0:T(8,128)S(1)}) custom-call(f32[16,16,128]{2,1,0:T(8,128)S(1)} %all_to_all.22.got, s32[16,128]{1,0:T(8,128)S(1)} %get-tuple-element.30.heads_tile, s32[16,128]{1,0:T(8,128)S(1)} %get-tuple-element.31.tails_tile, f32[16,1024]{1,0:T(8,128)S(1)} %get-tuple-element.46.scaled, ...), custom_call_target="tpu_custom_call" | custom-call | tf_op jit(solution)/shard_map/half/pallas_call | solution.py:453
  49.3 0.1 collective-permute-done.1.other
  49.4 2.7 %group.3 = (f32[32,16,128]{2,1,0:T(8,128)S(1)}, f32[16,1024]{1,0:T(8,128)S(1)}, f32[1,128]{1,0:T(1,128)S(1)}) custom-call(f32[16,16,128]{2,1,0:T(8,128)S(1)} %all_to_all.22.got, f32[16,16,128]{2,1,0:T(8,128)S(1)} %collective-permute-done.1.other, f32[30,16,128]{2,1,0:T(8,128)S(1)} %get-tuple-element.47.pulled, s32[1,2048]{1,0:T(1,128)S(1)} %get-tuple-element.34.heads, ...), custom_call_target="tpu_custom_call" | custom-call | tf_op jit(solution)/shard_map/group/pallas_call | solution.py:462
  52.1 12.3 %all_to_all.23.got = f32[32,16,128]{2,1,0:T(8,128)S(1)} all-to-all(f32[32,16,128]{2,1,0:T(8,128)S(1)} %get-tuple-element.50), channel_id=1, replica_groups=mesh['tm'=8,'clus'=4] {'tm','clus'}, dimensions={0} | all-to-all | bytes 524288 | tf_op jit(solution)/shard_map/all_to_all | solution.py:425
  64.4 0.9 %end.1 = (f32[15,1024]{1,0:T(8,128)}, f32[15,1024]{1,0:T(8,128)}) custom-call(f32[32,16,128]{2,1,0:T(8,128)S(1)} %all_to_all.23.got, f32[15,1024]{1,0:T(8,128)S(1)} %get-tuple-element.51.residual, f32[16,1024]{1,0:T(8,128)S(1)} %get-tuple-element.52.inertial, s32[1,1024]{1,0:T(1,128)S(1)} %bitcast.11, f32[16,1024]{1,0:T(8,128)S(1)} %get-tuple-element.32.scaled.first, ...), custom_call_target="tpu_custom_call" | custom-call | tf_op jit(solution)/shard_map/end/pallas_call | solution.py:507
Async XLA Ops:
  0.6 18.4 %copy-start = (f32[15,15,1024]{2,1,0:T(8,128)S(1)}, f32[15,15,1024]{2,1,0:T(8,128)}, u32[]{:S(2)}) copy-start(f32[15,15,1024]{2,1,0:T(8,128)} %transition.7) | copy-start | bytes 2764804
  19.0 2.4 %collective-permute-start = (f32[16,16,128]{2,1,0:T(8,128)S(1)}, f32[16,16,128]{2,1,0:T(8,128)S(1)}, u32[]{:S(2)}, u32[]{:S(2)}) collective-permute-start(f32[16,16,128]{2,1,0:T(8,128)S(1)} %all_to_all.20.got), channel_id=1, source_target_pairs={{0,1},{1,0},{2,3},{3,2},{4,5},{5,4},{6,7},{7,6},{8,9},{9,8},{10,11... | collective-permute-start | bytes 393224 | tf_op jit(solution)/shard_map/ppermute | solution.py:441
  21.4 15.1 %copy-start.1 = (f32[15,15,1024]{2,1,0:T(8,128)S(1)}, f32[15,15,1024]{2,1,0:T(8,128)}, u32[]{:S(2)}) copy-start(f32[15,15,1024]{2,1,0:T(8,128)} %precond.1) | copy-start | bytes 2764804
  21.4 15.1 %copy-start.2 = (f32[15,1024]{1,0:T(8,128)S(1)}, f32[15,1024]{1,0:T(8,128)}, u32[]{:S(2)}) copy-start(f32[15,1024]{1,0:T(8,128)} %right.1) | copy-start | bytes 184324
  21.4 15.0 %copy-start.3 = (s32[1024]{0:T(1024)S(1)}, s32[1024]{0:T(1024)}, u32[]{:S(2)}) copy-start(s32[1024]{0:T(1024)} %param.12) | copy-start | bytes 12292
  48.1 1.3 %collective-permute-start.1 = (f32[16,16,128]{2,1,0:T(8,128)S(1)}, f32[16,16,128]{2,1,0:T(8,128)S(1)}, u32[]{:S(2)}, u32[]{:S(2)}) collective-permute-start(f32[16,16,128]{2,1,0:T(8,128)S(1)} %all_to_all.22.got), channel_id=1, source_target_pairs={{0,1},{1,0},{2,3},{3,2},{4,5},{5,4},{6,7},{7,6},{8,9},{9,8},{10,11... | collective-permute-start | bytes 393224 | tf_op jit(solution)/shard_map/ppermute | solution.py:441

commit v10 on v9

--- a/solution.py
+++ b/solution.py
@@ -11,7 +11,6 @@
 ROWS = 16
 SUB = 256
 LANE = 128
-WIDE = 512
 VMEM_LIMIT = 16 * 1024 * 1024
 
 
@@ -37,19 +36,13 @@
 
 
 def hot_table(hot, index_ref, width):
-    size = hot.shape[0]
     ones, zeros = jnp.ones((), BF16), jnp.zeros((), BF16)
     rows = [spread_rows(iota((ROWS, SUB), 0) + r) for r in range(0, SUB, ROWS)]
     for start in range(0, width, SUB):
         at = slice(start, start + SUB)
-        index = index_ref[0:1, at]
-        for b in range(size // SUB):
-            low = index & (SUB - 1)
-            if size > SUB:
-                low = jnp.where((index & (size - 1)) >> 8 == b, low, WIDE)
-            low = spread_row(low, ROWS)
-            for r, row in enumerate(rows):
-                hot[b * SUB + r * ROWS : b * SUB + (r + 1) * ROWS, at] = jnp.where(row == low, ones, zeros)
+        low = spread_row(index_ref[0:1, at] & (SUB - 1), ROWS)
+        for r, row in enumerate(rows):
+            hot[r * ROWS : (r + 1) * ROWS, at] = jnp.where(row == low, ones, zeros)
 
 
 def masked(part, k, value):
@@ -136,30 +129,19 @@
 
 
 def begin_kernel(right_in, precond_in, slot_in, heads_in, tails_in, heads_tile_in, tails_tile_in, cluster_in, damping_in,
-                 send, scaled, origin, heads, tails, heads_tile, tails_tile, hot_pairs, lam,
-                 hot, left, right, precond, slot, cluster, damping, sems):
+                 send, scaled, origin, heads, tails, heads_tile, tails_tile, cluster, damping,
+                 hot, left, right, precond, slot, sems):
     state = right.shape[0]
     copies = fetch(sems, (precond_in, precond), (heads_in, heads), (tails_in, tails), (slot_in, slot), (right_in, right),
                    (cluster_in, cluster), (damping_in, damping), (heads_tile_in, heads_tile), (tails_tile_in, tails_tile))
-    pairs = heads.shape[1]
     copies[3].wait()
     invert(slot, hot, left, origin)
-    copies[1].wait()
-    hot_table(hot_pairs.at[:, 0:pairs], heads, pairs)
-    copies[2].wait()
-    hot_table(hot_pairs.at[:, pairs:], tails, pairs)
-    copies[5].wait()
-    copies[6].wait()
-    spare = jnp.zeros((1, LANE - damping.shape[1]), F32)
-    row = jnp.broadcast_to(jnp.concatenate([damping[...], spare], axis=1), lam.shape)
-    row = jnp.take_along_axis(row, cluster[...], axis=1)
-    lam[...] = row
     copies[4].wait()
     copies[0].wait()
     dot = apply_precond(precond, right, scaled)
     send_states(scaled, dot, origin, send, state)
-    copies[7].wait()
-    copies[8].wait()
+    for copy in copies[1:3] + copies[5:]:
+        copy.wait()
 
 
 def fetch(sems, *pairs):
@@ -213,8 +195,14 @@
     width = scaled.shape[1]
     chunks = heads_tile.shape[0]
     if once:
-        blocks_in, pulled, errors, inertial, blocks, field, sems = refs
+        heads, tails, cluster, damping, blocks_in, pulled, errors, inertial, hot, lam, blocks, field, sems = refs
         (copy,) = fetch(sems, (blocks_in, blocks))
+        pairs = heads.shape[1]
+        hot_table(hot.at[:, 0:pairs], heads, pairs)
+        hot_table(hot.at[:, pairs:], tails, pairs)
+        spare = jnp.zeros((1, LANE - damping.shape[1]), F32)
+        row = jnp.broadcast_to(jnp.concatenate([damping[...], spare], axis=1), lam.shape)
+        lam[...] = jnp.take_along_axis(row, cluster[...], axis=1)
     else:
         pulled, errors, inertial, field = refs
     fill(field, got)
@@ -253,8 +241,8 @@
     width = errors.shape[1]
     share = got.shape[2]
     pairs = heads.shape[1]
-    parts = n_clus * width // WIDE
-    per_part = WIDE // share
+    parts = n_clus * width // SUB
+    per_part = SUB // share
     chunks = pairs // LANE
     half = n_clus // 2
     time_at, clus_at = lax.axis_index(axes[0]), lax.axis_index(axes[1])
@@ -270,7 +258,7 @@
 
     def spread(ends, base, n):
         at = slice(base * LANE + n * SUB, base * LANE + (n + 1) * SUB)
-        part = spread_row(ends[0:1, n * SUB : (n + 1) * SUB] >> 9, ROWS)
+        part = spread_row(ends[0:1, n * SUB : (n + 1) * SUB] >> 8, ROWS)
         row = (base + n * (SUB // LANE)) * ROWS
         high, low = halves(join([values[row + m * ROWS : row + (m + 1) * ROWS, :] for m in range(SUB // LANE)]))
         for k in range(parts):
@@ -442,13 +430,13 @@
 
     def grouped(sent, scaled, carried, tables):
         got, other = collect(sent)
-        heads, tails, heads_tile, tails_tile, hot_of, lam = carried
+        heads, tails, heads_tile, tails_tile, cluster, damping_of = carried
         shapes = (like(2 * state, *dense), tile, tile)
         operands = (got, heads_tile, tails_tile, scaled, transition)
         scratch = [field]
         if not tables:
-            shapes += (like(*blocks.shape),)
-            operands += held(blocks)
+            shapes += (jax.ShapeDtypeStruct((SUB, 2 * pairs), BF16), like(width // LANE, LANE), like(*blocks.shape))
+            operands += (heads, tails, cluster, damping_of, *held(blocks))
             scratch += [pltpu.SemaphoreType.DMA((1,))]
         pulled, errors, partial, *fresh = pl.pallas_call(
             functools.partial(half_kernel, axes, not tables),
@@ -465,12 +453,12 @@
             scratch_shapes=[
                 field,
                 pltpu.VMEM((2 * pairs // LANE * ROWS, LANE), F32),
-                pltpu.VMEM((2 * ROWS * positions // WIDE, 2 * pairs), BF16),
+                pltpu.VMEM((2 * ROWS * positions // SUB, 2 * pairs), BF16),
                 pltpu.VMEM((ROWS, LANE), F32),
             ],
             compiler_params=params,
             name="group",
-        )(got, other, pulled, heads, tails, heads_tile, tails_tile, hot_of, lam, *tables, errors, partial, transition)
+        )(got, other, pulled, heads, tails, heads_tile, tails_tile, *tables, errors, partial, transition)
 
     sent, first, origin, *carried = pl.pallas_call(
         begin_kernel,
@@ -478,9 +466,7 @@
             outgoing,
             tile,
             jax.ShapeDtypeStruct((1, width), jnp.int32),
-            *(jax.ShapeDtypeStruct(array.shape, array.dtype) for array in small[:4]),
-            jax.ShapeDtypeStruct((WIDE, 2 * pairs), BF16),
-            like(width // LANE, LANE),
+            *(jax.ShapeDtypeStruct(array.shape, array.dtype) for array in small),
         ),
         in_specs=[in_hbm] * (3 + len(small)),
         scratch_shapes=[
@@ -489,8 +475,6 @@
             pltpu.VMEM(right_side.shape, F32),
             pltpu.VMEM(precond.shape, F32),
             pltpu.VMEM(slot.shape, jnp.int32),
-            pltpu.VMEM((width // LANE, LANE), jnp.int32),
-            pltpu.VMEM(damping.shape, F32),
             pltpu.SemaphoreType.DMA((3 + len(small),)),
         ],
         compiler_params=params,

time: 65.6 us -> 65.4 us (level)
  no operation moved by 1% of the time
where the time goes in v10:
time: 65.4 us; the launch traced here: 65.1 us
  blocking collectives  51.6 us (79%)
  Pallas kernels  12.7 us (19%)
  between operations  0.72 us (1%)
    all_to_all x2, blocking collectives, collect(): lax.all_to_all(sent, axes, split_axis=0, concat_axis=0, tiled=True, axis_...  26.9 us
    all_to_all x2, blocking collectives, exchange(): lax.all_to_all(sent.reshape(devices, ROWS, share), axes, split_axis=0, co...  24.6 us
    pallas_call x2, Pallas kernels, grouped(): pl.pallas_call(functools.partial(group_kernel, n_time, n_clus, axes), out...  5.18 us
    pallas_call x2, Pallas kernels, grouped(): pl.pallas_call(functools.partial(half_kernel, axes, not tables), out_shap...  4.2 us
    pallas_call x1, Pallas kernels, on_device(): pl.pallas_call(begin_kernel, out_shape=(outgoing, tile, jax.ShapeDtypeStr...  1.8 us
  transfers between devices with their start and end apart: 2, of which 1 were waited for; matrix products, arithmetic and copies ran while one was open for 0% of the time, Pallas kernels for 6%

profile of v10, /device:TPU:0, one launch (start us, length us, event | category | flops | bytes accessed | tf_op | source)
XLA Modules:
  0.0 65.1 jit_solution(10025237382858206958)
XLA Ops:
  0.6 0.0 copy-start
  0.6 1.8 %begin.1 = (f32[8,2,16,128]{3,2,1,0:T(8,128)S(1)}, f32[16,1024]{1,0:T(8,128)S(1)}, s32[1,1024]{1,0:T(1,128)S(1)}, s32[1,2048]{1,0:T(1,128)S(1)}, s32[1,2048]{1,0...) custom-call(f32[15,1024]{1,0:T(8,128)} %right.1, ...), custom_call_target="tpu_custom_call" | custom-call | tf_op jit(solution)/shard_map/begin/pallas_call | solution.py:463
  2.5 15.9 %all_to_all.20.got = f32[16,16,128]{2,1,0:T(8,128)S(1)} all-to-all(f32[16,16,128]{2,1,0:T(8,128)S(1)} %bitcast.7), channel_id=1, replica_groups={{0,2,4,6,8,10,12,14,16,18,20,22,24,26,28,30},{1,3,5,7,9,11,13,15,17,19,..., dimensions={0} | all-to-all | bytes 262144 | tf_op jit(solution)/shard_map/all_to_all | solution.py:428
  18.4 0.0 collective-permute-start
  18.4 0.0 copy-done
  18.4 2.9 %half.2 = (f32[30,16,128]{2,1,0:T(8,128)S(1)}, f32[16,1024]{1,0:T(8,128)S(1)}, f32[16,1024]{1,0:T(8,128)S(1)}, bf16[256,4096]{1,0:T(8,128)(2,1)S(1)}, f32[8,128]{1,0:T(8,128)S(1)}, /*index=5*/f32[225,16,128]{2,1,0:T(8,128)S(1)}) custom-call(f32[16,16,128]{2,1,0:T(8,128)S(1)} %all_to_all.20.got, s32[16,128]{1,0:T(8,128)S(1)} %get-tuple-element.32.heads_tile, ...), custom_call_target="tpu_custom_call" | custom-call | tf_op jit(solution)/shard_map/half/pallas_call | solution.py:441
  21.3 0.0 collective-permute-done.other
  21.3 0.0 copy-start.1
  21.3 0.0 copy-start.2
  21.4 0.0 copy-start.3
  21.4 2.6 %group.2 = (f32[32,16,128]{2,1,0:T(8,128)S(1)}, f32[16,1024]{1,0:T(8,128)S(1)}, f32[1,128]{1,0:T(1,128)S(1)}) custom-call(f32[16,16,128]{2,1,0:T(8,128)S(1)} %all_to_all.20.got, f32[16,16,128]{2,1,0:T(8,128)S(1)} %collective-permute-done.other, f32[30,16,128]{2,1,0:T(8,128)S(1)} %get-tuple-element.39.pulled, s32[1,2048]{1,0:T(1,128)S(1)} %get-tuple-element.35.refs_0_.heads, ...), custom_call_target="tpu_custom_call" | custom-call | tf_op jit(solution)/shard_map/group/pallas_call | solution.py:450
  24.0 12.3 %all_to_all.21.got = f32[32,16,128]{2,1,0:T(8,128)S(1)} all-to-all(f32[32,16,128]{2,1,0:T(8,128)S(1)} %get-tuple-element.45), channel_id=1, replica_groups=mesh['tm'=8,'clus'=4] {'tm','clus'}, dimensions={0} | all-to-all | bytes 524288 | tf_op jit(solution)/shard_map/all_to_all | solution.py:413
  36.3 0.0 copy-done.1
  36.3 0.0 copy-done.2
  36.3 0.0 copy-done.3
  36.3 0.6 step.1
  36.9 11.0 %all_to_all.22.got = f32[16,16,128]{2,1,0:T(8,128)S(1)} all-to-all(f32[16,16,128]{2,1,0:T(8,128)S(1)} %bitcast.8), channel_id=1, replica_groups={{0,2,4,6,8,10,12,14,16,18,20,22,24,26,28,30},{1,3,5,7,9,11,13,15,17,19,..., dimensions={0} | all-to-all | bytes 262144 | tf_op jit(solution)/shard_map/all_to_all | solution.py:428
  47.9 0.0 collective-permute-start.1
  47.9 1.3 %half.3 = (f32[30,16,128]{2,1,0:T(8,128)S(1)}, f32[16,1024]{1,0:T(8,128)S(1)}, f32[16,1024]{1,0:T(8,128)S(1)}) custom-call(f32[16,16,128]{2,1,0:T(8,128)S(1)} %all_to_all.22.got, s32[16,128]{1,0:T(8,128)S(1)} %get-tuple-element.32.heads_tile, s32[16,128]{1,0:T(8,128)S(1)} %get-tuple-element.33.tails_tile, f32[16,1024]{1,0:T(8,128)S(1)} %get-tuple-element.50.scaled, ...), custom_call_target="tpu_custom_call" | custom-call | tf_op jit(solution)/shard_map/half/pallas_call | solution.py:441
  49.2 0.1 collective-permute-done.1.other
  49.3 2.6 %group.3 = (f32[32,16,128]{2,1,0:T(8,128)S(1)}, f32[16,1024]{1,0:T(8,128)S(1)}, f32[1,128]{1,0:T(1,128)S(1)}) custom-call(f32[16,16,128]{2,1,0:T(8,128)S(1)} %all_to_all.22.got, f32[16,16,128]{2,1,0:T(8,128)S(1)} %collective-permute-done.1.other, f32[30,16,128]{2,1,0:T(8,128)S(1)} %get-tuple-element.51.pulled, ...), custom_call_target="tpu_custom_call" | custom-call | tf_op jit(solution)/shard_map/group/pallas_call | solution.py:450
  51.9 12.3 %all_to_all.23.got = f32[32,16,128]{2,1,0:T(8,128)S(1)} all-to-all(f32[32,16,128]{2,1,0:T(8,128)S(1)} %get-tuple-element.54), channel_id=1, replica_groups=mesh['tm'=8,'clus'=4] {'tm','clus'}, dimensions={0} | all-to-all | bytes 524288 | tf_op jit(solution)/shard_map/all_to_all | solution.py:413
  64.2 0.9 %end.1 = (f32[15,1024]{1,0:T(8,128)}, f32[15,1024]{1,0:T(8,128)}) custom-call(f32[32,16,128]{2,1,0:T(8,128)S(1)} %all_to_all.23.got, f32[15,1024]{1,0:T(8,128)S(1)} %get-tuple-element.55.residual, f32[16,1024]{1,0:T(8,128)S(1)} %get-tuple-element.56.inertial, s32[1,1024]{1,0:T(1,128)S(1)} %bitcast.11, f32[16,1024]{1,0:T(8,128)S(1)} %get-tuple-element.34.scaled.first, ...), custom_call_target="tpu_custom_call" | custom-call | tf_op jit(solution)/shard_map/end/pallas_call | solution.py:491
Async XLA Ops:
  0.6 17.7 %copy-start = (f32[15,15,1024]{2,1,0:T(8,128)S(1)}, f32[15,15,1024]{2,1,0:T(8,128)}, u32[]{:S(2)}) copy-start(f32[15,15,1024]{2,1,0:T(8,128)} %transition.7) | copy-start | bytes 2764804
  18.4 3.0 %collective-permute-start = (f32[16,16,128]{2,1,0:T(8,128)S(1)}, f32[16,16,128]{2,1,0:T(8,128)S(1)}, u32[]{:S(2)}, u32[]{:S(2)}) collective-permute-start(f32[16,16,128]{2,1,0:T(8,128)S(1)} %all_to_all.20.got), channel_id=1, source_target_pairs={{0,1},{1,0},{2,3},{3,2},{4,5},{5,4},{6,7},{7,6},{8,9},{9,8},{10,11... | collective-permute-start | bytes 393224 | tf_op jit(solution)/shard_map/ppermute | solution.py:429
  21.3 15.0 %copy-start.1 = (f32[15,15,1024]{2,1,0:T(8,128)S(1)}, f32[15,15,1024]{2,1,0:T(8,128)}, u32[]{:S(2)}) copy-start(f32[15,15,1024]{2,1,0:T(8,128)} %precond.1) | copy-start | bytes 2764804
  21.3 15.0 %copy-start.2 = (f32[15,1024]{1,0:T(8,128)S(1)}, f32[15,1024]{1,0:T(8,128)}, u32[]{:S(2)}) copy-start(f32[15,1024]{1,0:T(8,128)} %right.1) | copy-start | bytes 184324
  21.4 14.9 %copy-start.3 = (s32[1024]{0:T(1024)S(1)}, s32[1024]{0:T(1024)}, u32[]{:S(2)}) copy-start(s32[1024]{0:T(1024)} %param.12) | copy-start | bytes 12292
  47.9 1.3 %collective-permute-start.1 = (f32[16,16,128]{2,1,0:T(8,128)S(1)}, f32[16,16,128]{2,1,0:T(8,128)S(1)}, u32[]{:S(2)}, u32[]{:S(2)}) collective-permute-start(f32[16,16,128]{2,1,0:T(8,128)S(1)} %all_to_all.22.got), channel_id=1, source_target_pairs={{0,1},{1,0},{2,3},{3,2},{4,5},{5,4},{6,7},{7,6},{8,9},{9,8},{10,11... | collective-permute-start | bytes 393224 | tf_op jit(solution)/shard_map/ppermute | solution.py:429

commit v11 on v9

--- a/solution.py
+++ b/solution.py
@@ -11,7 +11,6 @@
 ROWS = 16
 SUB = 256
 LANE = 128
-WIDE = 512
 VMEM_LIMIT = 16 * 1024 * 1024
 
 
@@ -37,23 +36,16 @@
 
 
 def hot_table(hot, index_ref, width):
-    size = hot.shape[0]
-    ones, zeros = jnp.ones((), BF16), jnp.zeros((), BF16)
     rows = [spread_rows(iota((ROWS, SUB), 0) + r) for r in range(0, SUB, ROWS)]
     for start in range(0, width, SUB):
         at = slice(start, start + SUB)
-        index = index_ref[0:1, at]
-        for b in range(size // SUB):
-            low = index & (SUB - 1)
-            if size > SUB:
-                low = jnp.where((index & (size - 1)) >> 8 == b, low, WIDE)
-            low = spread_row(low, ROWS)
-            for r, row in enumerate(rows):
-                hot[b * SUB + r * ROWS : b * SUB + (r + 1) * ROWS, at] = jnp.where(row == low, ones, zeros)
-
-
-def masked(part, k, value):
-    return jnp.where(part == jnp.asarray(k, BF16), value, jnp.zeros((), BF16))
+        low = spread_row(index_ref[0:1, at] & (SUB - 1), ROWS)
+        for r, row in enumerate(rows):
+            hot[r * ROWS : (r + 1) * ROWS, at] = equal(row, low)
+
+
+def equal(one, other):
+    return jnp.maximum(jnp.asarray(1, BF16) - jnp.abs(one - other), jnp.asarray(0, BF16))
 
 
 def both(left, right, contract):
@@ -128,7 +120,7 @@
         digits = jnp.where(sub == 0, number >> 5, jnp.where(sub == 1, number & 31, 0)).astype(F32).astype(BF16)
         part = spread_row(slot[0:1, start : start + SUB] >> 8, ROWS)
         for k in range(width // SUB):
-            left[k * ROWS : (k + 1) * ROWS, start : start + SUB] = masked(part, k, digits)
+            left[k * ROWS : (k + 1) * ROWS, start : start + SUB] = equal(part, jnp.asarray(k, BF16)) * digits
     found = both(left[...], hot[...], ((1,), (1,)))
     for k in range(width // SUB):
         row = 32.0 * found[k * ROWS : k * ROWS + 1] + found[k * ROWS + 1 : k * ROWS + 2]
@@ -144,16 +136,13 @@
     pairs = heads.shape[1]
     copies[3].wait()
     invert(slot, hot, left, origin)
-    copies[1].wait()
+    for copy in copies[1:3] + copies[5:7]:
+        copy.wait()
     hot_table(hot_pairs.at[:, 0:pairs], heads, pairs)
-    copies[2].wait()
     hot_table(hot_pairs.at[:, pairs:], tails, pairs)
-    copies[5].wait()
-    copies[6].wait()
     spare = jnp.zeros((1, LANE - damping.shape[1]), F32)
     row = jnp.broadcast_to(jnp.concatenate([damping[...], spare], axis=1), lam.shape)
-    row = jnp.take_along_axis(row, cluster[...], axis=1)
-    lam[...] = row
+    lam[...] = jnp.take_along_axis(row, cluster[...], axis=1)
     copies[4].wait()
     copies[0].wait()
     dot = apply_precond(precond, right, scaled)
@@ -253,8 +242,8 @@
     width = errors.shape[1]
     share = got.shape[2]
     pairs = heads.shape[1]
-    parts = n_clus * width // WIDE
-    per_part = WIDE // share
+    parts = n_clus * width // SUB
+    per_part = SUB // share
     chunks = pairs // LANE
     half = n_clus // 2
     time_at, clus_at = lax.axis_index(axes[0]), lax.axis_index(axes[1])
@@ -270,12 +259,13 @@
 
     def spread(ends, base, n):
         at = slice(base * LANE + n * SUB, base * LANE + (n + 1) * SUB)
-        part = spread_row(ends[0:1, n * SUB : (n + 1) * SUB] >> 9, ROWS)
+        part = spread_row(ends[0:1, n * SUB : (n + 1) * SUB] >> 8, ROWS)
         row = (base + n * (SUB // LANE)) * ROWS
         high, low = halves(join([values[row + m * ROWS : row + (m + 1) * ROWS, :] for m in range(SUB // LANE)]))
         for k in range(parts):
-            left[k * 2 * ROWS : k * 2 * ROWS + ROWS, at] = masked(part, k, high)
-            left[k * 2 * ROWS + ROWS : (k + 1) * 2 * ROWS, at] = masked(part, k, low)
+            here = equal(part, jnp.asarray(k, BF16))
+            left[k * 2 * ROWS : k * 2 * ROWS + ROWS, at] = here * high
+            left[k * 2 * ROWS + ROWS : (k + 1) * 2 * ROWS, at] = here * low
 
     squares = jnp.zeros((8, LANE), F32)
     for h in range(0, chunks, 8):
@@ -465,7 +455,7 @@
             scratch_shapes=[
                 field,
                 pltpu.VMEM((2 * pairs // LANE * ROWS, LANE), F32),
-                pltpu.VMEM((2 * ROWS * positions // WIDE, 2 * pairs), BF16),
+                pltpu.VMEM((2 * ROWS * positions // SUB, 2 * pairs), BF16),
                 pltpu.VMEM((ROWS, LANE), F32),
             ],
             compiler_params=params,
@@ -479,7 +469,7 @@
             tile,
             jax.ShapeDtypeStruct((1, width), jnp.int32),
             *(jax.ShapeDtypeStruct(array.shape, array.dtype) for array in small[:4]),
-            jax.ShapeDtypeStruct((WIDE, 2 * pairs), BF16),
+            jax.ShapeDtypeStruct((SUB, 2 * pairs), BF16),
             like(width // LANE, LANE),
         ),
         in_specs=[in_hbm] * (3 + len(small)),

time: 65.6 us -> 65.2 us (level)
  no operation moved by 1% of the time
where the time goes in v11:
time: 65.2 us; the launch traced here: 64.9 us
  blocking collectives  51.6 us (79%)
  Pallas kernels  12.5 us (19%)
  between operations  0.72 us (1%)
    all_to_all x2, blocking collectives, collect(): lax.all_to_all(sent, axes, split_axis=0, concat_axis=0, tiled=True, axis_...  26.9 us
    all_to_all x2, blocking collectives, exchange(): lax.all_to_all(sent.reshape(devices, ROWS, share), axes, split_axis=0, co...  24.6 us
    pallas_call x2, Pallas kernels, grouped(): pl.pallas_call(functools.partial(group_kernel, n_time, n_clus, axes), out...  5.19 us
    pallas_call x2, Pallas kernels, grouped(): pl.pallas_call(functools.partial(half_kernel, axes, not tables), out_shap...  3.6 us
    pallas_call x1, Pallas kernels, on_device(): pl.pallas_call(begin_kernel, out_shape=(outgoing, tile, jax.ShapeDtypeStr...  2.17 us
  transfers between devices with their start and end apart: 2, of which 1 were waited for; matrix products, arithmetic and copies ran while one was open for 0% of the time, Pallas kernels for 6%

profile of v11, /device:TPU:0, one launch (start us, length us, event | category | flops | bytes accessed | tf_op | source)
XLA Modules:
  0.0 64.9 jit_solution(8979844539142099807)
XLA Ops:
  0.6 0.0 copy-start
  0.6 2.2 %begin.1 = (f32[8,2,16,128]{3,2,1,0:T(8,128)S(1)}, f32[16,1024]{1,0:T(8,128)S(1)}, s32[1,1024]{1,0:T(1,128)S(1)}, s32[1,2048]{1,0:T(1,128)S(1)}, s32[1,2048]{1,0...) custom-call(f32[15,1024]{1,0:T(8,128)} %right.1, ...), custom_call_target="tpu_custom_call" | custom-call | tf_op jit(solution)/shard_map/begin/pallas_call | solution.py:465
  2.8 15.9 %all_to_all.20.got = f32[16,16,128]{2,1,0:T(8,128)S(1)} all-to-all(f32[16,16,128]{2,1,0:T(8,128)S(1)} %bitcast.7), channel_id=1, replica_groups={{0,2,4,6,8,10,12,14,16,18,20,22,24,26,28,30},{1,3,5,7,9,11,13,15,17,19,..., dimensions={0} | all-to-all | bytes 262144 | tf_op jit(solution)/shard_map/all_to_all | solution.py:430
  18.7 0.0 collective-permute-start
  18.7 0.0 copy-done
  18.7 2.4 %half.2 = (f32[30,16,128]{2,1,0:T(8,128)S(1)}, f32[16,1024]{1,0:T(8,128)S(1)}, f32[16,1024]{1,0:T(8,128)S(1)}, f32[225,16,128]{2,1,0:T(8,128)S(1)}) custom-call(f32[16,16,128]{2,1,0:T(8,128)S(1)} %all_to_all.20.got, s32[16,128]{1,0:T(8,128)S(1)} %get-tuple-element.30.heads_tile, s32[16,128]{1,0:T(8,128)S(1)} %get-tuple-element.31.tails_tile, ...), custom_call_target="tpu_custom_call" | custom-call | tf_op jit(solution)/shard_map/half/pallas_call | solution.py:443
  21.1 0.0 collective-permute-done.other
  21.1 0.0 copy-start.1
  21.1 0.0 copy-start.2
  21.1 0.0 copy-start.3
  21.1 2.6 %group.2 = (f32[32,16,128]{2,1,0:T(8,128)S(1)}, f32[16,1024]{1,0:T(8,128)S(1)}, f32[1,128]{1,0:T(1,128)S(1)}) custom-call(f32[16,16,128]{2,1,0:T(8,128)S(1)} %all_to_all.20.got, f32[16,16,128]{2,1,0:T(8,128)S(1)} %collective-permute-done.other, f32[30,16,128]{2,1,0:T(8,128)S(1)} %get-tuple-element.33.pulled, s32[1,2048]{1,0:T(1,128)S(1)} %get-tuple-element.34.heads, ...), custom_call_target="tpu_custom_call" | custom-call | tf_op jit(solution)/shard_map/group/pallas_call | solution.py:452
  23.8 12.3 %all_to_all.21.got = f32[32,16,128]{2,1,0:T(8,128)S(1)} all-to-all(f32[32,16,128]{2,1,0:T(8,128)S(1)} %get-tuple-element.41), channel_id=1, replica_groups=mesh['tm'=8,'clus'=4] {'tm','clus'}, dimensions={0} | all-to-all | bytes 524288 | tf_op jit(solution)/shard_map/all_to_all | solution.py:415
  36.1 0.0 copy-done.1
  36.1 0.0 copy-done.2
  36.1 0.0 copy-done.3
  36.1 0.6 step.1
  36.7 11.0 %all_to_all.22.got = f32[16,16,128]{2,1,0:T(8,128)S(1)} all-to-all(f32[16,16,128]{2,1,0:T(8,128)S(1)} %bitcast.8), channel_id=1, replica_groups={{0,2,4,6,8,10,12,14,16,18,20,22,24,26,28,30},{1,3,5,7,9,11,13,15,17,19,..., dimensions={0} | all-to-all | bytes 262144 | tf_op jit(solution)/shard_map/all_to_all | solution.py:430
  47.7 0.0 collective-permute-start.1
  47.7 1.2 %half.3 = (f32[30,16,128]{2,1,0:T(8,128)S(1)}, f32[16,1024]{1,0:T(8,128)S(1)}, f32[16,1024]{1,0:T(8,128)S(1)}) custom-call(f32[16,16,128]{2,1,0:T(8,128)S(1)} %all_to_all.22.got, s32[16,128]{1,0:T(8,128)S(1)} %get-tuple-element.30.heads_tile, s32[16,128]{1,0:T(8,128)S(1)} %get-tuple-element.31.tails_tile, f32[16,1024]{1,0:T(8,128)S(1)} %get-tuple-element.46.scaled, ...), custom_call_target="tpu_custom_call" | custom-call | tf_op jit(solution)/shard_map/half/pallas_call | solution.py:443
  48.9 0.1 collective-permute-done.1.other
  49.0 2.6 %group.3 = (f32[32,16,128]{2,1,0:T(8,128)S(1)}, f32[16,1024]{1,0:T(8,128)S(1)}, f32[1,128]{1,0:T(1,128)S(1)}) custom-call(f32[16,16,128]{2,1,0:T(8,128)S(1)} %all_to_all.22.got, f32[16,16,128]{2,1,0:T(8,128)S(1)} %collective-permute-done.1.other, f32[30,16,128]{2,1,0:T(8,128)S(1)} %get-tuple-element.47.pulled, s32[1,2048]{1,0:T(1,128)S(1)} %get-tuple-element.34.heads, ...), custom_call_target="tpu_custom_call" | custom-call | tf_op jit(solution)/shard_map/group/pallas_call | solution.py:452
  51.6 12.3 %all_to_all.23.got = f32[32,16,128]{2,1,0:T(8,128)S(1)} all-to-all(f32[32,16,128]{2,1,0:T(8,128)S(1)} %get-tuple-element.50), channel_id=1, replica_groups=mesh['tm'=8,'clus'=4] {'tm','clus'}, dimensions={0} | all-to-all | bytes 524288 | tf_op jit(solution)/shard_map/all_to_all | solution.py:415
  63.9 0.9 %end.1 = (f32[15,1024]{1,0:T(8,128)}, f32[15,1024]{1,0:T(8,128)}) custom-call(f32[32,16,128]{2,1,0:T(8,128)S(1)} %all_to_all.23.got, f32[15,1024]{1,0:T(8,128)S(1)} %get-tuple-element.51.residual, f32[16,1024]{1,0:T(8,128)S(1)} %get-tuple-element.52.inertial, s32[1,1024]{1,0:T(1,128)S(1)} %bitcast.11, f32[16,1024]{1,0:T(8,128)S(1)} %get-tuple-element.32.scaled.first, ...), custom_call_target="tpu_custom_call" | custom-call | tf_op jit(solution)/shard_map/end/pallas_call | solution.py:497
Async XLA Ops:
  0.6 18.1 %copy-start = (f32[15,15,1024]{2,1,0:T(8,128)S(1)}, f32[15,15,1024]{2,1,0:T(8,128)}, u32[]{:S(2)}) copy-start(f32[15,15,1024]{2,1,0:T(8,128)} %transition.7) | copy-start | bytes 2764804
  18.7 2.4 %collective-permute-start = (f32[16,16,128]{2,1,0:T(8,128)S(1)}, f32[16,16,128]{2,1,0:T(8,128)S(1)}, u32[]{:S(2)}, u32[]{:S(2)}) collective-permute-start(f32[16,16,128]{2,1,0:T(8,128)S(1)} %all_to_all.20.got), channel_id=1, source_target_pairs={{0,1},{1,0},{2,3},{3,2},{4,5},{5,4},{6,7},{7,6},{8,9},{9,8},{10,11... | collective-permute-start | bytes 393224 | tf_op jit(solution)/shard_map/ppermute | solution.py:431
  21.1 15.0 %copy-start.1 = (f32[15,15,1024]{2,1,0:T(8,128)S(1)}, f32[15,15,1024]{2,1,0:T(8,128)}, u32[]{:S(2)}) copy-start(f32[15,15,1024]{2,1,0:T(8,128)} %precond.1) | copy-start | bytes 2764804
  21.1 15.0 %copy-start.2 = (f32[15,1024]{1,0:T(8,128)S(1)}, f32[15,1024]{1,0:T(8,128)}, u32[]{:S(2)}) copy-start(f32[15,1024]{1,0:T(8,128)} %right.1) | copy-start | bytes 184324
  21.1 14.9 %copy-start.3 = (s32[1024]{0:T(1024)S(1)}, s32[1024]{0:T(1024)}, u32[]{:S(2)}) copy-start(s32[1024]{0:T(1024)} %param.12) | copy-start | bytes 12292
  47.7 1.3 %collective-permute-start.1 = (f32[16,16,128]{2,1,0:T(8,128)S(1)}, f32[16,16,128]{2,1,0:T(8,128)S(1)}, u32[]{:S(2)}, u32[]{:S(2)}) collective-permute-start(f32[16,16,128]{2,1,0:T(8,128)S(1)} %all_to_all.22.got), channel_id=1, source_target_pairs={{0,1},{1,0},{2,3},{3,2},{4,5},{5,4},{6,7},{7,6},{8,9},{9,8},{10,11... | collective-permute-start | bytes 393224 | tf_op jit(solution)/shard_map/ppermute | solution.py:431

commit v12 on v11

--- a/solution.py
+++ b/solution.py
@@ -21,6 +21,18 @@
 def halves(value):
     high = value.astype(BF16)
     return high, (value - high.astype(F32)).astype(BF16)
+
+
+def pick(rows, index):
+    numbers = lax.GatherDimensionNumbers(
+        offset_dims=(),
+        collapsed_slice_dims=(1,),
+        start_index_map=(1,),
+        operand_batching_dims=(0,),
+        start_indices_batching_dims=(0,),
+    )
+    mode = lax.GatherScatterMode.PROMISE_IN_BOUNDS
+    return lax.gather(rows, index[:, :, None], numbers, (1, 1), mode=mode)
 
 
 def join(pieces):
@@ -93,7 +105,7 @@
     part = jnp.broadcast_to(index >> 7, (ROWS, LANE))
     out = jnp.zeros((ROWS, LANE), F32)
     for k, one in enumerate(tiles):
-        out = jnp.where(part == k, jnp.take_along_axis(one, low, axis=1), out)
+        out = jnp.where(part == k, pick(one, low), out)
     return out
 
 
@@ -142,7 +154,7 @@
     hot_table(hot_pairs.at[:, pairs:], tails, pairs)
     spare = jnp.zeros((1, LANE - damping.shape[1]), F32)
     row = jnp.broadcast_to(jnp.concatenate([damping[...], spare], axis=1), lam.shape)
-    lam[...] = jnp.take_along_axis(row, cluster[...], axis=1)
+    lam[...] = pick(row, cluster[...])
     copies[4].wait()
     copies[0].wait()
     dot = apply_precond(precond, right, scaled)
@@ -175,7 +187,7 @@
             here = part == (2 * i + parity) * tiles + r
             for c in range(state):
                 from_row = jnp.broadcast_to(field[i, r, c : c + 1, :], (8, LANE))
-                out[c] = jnp.where(here, jnp.take_along_axis(from_row, low, axis=1), out[c])
+                out[c] = jnp.where(here, pick(from_row, low), out[c])
     return out
 
 
@@ -206,34 +218,40 @@
         (copy,) = fetch(sems, (blocks_in, blocks))
     else:
         pulled, errors, inertial, field = refs
-    fill(field, got)
     parity = lax.axis_index(axes[1]) % 2
-    zero = [jnp.zeros((8, LANE), F32)] * state
-    for h in range(0, chunks, 8):
-        for which, ends in enumerate((heads_tile, tails_tile)):
-            for c, value in enumerate(pull(ends, h, field, parity, state, zero)):
-                pulled[which * state + c, h : h + 8, :] = value
-    lane = iota((ROWS, width), 1)
-    ahead = jnp.where(lane == width - 1, 0.0, pltpu.roll(scaled[...], width - 1, 1))
-    empty = jnp.zeros((ROWS - state, LANE), F32)
-    for start in range(0, width, LANE):
-        at = slice(start, start + LANE)
-        low, high = scaled[0:8, at], scaled[8:state, at]
-        for first in range(0, ROWS, 8):
-            moved = [
-                transition[i, 0:8, at] * low + jnp.concatenate([transition[i, 8:state, at] * high, empty], axis=0)
-                for i in range(first, min(first + 8, state))
-            ]
-            moved += [jnp.zeros((8, LANE), F32)] * (8 - len(moved))
-            errors[first : first + 8, at] = ahead[first : first + 8, at] - row_sums(moved)
-    prior = jnp.where(lane == 0, 0.0, pltpu.roll(errors[...], 1, 1))
-    inertial[state:ROWS, :] = jnp.zeros((ROWS - state, width), F32)
-    for start in range(0, width - LANE, LANE):
-        at = slice(start, start + LANE)
-        inertial[0:state, at] = prior[0:state, at] - back_product(transition, errors, at)
-    inertial[0:state, width - LANE :] = prior[0:state, width - LANE :]
+
+    def work():
+        fill(field, got)
+        zero = [jnp.zeros((8, LANE), F32)] * state
+        for h in range(0, chunks, 8):
+            for which, ends in enumerate((heads_tile, tails_tile)):
+                for c, value in enumerate(pull(ends, h, field, parity, state, zero)):
+                    pulled[which * state + c, h : h + 8, :] = value
+        lane = iota((ROWS, width), 1)
+        ahead = jnp.where(lane == width - 1, 0.0, pltpu.roll(scaled[...], width - 1, 1))
+        empty = jnp.zeros((ROWS - state, LANE), F32)
+        for start in range(0, width, LANE):
+            at = slice(start, start + LANE)
+            low, high = scaled[0:8, at], scaled[8:state, at]
+            for first in range(0, ROWS, 8):
+                moved = [
+                    transition[i, 0:8, at] * low + jnp.concatenate([transition[i, 8:state, at] * high, empty], axis=0)
+                    for i in range(first, min(first + 8, state))
+                ]
+                moved += [jnp.zeros((8, LANE), F32)] * (8 - len(moved))
+                errors[first : first + 8, at] = ahead[first : first + 8, at] - row_sums(moved)
+        prior = jnp.where(lane == 0, 0.0, pltpu.roll(errors[...], 1, 1))
+        inertial[state:ROWS, :] = jnp.zeros((ROWS - state, width), F32)
+        for start in range(0, width - LANE, LANE):
+            at = slice(start, start + LANE)
+            inertial[0:state, at] = prior[0:state, at] - back_product(transition, errors, at)
+        inertial[0:state, width - LANE :] = prior[0:state, width - LANE :]
+
     if once:
+        pl.when(parity >= 0)(work)
         copy.wait()
+    else:
+        work()
 
 
 def group_kernel(n_time, n_clus, axes, got, other, pulled, heads, tails, heads_tile, tails_tile, hot, lam, blocks,

time: 65.2 us -> 64.3 us (0.986)
  Pallas kernels: 12.5 us -> 11.7 us
    pallas_call x2, Pallas kernels: 3.6 us -> 2.76 us  [grouped(): pl.pallas_call(functools.partial(half_kernel, axes, not tables), out_shap...]
  transfers between devices with their start and end apart: 2 -> 2, of which waited for: 1 -> 1; matrix products, arithmetic and copies ran while one was open for 0% -> 0% of each run, Pallas kernels for 6% -> 4%
where the time goes in v12:
time: 64.3 us; the launch traced here: 64.1 us
  blocking collectives  51.6 us (80%)
  Pallas kernels  11.7 us (18%)
  between operations  0.72 us (1%)
    all_to_all x2, blocking collectives, collect(): lax.all_to_all(sent, axes, split_axis=0, concat_axis=0, tiled=True, axis_...  26.9 us
    all_to_all x2, blocking collectives, exchange(): lax.all_to_all(sent.reshape(devices, ROWS, share), axes, split_axis=0, co...  24.6 us
    pallas_call x2, Pallas kernels, grouped(): pl.pallas_call(functools.partial(group_kernel, n_time, n_clus, axes), out...  5.23 us
    pallas_call x2, Pallas kernels, grouped(): pl.pallas_call(functools.partial(half_kernel, axes, not tables), out_shap...  2.76 us
    pallas_call x1, Pallas kernels, on_device(): pl.pallas_call(begin_kernel, out_shape=(outgoing, tile, jax.ShapeDtypeStr...  2.17 us
  transfers between devices with their start and end apart: 2, of which 1 were waited for; matrix products, arithmetic and copies ran while one was open for 0% of the time, Pallas kernels for 4%

profile of v12, /device:TPU:0, one launch (start us, length us, event | category | flops | bytes accessed | tf_op | source)
XLA Modules:
  0.0 64.1 jit_solution(15740492433835765040)
XLA Ops:
  0.6 0.0 copy-start
  0.6 2.2 %begin.1 = (f32[8,2,16,128]{3,2,1,0:T(8,128)S(1)}, f32[16,1024]{1,0:T(8,128)S(1)}, s32[1,1024]{1,0:T(1,128)S(1)}, s32[1,2048]{1,0:T(1,128)S(1)}, s32[1,2048]{1,0...) custom-call(f32[15,1024]{1,0:T(8,128)} %right.1, ...), custom_call_target="tpu_custom_call" | custom-call | tf_op jit(solution)/shard_map/begin/pallas_call | solution.py:483
  2.8 15.9 %all_to_all.20.got = f32[16,16,128]{2,1,0:T(8,128)S(1)} all-to-all(f32[16,16,128]{2,1,0:T(8,128)S(1)} %bitcast.7), channel_id=1, replica_groups={{0,2,4,6,8,10,12,14,16,18,20,22,24,26,28,30},{1,3,5,7,9,11,13,15,17,19,..., dimensions={0} | all-to-all | bytes 262144 | tf_op jit(solution)/shard_map/all_to_all | solution.py:448
  18.7 0.0 collective-permute-start
  18.7 0.0 copy-done
  18.7 1.5 %half.2 = (f32[30,16,128]{2,1,0:T(8,128)S(1)}, f32[16,1024]{1,0:T(8,128)S(1)}, f32[16,1024]{1,0:T(8,128)S(1)}, f32[225,16,128]{2,1,0:T(8,128)S(1)}) custom-call(f32[16,16,128]{2,1,0:T(8,128)S(1)} %all_to_all.20.got, s32[16,128]{1,0:T(8,128)S(1)} %get-tuple-element.30.heads_tile, s32[16,128]{1,0:T(8,128)S(1)} %get-tuple-element.31.tails_tile, ...), custom_call_target="tpu_custom_call" | custom-call | tf_op jit(solution)/shard_map/half/pallas_call | solution.py:461
  20.3 0.0 collective-permute-done.other
  20.3 0.0 copy-start.1
  20.3 0.0 copy-start.2
  20.3 0.0 copy-start.3
  20.3 2.6 %group.2 = (f32[32,16,128]{2,1,0:T(8,128)S(1)}, f32[16,1024]{1,0:T(8,128)S(1)}, f32[1,128]{1,0:T(1,128)S(1)}) custom-call(f32[16,16,128]{2,1,0:T(8,128)S(1)} %all_to_all.20.got, f32[16,16,128]{2,1,0:T(8,128)S(1)} %collective-permute-done.other, f32[30,16,128]{2,1,0:T(8,128)S(1)} %get-tuple-element.33.pulled, s32[1,2048]{1,0:T(1,128)S(1)} %get-tuple-element.34.heads, ...), custom_call_target="tpu_custom_call" | custom-call | tf_op jit(solution)/shard_map/group/pallas_call | solution.py:470
  22.9 12.3 %all_to_all.21.got = f32[32,16,128]{2,1,0:T(8,128)S(1)} all-to-all(f32[32,16,128]{2,1,0:T(8,128)S(1)} %get-tuple-element.41), channel_id=1, replica_groups=mesh['tm'=8,'clus'=4] {'tm','clus'}, dimensions={0} | all-to-all | bytes 524288 | tf_op jit(solution)/shard_map/all_to_all | solution.py:433
  35.3 0.0 copy-done.1
  35.3 0.0 copy-done.2
  35.3 0.0 copy-done.3
  35.3 0.6 step.1
  35.8 11.0 %all_to_all.22.got = f32[16,16,128]{2,1,0:T(8,128)S(1)} all-to-all(f32[16,16,128]{2,1,0:T(8,128)S(1)} %bitcast.8), channel_id=1, replica_groups={{0,2,4,6,8,10,12,14,16,18,20,22,24,26,28,30},{1,3,5,7,9,11,13,15,17,19,..., dimensions={0} | all-to-all | bytes 262144 | tf_op jit(solution)/shard_map/all_to_all | solution.py:448
  46.9 0.0 collective-permute-start.1
  46.9 1.2 %half.3 = (f32[30,16,128]{2,1,0:T(8,128)S(1)}, f32[16,1024]{1,0:T(8,128)S(1)}, f32[16,1024]{1,0:T(8,128)S(1)}) custom-call(f32[16,16,128]{2,1,0:T(8,128)S(1)} %all_to_all.22.got, s32[16,128]{1,0:T(8,128)S(1)} %get-tuple-element.30.heads_tile, s32[16,128]{1,0:T(8,128)S(1)} %get-tuple-element.31.tails_tile, f32[16,1024]{1,0:T(8,128)S(1)} %get-tuple-element.46.scaled, ...), custom_call_target="tpu_custom_call" | custom-call | tf_op jit(solution)/shard_map/half/pallas_call | solution.py:461
  48.1 0.1 collective-permute-done.1.other
  48.2 2.6 %group.3 = (f32[32,16,128]{2,1,0:T(8,128)S(1)}, f32[16,1024]{1,0:T(8,128)S(1)}, f32[1,128]{1,0:T(1,128)S(1)}) custom-call(f32[16,16,128]{2,1,0:T(8,128)S(1)} %all_to_all.22.got, f32[16,16,128]{2,1,0:T(8,128)S(1)} %collective-permute-done.1.other, f32[30,16,128]{2,1,0:T(8,128)S(1)} %get-tuple-element.47.pulled, s32[1,2048]{1,0:T(1,128)S(1)} %get-tuple-element.34.heads, ...), custom_call_target="tpu_custom_call" | custom-call | tf_op jit(solution)/shard_map/group/pallas_call | solution.py:470
  50.8 12.3 %all_to_all.23.got = f32[32,16,128]{2,1,0:T(8,128)S(1)} all-to-all(f32[32,16,128]{2,1,0:T(8,128)S(1)} %get-tuple-element.50), channel_id=1, replica_groups=mesh['tm'=8,'clus'=4] {'tm','clus'}, dimensions={0} | all-to-all | bytes 524288 | tf_op jit(solution)/shard_map/all_to_all | solution.py:433
  63.1 0.9 %end.1 = (f32[15,1024]{1,0:T(8,128)}, f32[15,1024]{1,0:T(8,128)}) custom-call(f32[32,16,128]{2,1,0:T(8,128)S(1)} %all_to_all.23.got, f32[15,1024]{1,0:T(8,128)S(1)} %get-tuple-element.51.residual, f32[16,1024]{1,0:T(8,128)S(1)} %get-tuple-element.52.inertial, s32[1,1024]{1,0:T(1,128)S(1)} %bitcast.11, f32[16,1024]{1,0:T(8,128)S(1)} %get-tuple-element.32.scaled.first, ...), custom_call_target="tpu_custom_call" | custom-call | tf_op jit(solution)/shard_map/end/pallas_call | solution.py:515
Async XLA Ops:
  0.6 18.1 %copy-start = (f32[15,15,1024]{2,1,0:T(8,128)S(1)}, f32[15,15,1024]{2,1,0:T(8,128)}, u32[]{:S(2)}) copy-start(f32[15,15,1024]{2,1,0:T(8,128)} %transition.7) | copy-start | bytes 2764804
  18.7 1.5 %collective-permute-start = (f32[16,16,128]{2,1,0:T(8,128)S(1)}, f32[16,16,128]{2,1,0:T(8,128)S(1)}, u32[]{:S(2)}, u32[]{:S(2)}) collective-permute-start(f32[16,16,128]{2,1,0:T(8,128)S(1)} %all_to_all.20.got), channel_id=1, source_target_pairs={{0,1},{1,0},{2,3},{3,2},{4,5},{5,4},{6,7},{7,6},{8,9},{9,8},{10,11... | collective-permute-start | bytes 393224 | tf_op jit(solution)/shard_map/ppermute | solution.py:449
  20.3 15.0 %copy-start.1 = (f32[15,15,1024]{2,1,0:T(8,128)S(1)}, f32[15,15,1024]{2,1,0:T(8,128)}, u32[]{:S(2)}) copy-start(f32[15,15,1024]{2,1,0:T(8,128)} %precond.1) | copy-start | bytes 2764804
  20.3 15.0 %copy-start.2 = (f32[15,1024]{1,0:T(8,128)S(1)}, f32[15,1024]{1,0:T(8,128)}, u32[]{:S(2)}) copy-start(f32[15,1024]{1,0:T(8,128)} %right.1) | copy-start | bytes 184324
  20.3 15.0 %copy-start.3 = (s32[1024]{0:T(1024)S(1)}, s32[1024]{0:T(1024)}, u32[]{:S(2)}) copy-start(s32[1024]{0:T(1024)} %param.12) | copy-start | bytes 12292
  46.9 1.3 %collective-permute-start.1 = (f32[16,16,128]{2,1,0:T(8,128)S(1)}, f32[16,16,128]{2,1,0:T(8,128)S(1)}, u32[]{:S(2)}, u32[]{:S(2)}) collective-permute-start(f32[16,16,128]{2,1,0:T(8,128)S(1)} %all_to_all.22.got), channel_id=1, source_target_pairs={{0,1},{1,0},{2,3},{3,2},{4,5},{5,4},{6,7},{7,6},{8,9},{9,8},{10,11... | collective-permute-start | bytes 393224 | tf_op jit(solution)/shard_map/ppermute | solution.py:449

commit v13 on v12

--- a/solution.py
+++ b/solution.py
@@ -140,18 +140,15 @@
 
 
 def begin_kernel(right_in, precond_in, slot_in, heads_in, tails_in, heads_tile_in, tails_tile_in, cluster_in, damping_in,
-                 send, scaled, origin, heads, tails, heads_tile, tails_tile, hot_pairs, lam,
+                 send, scaled, origin, heads, tails, heads_tile, tails_tile, lam,
                  hot, left, right, precond, slot, cluster, damping, sems):
     state = right.shape[0]
     copies = fetch(sems, (precond_in, precond), (heads_in, heads), (tails_in, tails), (slot_in, slot), (right_in, right),
                    (cluster_in, cluster), (damping_in, damping), (heads_tile_in, heads_tile), (tails_tile_in, tails_tile))
-    pairs = heads.shape[1]
     copies[3].wait()
     invert(slot, hot, left, origin)
-    for copy in copies[1:3] + copies[5:7]:
-        copy.wait()
-    hot_table(hot_pairs.at[:, 0:pairs], heads, pairs)
-    hot_table(hot_pairs.at[:, pairs:], tails, pairs)
+    copies[5].wait()
+    copies[6].wait()
     spare = jnp.zeros((1, LANE - damping.shape[1]), F32)
     row = jnp.broadcast_to(jnp.concatenate([damping[...], spare], axis=1), lam.shape)
     lam[...] = pick(row, cluster[...])
@@ -159,8 +156,8 @@
     copies[0].wait()
     dot = apply_precond(precond, right, scaled)
     send_states(scaled, dot, origin, send, state)
-    copies[7].wait()
-    copies[8].wait()
+    for copy in copies[1:3] + copies[7:]:
+        copy.wait()
 
 
 def fetch(sems, *pairs):
@@ -214,7 +211,7 @@
     width = scaled.shape[1]
     chunks = heads_tile.shape[0]
     if once:
-        blocks_in, pulled, errors, inertial, blocks, field, sems = refs
+        heads, tails, blocks_in, pulled, errors, inertial, hot, blocks, field, sems = refs
         (copy,) = fetch(sems, (blocks_in, blocks))
     else:
         pulled, errors, inertial, field = refs
@@ -222,6 +219,10 @@
 
     def work():
         fill(field, got)
+        if once:
+            pairs = heads.shape[1]
+            hot_table(hot.at[:, 0:pairs], heads, pairs)
+            hot_table(hot.at[:, pairs:], tails, pairs)
         zero = [jnp.zeros((8, LANE), F32)] * state
         for h in range(0, chunks, 8):
             for which, ends in enumerate((heads_tile, tails_tile)):
@@ -254,7 +255,7 @@
         work()
 
 
-def group_kernel(n_time, n_clus, axes, got, other, pulled, heads, tails, heads_tile, tails_tile, hot, lam, blocks,
+def group_kernel(n_time, n_clus, axes, got, other, pulled, heads, tails, heads_tile, tails_tile, lam, hot, blocks,
                  errors, partial, transition, send, inertial, sums, field, values, left, last):
     state = transition.shape[0]
     width = errors.shape[1]
@@ -450,13 +451,13 @@
 
     def grouped(sent, scaled, carried, tables):
         got, other = collect(sent)
-        heads, tails, heads_tile, tails_tile, hot_of, lam = carried
+        heads, tails, heads_tile, tails_tile, lam = carried
         shapes = (like(2 * state, *dense), tile, tile)
         operands = (got, heads_tile, tails_tile, scaled, transition)
         scratch = [field]
         if not tables:
-            shapes += (like(*blocks.shape),)
-            operands += held(blocks)
+            shapes += (jax.ShapeDtypeStruct((SUB, 2 * pairs), BF16), like(*blocks.shape))
+            operands += (heads, tails, *held(blocks))
             scratch += [pltpu.SemaphoreType.DMA((1,))]
         pulled, errors, partial, *fresh = pl.pallas_call(
             functools.partial(half_kernel, axes, not tables),
@@ -478,7 +479,7 @@
             ],
             compiler_params=params,
             name="group",
-        )(got, other, pulled, heads, tails, heads_tile, tails_tile, hot_of, lam, *tables, errors, partial, transition)
+        )(got, other, pulled, heads, tails, heads_tile, tails_tile, lam, *tables, errors, partial, transition)
 
     sent, first, origin, *carried = pl.pallas_call(
         begin_kernel,
@@ -487,7 +488,6 @@
             tile,
             jax.ShapeDtypeStruct((1, width), jnp.int32),
             *(jax.ShapeDtypeStruct(array.shape, array.dtype) for array in small[:4]),
-            jax.ShapeDtypeStruct((SUB, 2 * pairs), BF16),
             like(width // LANE, LANE),
         ),
         in_specs=[in_hbm] * (3 + len(small)),

time: 64.3 us -> 64.2 us (level)
  transfers between devices with their start and end apart: 2 -> 2, of which waited for: 1 -> 1; matrix products, arithmetic and copies ran while one was open for 0% -> 0% of each run, Pallas kernels for 4% -> 5%
where the time goes in v13:
time: 64.2 us; the launch traced here: 63.9 us
  blocking collectives  51.6 us (80%)
  Pallas kernels  11.5 us (18%)
  between operations  0.72 us (1%)
    all_to_all x2, blocking collectives, collect(): lax.all_to_all(sent, axes, split_axis=0, concat_axis=0, tiled=True, axis_...  26.9 us
    all_to_all x2, blocking collectives, exchange(): lax.all_to_all(sent.reshape(devices, ROWS, share), axes, split_axis=0, co...  24.6 us
    pallas_call x2, Pallas kernels, grouped(): pl.pallas_call(functools.partial(group_kernel, n_time, n_clus, axes), out...  5.26 us
    pallas_call x2, Pallas kernels, grouped(): pl.pallas_call(functools.partial(half_kernel, axes, not tables), out_shap...  2.9 us
    pallas_call x1, Pallas kernels, on_device(): pl.pallas_call(begin_kernel, out_shape=(outgoing, tile, jax.ShapeDtypeStr...  1.88 us
  transfers between devices with their start and end apart: 2, of which 1 were waited for; matrix products, arithmetic and copies ran while one was open for 0% of the time, Pallas kernels for 5%

profile of v13, /device:TPU:0, one launch (start us, length us, event | category | flops | bytes accessed | tf_op | source)
XLA Modules:
  0.0 63.9 jit_solution(5839863493249900758)
XLA Ops:
  0.6 0.0 copy-start
  0.6 1.9 %begin.1 = (f32[8,2,16,128]{3,2,1,0:T(8,128)S(1)}, f32[16,1024]{1,0:T(8,128)S(1)}, s32[1,1024]{1,0:T(1,128)S(1)}, s32[1,2048]{1,0:T(1,128)S(1)}, s32[1,2048]{1,0...) custom-call(f32[15,1024]{1,0:T(8,128)} %right.1, f32[15,15,1024]{2,1,0:T(8,128)} %precond.1, ...), custom_call_target="tpu_custom_call" | custom-call | tf_op jit(solution)/shard_map/begin/pallas_call | solution.py:484
  2.5 15.9 %all_to_all.20.got = f32[16,16,128]{2,1,0:T(8,128)S(1)} all-to-all(f32[16,16,128]{2,1,0:T(8,128)S(1)} %bitcast.7), channel_id=1, replica_groups={{0,2,4,6,8,10,12,14,16,18,20,22,24,26,28,30},{1,3,5,7,9,11,13,15,17,19,..., dimensions={0} | all-to-all | bytes 262144 | tf_op jit(solution)/shard_map/all_to_all | solution.py:449
  18.4 0.0 collective-permute-start
  18.4 0.0 copy-done
  18.4 1.6 %half.2 = (f32[30,16,128]{2,1,0:T(8,128)S(1)}, f32[16,1024]{1,0:T(8,128)S(1)}, f32[16,1024]{1,0:T(8,128)S(1)}, bf16[256,4096]{1,0:T(8,128)(2,1)S(1)}, f32[225,16,128]{2,1,0:T(8,128)S(1)}) custom-call(f32[16,16,128]{2,1,0:T(8,128)S(1)} %all_to_all.20.got, s32[16,128]{1,0:T(8,128)S(1)} %get-tuple-element.30.heads_tile, ...), custom_call_target="tpu_custom_call" | custom-call | tf_op jit(solution)/shard_map/half/pallas_call | solution.py:462
  20.1 0.0 collective-permute-done.other
  20.1 0.0 copy-start.1
  20.1 0.0 copy-start.2
  20.1 0.0 copy-start.3
  20.1 2.6 %group.2 = (f32[32,16,128]{2,1,0:T(8,128)S(1)}, f32[16,1024]{1,0:T(8,128)S(1)}, f32[1,128]{1,0:T(1,128)S(1)}) custom-call(f32[16,16,128]{2,1,0:T(8,128)S(1)} %all_to_all.20.got, f32[16,16,128]{2,1,0:T(8,128)S(1)} %collective-permute-done.other, f32[30,16,128]{2,1,0:T(8,128)S(1)} %get-tuple-element.35.pulled, s32[1,2048]{1,0:T(1,128)S(1)} %get-tuple-element.33.refs_0_.heads, ...), custom_call_target="tpu_custom_call" | custom-call | tf_op jit(solution)/shard_map/group/pallas_call | solution.py:471
  22.8 12.3 %all_to_all.21.got = f32[32,16,128]{2,1,0:T(8,128)S(1)} all-to-all(f32[32,16,128]{2,1,0:T(8,128)S(1)} %get-tuple-element.41), channel_id=1, replica_groups=mesh['tm'=8,'clus'=4] {'tm','clus'}, dimensions={0} | all-to-all | bytes 524288 | tf_op jit(solution)/shard_map/all_to_all | solution.py:434
  35.1 0.0 copy-done.1
  35.1 0.0 copy-done.2
  35.1 0.0 copy-done.3
  35.1 0.6 step.1
  35.7 11.0 %all_to_all.22.got = f32[16,16,128]{2,1,0:T(8,128)S(1)} all-to-all(f32[16,16,128]{2,1,0:T(8,128)S(1)} %bitcast.8), channel_id=1, replica_groups={{0,2,4,6,8,10,12,14,16,18,20,22,24,26,28,30},{1,3,5,7,9,11,13,15,17,19,..., dimensions={0} | all-to-all | bytes 262144 | tf_op jit(solution)/shard_map/all_to_all | solution.py:449
  46.7 0.0 collective-permute-start.1
  46.7 1.3 %half.3 = (f32[30,16,128]{2,1,0:T(8,128)S(1)}, f32[16,1024]{1,0:T(8,128)S(1)}, f32[16,1024]{1,0:T(8,128)S(1)}) custom-call(f32[16,16,128]{2,1,0:T(8,128)S(1)} %all_to_all.22.got, s32[16,128]{1,0:T(8,128)S(1)} %get-tuple-element.30.heads_tile, s32[16,128]{1,0:T(8,128)S(1)} %get-tuple-element.31.tails_tile, f32[16,1024]{1,0:T(8,128)S(1)} %get-tuple-element.46.scaled, ...), custom_call_target="tpu_custom_call" | custom-call | tf_op jit(solution)/shard_map/half/pallas_call | solution.py:462
  48.0 0.1 collective-permute-done.1.other
  48.1 2.6 %group.3 = (f32[32,16,128]{2,1,0:T(8,128)S(1)}, f32[16,1024]{1,0:T(8,128)S(1)}, f32[1,128]{1,0:T(1,128)S(1)}) custom-call(f32[16,16,128]{2,1,0:T(8,128)S(1)} %all_to_all.22.got, f32[16,16,128]{2,1,0:T(8,128)S(1)} %collective-permute-done.1.other, f32[30,16,128]{2,1,0:T(8,128)S(1)} %get-tuple-element.47.pulled, ...), custom_call_target="tpu_custom_call" | custom-call | tf_op jit(solution)/shard_map/group/pallas_call | solution.py:471
  50.7 12.3 %all_to_all.23.got = f32[32,16,128]{2,1,0:T(8,128)S(1)} all-to-all(f32[32,16,128]{2,1,0:T(8,128)S(1)} %get-tuple-element.50), channel_id=1, replica_groups=mesh['tm'=8,'clus'=4] {'tm','clus'}, dimensions={0} | all-to-all | bytes 524288 | tf_op jit(solution)/shard_map/all_to_all | solution.py:434
  63.0 0.9 %end.1 = (f32[15,1024]{1,0:T(8,128)}, f32[15,1024]{1,0:T(8,128)}) custom-call(f32[32,16,128]{2,1,0:T(8,128)S(1)} %all_to_all.23.got, f32[15,1024]{1,0:T(8,128)S(1)} %get-tuple-element.51.residual, f32[16,1024]{1,0:T(8,128)S(1)} %get-tuple-element.52.inertial, s32[1,1024]{1,0:T(1,128)S(1)} %bitcast.11, f32[16,1024]{1,0:T(8,128)S(1)} %get-tuple-element.32.scaled.first, ...), custom_call_target="tpu_custom_call" | custom-call | tf_op jit(solution)/shard_map/end/pallas_call | solution.py:515
Async XLA Ops:
  0.6 17.8 %copy-start = (f32[15,15,1024]{2,1,0:T(8,128)S(1)}, f32[15,15,1024]{2,1,0:T(8,128)}, u32[]{:S(2)}) copy-start(f32[15,15,1024]{2,1,0:T(8,128)} %transition.7) | copy-start | bytes 2764804
  18.4 1.7 %collective-permute-start = (f32[16,16,128]{2,1,0:T(8,128)S(1)}, f32[16,16,128]{2,1,0:T(8,128)S(1)}, u32[]{:S(2)}, u32[]{:S(2)}) collective-permute-start(f32[16,16,128]{2,1,0:T(8,128)S(1)} %all_to_all.20.got), channel_id=1, source_target_pairs={{0,1},{1,0},{2,3},{3,2},{4,5},{5,4},{6,7},{7,6},{8,9},{9,8},{10,11... | collective-permute-start | bytes 393224 | tf_op jit(solution)/shard_map/ppermute | solution.py:450
  20.1 15.0 %copy-start.1 = (f32[15,15,1024]{2,1,0:T(8,128)S(1)}, f32[15,15,1024]{2,1,0:T(8,128)}, u32[]{:S(2)}) copy-start(f32[15,15,1024]{2,1,0:T(8,128)} %precond.1) | copy-start | bytes 2764804
  20.1 15.0 %copy-start.2 = (f32[15,1024]{1,0:T(8,128)S(1)}, f32[15,1024]{1,0:T(8,128)}, u32[]{:S(2)}) copy-start(f32[15,1024]{1,0:T(8,128)} %right.1) | copy-start | bytes 184324
  20.1 15.0 %copy-start.3 = (s32[1024]{0:T(1024)S(1)}, s32[1024]{0:T(1024)}, u32[]{:S(2)}) copy-start(s32[1024]{0:T(1024)} %param.12) | copy-start | bytes 12292
  46.7 1.3 %collective-permute-start.1 = (f32[16,16,128]{2,1,0:T(8,128)S(1)}, f32[16,16,128]{2,1,0:T(8,128)S(1)}, u32[]{:S(2)}, u32[]{:S(2)}) collective-permute-start(f32[16,16,128]{2,1,0:T(8,128)S(1)} %all_to_all.22.got), channel_id=1, source_target_pairs={{0,1},{1,0},{2,3},{3,2},{4,5},{5,4},{6,7},{7,6},{8,9},{9,8},{10,11... | collective-permute-start | bytes 393224 | tf_op jit(solution)/shard_map/ppermute | solution.py:450

commit v14 on v13

--- a/solution.py
+++ b/solution.py
@@ -139,12 +139,12 @@
         origin[0:1, k * SUB : (k + 1) * SUB] = row.astype(jnp.int32)
 
 
-def begin_kernel(right_in, precond_in, slot_in, heads_in, tails_in, heads_tile_in, tails_tile_in, cluster_in, damping_in,
-                 send, scaled, origin, heads, tails, heads_tile, tails_tile, lam,
+def begin_kernel(right_in, precond_in, slot_in, heads_in, tails_in, heads_tile_in, cluster_in, damping_in,
+                 send, scaled, origin, heads, tails, heads_tile, lam,
                  hot, left, right, precond, slot, cluster, damping, sems):
     state = right.shape[0]
     copies = fetch(sems, (precond_in, precond), (heads_in, heads), (tails_in, tails), (slot_in, slot), (right_in, right),
-                   (cluster_in, cluster), (damping_in, damping), (heads_tile_in, heads_tile), (tails_tile_in, tails_tile))
+                   (cluster_in, cluster), (damping_in, damping), (heads_tile_in, heads_tile))
     copies[3].wait()
     invert(slot, hot, left, origin)
     copies[5].wait()
@@ -188,6 +188,38 @@
     return out
 
 
+def pull_dense(tails, hot, field, stack, parity, before, store):
+    half, tiles = field.shape[0], field.shape[1]
+    per = SUB // LANE
+    parts = tiles // per
+    pairs = tails.shape[1]
+    for i in range(half):
+        for k in range(parts):
+            row = (i * parts + k) * 2 * ROWS
+            high, low = halves(join([field[i, k * per + m] for m in range(per)]))
+            stack[row : row + ROWS, :] = high
+            stack[row + ROWS : row + 2 * ROWS, :] = low
+    for n in range(pairs // SUB):
+        at = slice(n * SUB, (n + 1) * SUB)
+        found = both(stack[...], hot[:, pairs + n * SUB : pairs + (n + 1) * SUB], ((1,), (0,)))
+        part = tails[0:1, at] >> 8
+        out = before(n)
+        for i in range(half):
+            for k in range(parts):
+                row = (i * parts + k) * 2 * ROWS
+                one = found[row : row + ROWS] + found[row + ROWS : row + 2 * ROWS]
+                out = jnp.where(part == (2 * i + parity) * parts + k, one, out)
+        for m in range(per):
+            store(n * per + m, out[:, m * LANE : (m + 1) * LANE])
+
+
+def keep(far):
+    def store(n, tile):
+        far[n * ROWS : (n + 1) * ROWS, :] = tile
+
+    return store
+
+
 def fill(field, got):
     half, tiles = field.shape[0], field.shape[1]
     per = LANE // got.shape[2]
@@ -206,15 +238,15 @@
     return tiles[0]
 
 
-def half_kernel(axes, once, got, heads_tile, tails_tile, scaled, transition, *refs):
+def half_kernel(axes, once, got, heads_tile, scaled, transition, *refs):
     state = transition.shape[0]
     width = scaled.shape[1]
     chunks = heads_tile.shape[0]
     if once:
-        heads, tails, blocks_in, pulled, errors, inertial, hot, blocks, field, sems = refs
+        heads, tails, blocks_in, pulled, far, errors, inertial, hot, blocks, field, stack, sems = refs
         (copy,) = fetch(sems, (blocks_in, blocks))
     else:
-        pulled, errors, inertial, field = refs
+        tails, hot, pulled, far, errors, inertial, field, stack = refs
     parity = lax.axis_index(axes[1]) % 2
 
     def work():
@@ -225,9 +257,9 @@
             hot_table(hot.at[:, pairs:], tails, pairs)
         zero = [jnp.zeros((8, LANE), F32)] * state
         for h in range(0, chunks, 8):
-            for which, ends in enumerate((heads_tile, tails_tile)):
-                for c, value in enumerate(pull(ends, h, field, parity, state, zero)):
-                    pulled[which * state + c, h : h + 8, :] = value
+            for c, value in enumerate(pull(heads_tile, h, field, parity, state, zero)):
+                pulled[c, h : h + 8, :] = value
+        pull_dense(tails, hot, field, stack, parity, lambda n: jnp.zeros((ROWS, SUB), F32), keep(far))
         lane = iota((ROWS, width), 1)
         ahead = jnp.where(lane == width - 1, 0.0, pltpu.roll(scaled[...], width - 1, 1))
         empty = jnp.zeros((ROWS - state, LANE), F32)
@@ -255,8 +287,8 @@
         work()
 
 
-def group_kernel(n_time, n_clus, axes, got, other, pulled, heads, tails, heads_tile, tails_tile, lam, hot, blocks,
-                 errors, partial, transition, send, inertial, sums, field, values, left, last):
+def group_kernel(n_time, n_clus, axes, got, other, pulled, far_half, heads, tails, heads_tile, lam, hot, blocks,
+                 errors, partial, transition, send, inertial, sums, field, stack, far_whole, values, left, last):
     state = transition.shape[0]
     width = errors.shape[1]
     share = got.shape[2]
@@ -286,12 +318,16 @@
             left[k * 2 * ROWS : k * 2 * ROWS + ROWS, at] = here * high
             left[k * 2 * ROWS + ROWS : (k + 1) * 2 * ROWS, at] = here * low
 
+    def begun(n):
+        tiles = range(n * (SUB // LANE), (n + 1) * (SUB // LANE))
+        return join([far_half[m * ROWS : (m + 1) * ROWS, :] for m in tiles])
+
+    pull_dense(tails, hot, field, stack, parity, begun, keep(far_whole))
+
     squares = jnp.zeros((8, LANE), F32)
     for h in range(0, chunks, 8):
-        near, far = (
-            pull(ends, h, field, parity, state, [pulled[which * state + c, h : h + 8, :] for c in range(state)])
-            for which, ends in enumerate((heads_tile, tails_tile))
-        )
+        near = pull(heads_tile, h, field, parity, state, [pulled[c, h : h + 8, :] for c in range(state)])
+        far = [far_whole[pl.ds(h * ROWS + j, 8, stride=ROWS), :] for j in range(state)]
         back = [None] * state
         for i in range(state):
             row = [blocks[i * state + j, h : h + 8, :] for j in range(state)]
@@ -439,7 +475,7 @@
     in_hbm = pl.BlockSpec(memory_space=pltpu.HBM)
     in_vmem = pl.BlockSpec(memory_space=pltpu.VMEM)
     dense = (pairs // LANE, LANE)
-    small = (pair_first, pair_second, pair_first.reshape(dense), pair_second.reshape(dense),
+    small = (pair_first, pair_second, pair_first.reshape(dense),
              cluster_id.reshape(width // LANE, LANE), damping)
     same = [[t * n_clus + c for t in range(n_time) for c in range(q, n_clus, 2)] for q in range(2)]
     field = pltpu.VMEM((n_clus // 2, width // LANE, ROWS, LANE), F32)
@@ -451,15 +487,19 @@
 
     def grouped(sent, scaled, carried, tables):
         got, other = collect(sent)
-        heads, tails, heads_tile, tails_tile, lam = carried
-        shapes = (like(2 * state, *dense), tile, tile)
-        operands = (got, heads_tile, tails_tile, scaled, transition)
-        scratch = [field]
+        heads, tails, heads_tile, lam = carried
+        far = (pairs // LANE * ROWS, LANE)
+        shapes = (like(state, *dense), like(*far), tile, tile)
+        operands = (got, heads_tile, scaled, transition)
+        stack = pltpu.VMEM((positions // SUB * ROWS, SUB), BF16)
+        scratch = [field, stack]
         if not tables:
             shapes += (jax.ShapeDtypeStruct((SUB, 2 * pairs), BF16), like(*blocks.shape))
             operands += (heads, tails, *held(blocks))
             scratch += [pltpu.SemaphoreType.DMA((1,))]
-        pulled, errors, partial, *fresh = pl.pallas_call(
+        else:
+            operands += (tails, tables[0])
+        pulled, far_half, errors, partial, *fresh = pl.pallas_call(
             functools.partial(half_kernel, axes, not tables),
             out_shape=shapes,
             in_specs=[in_vmem] * (len(operands) - 1) + [in_vmem if tables else in_hbm],
@@ -473,13 +513,15 @@
             out_shape=(message, tile, row),
             scratch_shapes=[
                 field,
+                stack,
+                pltpu.VMEM(far, F32),
                 pltpu.VMEM((2 * pairs // LANE * ROWS, LANE), F32),
                 pltpu.VMEM((2 * ROWS * positions // SUB, 2 * pairs), BF16),
                 pltpu.VMEM((ROWS, LANE), F32),
             ],
             compiler_params=params,
             name="group",
-        )(got, other, pulled, heads, tails, heads_tile, tails_tile, lam, *tables, errors, partial, transition)
+        )(got, other, pulled, far_half, heads, tails, heads_tile, lam, *tables, errors, partial, transition)
 
     sent, first, origin, *carried = pl.pallas_call(
         begin_kernel,
@@ -487,7 +529,7 @@
             outgoing,
             tile,
             jax.ShapeDtypeStruct((1, width), jnp.int32),
-            *(jax.ShapeDtypeStruct(array.shape, array.dtype) for array in small[:4]),
+            *(jax.ShapeDtypeStruct(array.shape, array.dtype) for array in small[:3]),
             like(width // LANE, LANE),
         ),
         in_specs=[in_hbm] * (3 + len(small)),

time: 64.2 us -> 63.7 us (level)
  Pallas kernels: 11.5 us -> 10.6 us
  transfers between devices with their start and end apart: 2 -> 2, of which waited for: 1 -> 1; matrix products, arithmetic and copies ran while one was open for 0% -> 0% of each run, Pallas kernels for 5% -> 4%
where the time goes in v14:
time: 63.7 us; the launch traced here: 63.4 us
  blocking collectives  51.6 us (81%)
  Pallas kernels  10.6 us (17%)
  between operations  0.72 us (1%)
    all_to_all x2, blocking collectives, collect(): lax.all_to_all(sent, axes, split_axis=0, concat_axis=0, tiled=True, axis_...  26.9 us
    all_to_all x2, blocking collectives, exchange(): lax.all_to_all(sent.reshape(devices, ROWS, share), axes, split_axis=0, co...  24.6 us
    pallas_call x2, Pallas kernels, grouped(): pl.pallas_call(functools.partial(group_kernel, n_time, n_clus, axes), out...  4.88 us
    pallas_call x2, Pallas kernels, grouped(): pl.pallas_call(functools.partial(half_kernel, axes, not tables), out_shap...  2.3 us
    pallas_call x1, Pallas kernels, on_device(): pl.pallas_call(begin_kernel, out_shape=(outgoing, tile, jax.ShapeDtypeStr...  1.86 us
  transfers between devices with their start and end apart: 2, of which 1 were waited for; matrix products, arithmetic and copies ran while one was open for 0% of the time, Pallas kernels for 4%

profile of v14, /device:TPU:0, one launch (start us, length us, event | category | flops | bytes accessed | tf_op | source)
XLA Modules:
  0.0 63.4 jit_solution(17859003109042187631)
XLA Ops:
  0.6 0.0 copy-start
  0.6 1.9 %begin.1 = (f32[8,2,16,128]{3,2,1,0:T(8,128)S(1)}, f32[16,1024]{1,0:T(8,128)S(1)}, s32[1,1024]{1,0:T(1,128)S(1)}, s32[1,2048]{1,0:T(1,128)S(1)}, s32[1,2048]{1,0...) custom-call(f32[15,1024]{1,0:T(8,128)} %right.1, f32[15,15,1024]{2,1,0:T(8,128)} %precond.1, ...), custom_call_target="tpu_custom_call" | custom-call | tf_op jit(solution)/shard_map/begin/pallas_call | solution.py:526
  2.5 15.9 %all_to_all.20.got = f32[16,16,128]{2,1,0:T(8,128)S(1)} all-to-all(f32[16,16,128]{2,1,0:T(8,128)S(1)} %bitcast.7), channel_id=1, replica_groups={{0,2,4,6,8,10,12,14,16,18,20,22,24,26,28,30},{1,3,5,7,9,11,13,15,17,19,..., dimensions={0} | all-to-all | bytes 262144 | tf_op jit(solution)/shard_map/all_to_all | solution.py:485
  18.4 0.0 collective-permute-start
  18.4 0.0 copy-done
  18.4 1.5 %half.2 = (f32[15,16,128]{2,1,0:T(8,128)S(1)}, f32[256,128]{1,0:T(8,128)S(1)}, f32[16,1024]{1,0:T(8,128)S(1)}, f32[16,1024]{1,0:T(8,128)S(1)}, bf16[256,4096]{1,...) custom-call(f32[16,16,128]{2,1,0:T(8,128)S(1)} %all_to_all.20.got, s32[16,128]{1,0:T(8,128)S(1)} %get-tuple-element.31.heads_tile, ...), custom_call_target="tpu_custom_call" | custom-call | tf_op jit(solution)/shard_map/half/pallas_call | solution.py:502
  19.9 0.0 collective-permute-done.other
  20.0 0.0 copy-start.1
  20.0 0.0 copy-start.2
  20.0 0.0 copy-start.3
  20.0 2.4 %group.2 = (f32[32,16,128]{2,1,0:T(8,128)S(1)}, f32[16,1024]{1,0:T(8,128)S(1)}, f32[1,128]{1,0:T(1,128)S(1)}) custom-call(f32[16,16,128]{2,1,0:T(8,128)S(1)} %all_to_all.20.got, f32[16,16,128]{2,1,0:T(8,128)S(1)} %collective-permute-done.other, f32[15,16,128]{2,1,0:T(8,128)S(1)} %get-tuple-element.35.pulled, f32[256,128]{1,0:T(8,128)S(1)} %get-tuple-element.36.far_half, ...), custom_call_target="tpu_custom_call" | custom-call | tf_op jit(solution)/shard_map/group/pallas_call | solution.py:511
  22.5 12.3 %all_to_all.21.got = f32[32,16,128]{2,1,0:T(8,128)S(1)} all-to-all(f32[32,16,128]{2,1,0:T(8,128)S(1)} %get-tuple-element.42), channel_id=1, replica_groups=mesh['tm'=8,'clus'=4] {'tm','clus'}, dimensions={0} | all-to-all | bytes 524288 | tf_op jit(solution)/shard_map/all_to_all | solution.py:470
  34.8 0.0 copy-done.1
  34.8 0.0 copy-done.2
  34.8 0.0 copy-done.3
  34.8 0.6 step.1
  35.4 11.0 %all_to_all.22.got = f32[16,16,128]{2,1,0:T(8,128)S(1)} all-to-all(f32[16,16,128]{2,1,0:T(8,128)S(1)} %bitcast.6), channel_id=1, replica_groups={{0,2,4,6,8,10,12,14,16,18,20,22,24,26,28,30},{1,3,5,7,9,11,13,15,17,19,..., dimensions={0} | all-to-all | bytes 262144 | tf_op jit(solution)/shard_map/all_to_all | solution.py:485
  46.4 0.0 collective-permute-start.1
  46.4 0.8 %half.3 = (f32[15,16,128]{2,1,0:T(8,128)S(1)}, f32[256,128]{1,0:T(8,128)S(1)}, f32[16,1024]{1,0:T(8,128)S(1)}, f32[16,1024]{1,0:T(8,128)S(1)}) custom-call(f32[16,16,128]{2,1,0:T(8,128)S(1)} %all_to_all.22.got, s32[16,128]{1,0:T(8,128)S(1)} %get-tuple-element.31.heads_tile, f32[16,1024]{1,0:T(8,128)S(1)} %get-tuple-element.47.scaled, ...), custom_call_target="tpu_custom_call" | custom-call | tf_op jit(solution)/shard_map/half/pallas_call | solution.py:502
  47.2 0.6 collective-permute-done.1.other
  47.7 2.4 %group.3 = (f32[32,16,128]{2,1,0:T(8,128)S(1)}, f32[16,1024]{1,0:T(8,128)S(1)}, f32[1,128]{1,0:T(1,128)S(1)}) custom-call(f32[16,16,128]{2,1,0:T(8,128)S(1)} %all_to_all.22.got, f32[16,16,128]{2,1,0:T(8,128)S(1)} %collective-permute-done.1.other, f32[15,16,128]{2,1,0:T(8,128)S(1)} %get-tuple-element.48.pulled, f32[256,128]{1,0:T(8,128)S(1)} %get-tuple-element.49.far_half, ...), custom_call_target="tpu_custom_call" | custom-call | tf_op jit(solution)/shard_map/group/pallas_call | solution.py:511
  50.2 12.3 %all_to_all.23.got = f32[32,16,128]{2,1,0:T(8,128)S(1)} all-to-all(f32[32,16,128]{2,1,0:T(8,128)S(1)} %get-tuple-element.52), channel_id=1, replica_groups=mesh['tm'=8,'clus'=4] {'tm','clus'}, dimensions={0} | all-to-all | bytes 524288 | tf_op jit(solution)/shard_map/all_to_all | solution.py:470
  62.5 0.9 %end.1 = (f32[15,1024]{1,0:T(8,128)}, f32[15,1024]{1,0:T(8,128)}) custom-call(f32[32,16,128]{2,1,0:T(8,128)S(1)} %all_to_all.23.got, f32[15,1024]{1,0:T(8,128)S(1)} %get-tuple-element.53.residual, f32[16,1024]{1,0:T(8,128)S(1)} %get-tuple-element.54.inertial, s32[1,1024]{1,0:T(1,128)S(1)} %bitcast.10, f32[16,1024]{1,0:T(8,128)S(1)} %get-tuple-element.32.scaled.first, ...), custom_call_target="tpu_custom_call" | custom-call | tf_op jit(solution)/shard_map/end/pallas_call | solution.py:557
Async XLA Ops:
  0.6 17.8 %copy-start = (f32[15,15,1024]{2,1,0:T(8,128)S(1)}, f32[15,15,1024]{2,1,0:T(8,128)}, u32[]{:S(2)}) copy-start(f32[15,15,1024]{2,1,0:T(8,128)} %transition.7) | copy-start | bytes 2764804
  18.4 1.5 %collective-permute-start = (f32[16,16,128]{2,1,0:T(8,128)S(1)}, f32[16,16,128]{2,1,0:T(8,128)S(1)}, u32[]{:S(2)}, u32[]{:S(2)}) collective-permute-start(f32[16,16,128]{2,1,0:T(8,128)S(1)} %all_to_all.20.got), channel_id=1, source_target_pairs={{0,1},{1,0},{2,3},{3,2},{4,5},{5,4},{6,7},{7,6},{8,9},{9,8},{10,11... | collective-permute-start | bytes 393224 | tf_op jit(solution)/shard_map/ppermute | solution.py:486
  20.0 14.8 %copy-start.1 = (f32[15,15,1024]{2,1,0:T(8,128)S(1)}, f32[15,15,1024]{2,1,0:T(8,128)}, u32[]{:S(2)}) copy-start(f32[15,15,1024]{2,1,0:T(8,128)} %precond.1) | copy-start | bytes 2764804
  20.0 14.8 %copy-start.2 = (f32[15,1024]{1,0:T(8,128)S(1)}, f32[15,1024]{1,0:T(8,128)}, u32[]{:S(2)}) copy-start(f32[15,1024]{1,0:T(8,128)} %right.1) | copy-start | bytes 184324
  20.0 14.8 %copy-start.3 = (s32[1024]{0:T(1024)S(1)}, s32[1024]{0:T(1024)}, u32[]{:S(2)}) copy-start(s32[1024]{0:T(1024)} %param.12) | copy-start | bytes 12292
  46.4 1.3 %collective-permute-start.1 = (f32[16,16,128]{2,1,0:T(8,128)S(1)}, f32[16,16,128]{2,1,0:T(8,128)S(1)}, u32[]{:S(2)}, u32[]{:S(2)}) collective-permute-start(f32[16,16,128]{2,1,0:T(8,128)S(1)} %all_to_all.22.got), channel_id=1, source_target_pairs={{0,1},{1,0},{2,3},{3,2},{4,5},{5,4},{6,7},{7,6},{8,9},{9,8},{10,11... | collective-permute-start | bytes 393224 | tf_op jit(solution)/shard_map/ppermute | solution.py:486

commit v15 on v14

--- a/solution.py
+++ b/solution.py
@@ -143,21 +143,30 @@
                  send, scaled, origin, heads, tails, heads_tile, lam,
                  hot, left, right, precond, slot, cluster, damping, sems):
     state = right.shape[0]
-    copies = fetch(sems, (precond_in, precond), (heads_in, heads), (tails_in, tails), (slot_in, slot), (right_in, right),
+    matrix = planes(precond_in, precond, 3)
+    copies = fetch(sems, *matrix, (heads_in, heads), (tails_in, tails), (slot_in, slot), (right_in, right),
                    (cluster_in, cluster), (damping_in, damping), (heads_tile_in, heads_tile))
-    copies[3].wait()
+    copies, small = copies[: len(matrix)], copies[len(matrix) :]
+    small[2].wait()
     invert(slot, hot, left, origin)
-    copies[5].wait()
-    copies[6].wait()
+    small[4].wait()
+    small[5].wait()
     spare = jnp.zeros((1, LANE - damping.shape[1]), F32)
     row = jnp.broadcast_to(jnp.concatenate([damping[...], spare], axis=1), lam.shape)
     lam[...] = pick(row, cluster[...])
-    copies[4].wait()
-    copies[0].wait()
+    small[3].wait()
+    for copy in copies:
+        copy.wait()
     dot = apply_precond(precond, right, scaled)
     send_states(scaled, dot, origin, send, state)
-    for copy in copies[1:3] + copies[7:]:
+    for copy in small[0:2] + small[6:]:
         copy.wait()
+
+
+def planes(source, place, count):
+    length = source.shape[0]
+    step = length // count if length % count == 0 else length
+    return [(source.at[first : first + step], place.at[first : first + step]) for first in range(0, length, step)]
 
 
 def fetch(sems, *pairs):
@@ -244,7 +253,7 @@
     chunks = heads_tile.shape[0]
     if once:
         heads, tails, blocks_in, pulled, far, errors, inertial, hot, blocks, field, stack, sems = refs
-        (copy,) = fetch(sems, (blocks_in, blocks))
+        copies = fetch(sems, *planes(blocks_in, blocks, 5))
     else:
         tails, hot, pulled, far, errors, inertial, field, stack = refs
     parity = lax.axis_index(axes[1]) % 2
@@ -282,7 +291,8 @@
 
     if once:
         pl.when(parity >= 0)(work)
-        copy.wait()
+        for copy in copies:
+            copy.wait()
     else:
         work()
 
@@ -496,7 +506,7 @@
         if not tables:
             shapes += (jax.ShapeDtypeStruct((SUB, 2 * pairs), BF16), like(*blocks.shape))
             operands += (heads, tails, *held(blocks))
-            scratch += [pltpu.SemaphoreType.DMA((1,))]
+            scratch += [pltpu.SemaphoreType.DMA((5,))]
         else:
             operands += (tails, tables[0])
         pulled, far_half, errors, partial, *fresh = pl.pallas_call(
@@ -541,7 +551,7 @@
             pltpu.VMEM(slot.shape, jnp.int32),
             pltpu.VMEM((width // LANE, LANE), jnp.int32),
             pltpu.VMEM(damping.shape, F32),
-            pltpu.SemaphoreType.DMA((3 + len(small),)),
+            pltpu.SemaphoreType.DMA((5 + len(small),)),
         ],
         compiler_params=params,
         name="begin",

time: 63.7 us -> 63.7 us (level)
  no operation moved by 1% of the time
where the time goes in v15:
time: 63.7 us; the launch traced here: 63.4 us
  blocking collectives  51.6 us (81%)
  Pallas kernels  10.6 us (17%)
  between operations  0.72 us (1%)
    all_to_all x2, blocking collectives, collect(): lax.all_to_all(sent, axes, split_axis=0, concat_axis=0, tiled=True, axis_...  26.9 us
    all_to_all x2, blocking collectives, exchange(): lax.all_to_all(sent.reshape(devices, ROWS, share), axes, split_axis=0, co...  24.6 us
    pallas_call x2, Pallas kernels, grouped(): pl.pallas_call(functools.partial(group_kernel, n_time, n_clus, axes), out...  4.89 us
    pallas_call x2, Pallas kernels, grouped(): pl.pallas_call(functools.partial(half_kernel, axes, not tables), out_shap...  2.27 us
    pallas_call x1, Pallas kernels, on_device(): pl.pallas_call(begin_kernel, out_shape=(outgoing, tile, jax.ShapeDtypeStr...  1.89 us
  transfers between devices with their start and end apart: 2, of which 1 were waited for; matrix products, arithmetic and copies ran while one was open for 0% of the time, Pallas kernels for 4%

profile of v15, /device:TPU:0, one launch (start us, length us, event | category | flops | bytes accessed | tf_op | source)
XLA Modules:
  0.0 63.4 jit_solution(1977586005293852952)
XLA Ops:
  0.6 0.0 copy-start
  0.6 1.9 %begin.1 = (f32[8,2,16,128]{3,2,1,0:T(8,128)S(1)}, f32[16,1024]{1,0:T(8,128)S(1)}, s32[1,1024]{1,0:T(1,128)S(1)}, s32[1,2048]{1,0:T(1,128)S(1)}, s32[1,2048]{1,0...) custom-call(f32[15,1024]{1,0:T(8,128)} %right.1, f32[15,15,1024]{2,1,0:T(8,128)} %precond.1, ...), custom_call_target="tpu_custom_call" | custom-call | tf_op jit(solution)/shard_map/begin/pallas_call | solution.py:536
  2.5 15.9 %all_to_all.20.got = f32[16,16,128]{2,1,0:T(8,128)S(1)} all-to-all(f32[16,16,128]{2,1,0:T(8,128)S(1)} %bitcast.7), channel_id=1, replica_groups={{0,2,4,6,8,10,12,14,16,18,20,22,24,26,28,30},{1,3,5,7,9,11,13,15,17,19,..., dimensions={0} | all-to-all | bytes 262144 | tf_op jit(solution)/shard_map/all_to_all | solution.py:495
  18.4 0.0 collective-permute-start
  18.4 0.0 copy-done
  18.5 1.5 %half.2 = (f32[15,16,128]{2,1,0:T(8,128)S(1)}, f32[256,128]{1,0:T(8,128)S(1)}, f32[16,1024]{1,0:T(8,128)S(1)}, f32[16,1024]{1,0:T(8,128)S(1)}, bf16[256,4096]{1,...) custom-call(f32[16,16,128]{2,1,0:T(8,128)S(1)} %all_to_all.20.got, s32[16,128]{1,0:T(8,128)S(1)} %get-tuple-element.31.heads_tile, ...), custom_call_target="tpu_custom_call" | custom-call | tf_op jit(solution)/shard_map/half/pallas_call | solution.py:512
  19.9 0.0 collective-permute-done.other
  19.9 0.0 copy-start.1
  20.0 0.0 copy-start.2
  20.0 0.0 copy-start.3
  20.0 2.4 %group.2 = (f32[32,16,128]{2,1,0:T(8,128)S(1)}, f32[16,1024]{1,0:T(8,128)S(1)}, f32[1,128]{1,0:T(1,128)S(1)}) custom-call(f32[16,16,128]{2,1,0:T(8,128)S(1)} %all_to_all.20.got, f32[16,16,128]{2,1,0:T(8,128)S(1)} %collective-permute-done.other, f32[15,16,128]{2,1,0:T(8,128)S(1)} %get-tuple-element.35.pulled, f32[256,128]{1,0:T(8,128)S(1)} %get-tuple-element.36.far_half, ...), custom_call_target="tpu_custom_call" | custom-call | tf_op jit(solution)/shard_map/group/pallas_call | solution.py:521
  22.4 12.3 %all_to_all.21.got = f32[32,16,128]{2,1,0:T(8,128)S(1)} all-to-all(f32[32,16,128]{2,1,0:T(8,128)S(1)} %get-tuple-element.42), channel_id=1, replica_groups=mesh['tm'=8,'clus'=4] {'tm','clus'}, dimensions={0} | all-to-all | bytes 524288 | tf_op jit(solution)/shard_map/all_to_all | solution.py:480
  34.8 0.0 copy-done.1
  34.8 0.0 copy-done.2
  34.8 0.0 copy-done.3
  34.8 0.6 step.1
  35.4 11.0 %all_to_all.22.got = f32[16,16,128]{2,1,0:T(8,128)S(1)} all-to-all(f32[16,16,128]{2,1,0:T(8,128)S(1)} %bitcast.6), channel_id=1, replica_groups={{0,2,4,6,8,10,12,14,16,18,20,22,24,26,28,30},{1,3,5,7,9,11,13,15,17,19,..., dimensions={0} | all-to-all | bytes 262144 | tf_op jit(solution)/shard_map/all_to_all | solution.py:495
  46.4 0.0 collective-permute-start.1
  46.4 0.8 %half.3 = (f32[15,16,128]{2,1,0:T(8,128)S(1)}, f32[256,128]{1,0:T(8,128)S(1)}, f32[16,1024]{1,0:T(8,128)S(1)}, f32[16,1024]{1,0:T(8,128)S(1)}) custom-call(f32[16,16,128]{2,1,0:T(8,128)S(1)} %all_to_all.22.got, s32[16,128]{1,0:T(8,128)S(1)} %get-tuple-element.31.heads_tile, f32[16,1024]{1,0:T(8,128)S(1)} %get-tuple-element.47.scaled, ...), custom_call_target="tpu_custom_call" | custom-call | tf_op jit(solution)/shard_map/half/pallas_call | solution.py:512
  47.2 0.5 collective-permute-done.1.other
  47.7 2.4 %group.3 = (f32[32,16,128]{2,1,0:T(8,128)S(1)}, f32[16,1024]{1,0:T(8,128)S(1)}, f32[1,128]{1,0:T(1,128)S(1)}) custom-call(f32[16,16,128]{2,1,0:T(8,128)S(1)} %all_to_all.22.got, f32[16,16,128]{2,1,0:T(8,128)S(1)} %collective-permute-done.1.other, f32[15,16,128]{2,1,0:T(8,128)S(1)} %get-tuple-element.48.pulled, f32[256,128]{1,0:T(8,128)S(1)} %get-tuple-element.49.far_half, ...), custom_call_target="tpu_custom_call" | custom-call | tf_op jit(solution)/shard_map/group/pallas_call | solution.py:521
  50.2 12.3 %all_to_all.23.got = f32[32,16,128]{2,1,0:T(8,128)S(1)} all-to-all(f32[32,16,128]{2,1,0:T(8,128)S(1)} %get-tuple-element.52), channel_id=1, replica_groups=mesh['tm'=8,'clus'=4] {'tm','clus'}, dimensions={0} | all-to-all | bytes 524288 | tf_op jit(solution)/shard_map/all_to_all | solution.py:480
  62.5 0.9 %end.1 = (f32[15,1024]{1,0:T(8,128)}, f32[15,1024]{1,0:T(8,128)}) custom-call(f32[32,16,128]{2,1,0:T(8,128)S(1)} %all_to_all.23.got, f32[15,1024]{1,0:T(8,128)S(1)} %get-tuple-element.53.residual, f32[16,1024]{1,0:T(8,128)S(1)} %get-tuple-element.54.inertial, s32[1,1024]{1,0:T(1,128)S(1)} %bitcast.10, f32[16,1024]{1,0:T(8,128)S(1)} %get-tuple-element.32.scaled.first, ...), custom_call_target="tpu_custom_call" | custom-call | tf_op jit(solution)/shard_map/end/pallas_call | solution.py:567
Async XLA Ops:
  0.6 17.8 %copy-start = (f32[15,15,1024]{2,1,0:T(8,128)S(1)}, f32[15,15,1024]{2,1,0:T(8,128)}, u32[]{:S(2)}) copy-start(f32[15,15,1024]{2,1,0:T(8,128)} %transition.7) | copy-start | bytes 2764804
  18.4 1.5 %collective-permute-start = (f32[16,16,128]{2,1,0:T(8,128)S(1)}, f32[16,16,128]{2,1,0:T(8,128)S(1)}, u32[]{:S(2)}, u32[]{:S(2)}) collective-permute-start(f32[16,16,128]{2,1,0:T(8,128)S(1)} %all_to_all.20.got), channel_id=1, source_target_pairs={{0,1},{1,0},{2,3},{3,2},{4,5},{5,4},{6,7},{7,6},{8,9},{9,8},{10,11... | collective-permute-start | bytes 393224 | tf_op jit(solution)/shard_map/ppermute | solution.py:496
  19.9 14.8 %copy-start.1 = (f32[15,15,1024]{2,1,0:T(8,128)S(1)}, f32[15,15,1024]{2,1,0:T(8,128)}, u32[]{:S(2)}) copy-start(f32[15,15,1024]{2,1,0:T(8,128)} %precond.1) | copy-start | bytes 2764804
  20.0 14.8 %copy-start.2 = (f32[15,1024]{1,0:T(8,128)S(1)}, f32[15,1024]{1,0:T(8,128)}, u32[]{:S(2)}) copy-start(f32[15,1024]{1,0:T(8,128)} %right.1) | copy-start | bytes 184324
  20.0 14.8 %copy-start.3 = (s32[1024]{0:T(1024)S(1)}, s32[1024]{0:T(1024)}, u32[]{:S(2)}) copy-start(s32[1024]{0:T(1024)} %param.12) | copy-start | bytes 12292
  46.4 1.3 %collective-permute-start.1 = (f32[16,16,128]{2,1,0:T(8,128)S(1)}, f32[16,16,128]{2,1,0:T(8,128)S(1)}, u32[]{:S(2)}, u32[]{:S(2)}) collective-permute-start(f32[16,16,128]{2,1,0:T(8,128)S(1)} %all_to_all.22.got), channel_id=1, source_target_pairs={{0,1},{1,0},{2,3},{3,2},{4,5},{5,4},{6,7},{7,6},{8,9},{9,8},{10,11... | collective-permute-start | bytes 393224 | tf_op jit(solution)/shard_map/ppermute | solution.py:496

commit v16 on v14

--- a/solution.py
+++ b/solution.py
@@ -243,10 +243,10 @@
     width = scaled.shape[1]
     chunks = heads_tile.shape[0]
     if once:
-        heads, tails, blocks_in, pulled, far, errors, inertial, hot, blocks, field, stack, sems = refs
+        heads, tails, blocks_in, pulled, far, errors, inertial, energy, hot, blocks, field, stack, sems = refs
         (copy,) = fetch(sems, (blocks_in, blocks))
     else:
-        tails, hot, pulled, far, errors, inertial, field, stack = refs
+        tails, hot, pulled, far, errors, inertial, energy, field, stack = refs
     parity = lax.axis_index(axes[1]) % 2
 
     def work():
@@ -279,6 +279,10 @@
             at = slice(start, start + LANE)
             inertial[0:state, at] = prior[0:state, at] - back_product(transition, errors, at)
         inertial[0:state, width - LANE :] = prior[0:state, width - LANE :]
+        squares = jnp.zeros((ROWS, LANE), F32)
+        for start in range(0, width - LANE, LANE):
+            squares = squares + errors[:, start : start + LANE] * errors[:, start : start + LANE]
+        energy[...] = squares
 
     if once:
         pl.when(parity >= 0)(work)
@@ -288,7 +292,7 @@
 
 
 def group_kernel(n_time, n_clus, axes, got, other, pulled, far_half, heads, tails, heads_tile, lam, hot, blocks,
-                 errors, partial, transition, send, inertial, sums, field, stack, far_whole, values, left, last):
+                 errors, partial, begun_energy, transition, send, inertial, sums, field, stack, far_whole, values, left, last):
     state = transition.shape[0]
     width = errors.shape[1]
     share = got.shape[2]
@@ -355,10 +359,7 @@
     closed = ending & (flat == devices - 1)
     ahead = jnp.where(ending, errors[:, at] + following, errors[:, at])
     last[...] = jnp.where(closed | (iota((ROWS, LANE), 0) >= state), 0.0, ahead)
-    energy = last[...] * last[...]
-    for start in range(0, width - LANE, LANE):
-        block = errors[:, start : start + LANE]
-        energy = energy + jnp.where(iota((ROWS, LANE), 0) < state, block * block, 0.0)
+    energy = last[...] * last[...] + begun_energy[...]
     product = total(squares) + total(energy)
     inertial[...] = partial[...]
     back = transition[0, :, at] * last[0:1, :]
@@ -489,7 +490,7 @@
         got, other = collect(sent)
         heads, tails, heads_tile, lam = carried
         far = (pairs // LANE * ROWS, LANE)
-        shapes = (like(state, *dense), like(*far), tile, tile)
+        shapes = (like(state, *dense), like(*far), tile, tile, like(ROWS, LANE))
         operands = (got, heads_tile, scaled, transition)
         stack = pltpu.VMEM((positions // SUB * ROWS, SUB), BF16)
         scratch = [field, stack]
@@ -499,7 +500,7 @@
             scratch += [pltpu.SemaphoreType.DMA((1,))]
         else:
             operands += (tails, tables[0])
-        pulled, far_half, errors, partial, *fresh = pl.pallas_call(
+        pulled, far_half, errors, partial, energy, *fresh = pl.pallas_call(
             functools.partial(half_kernel, axes, not tables),
             out_shape=shapes,
             in_specs=[in_vmem] * (len(operands) - 1) + [in_vmem if tables else in_hbm],
@@ -521,7 +522,7 @@
             ],
             compiler_params=params,
             name="group",
-        )(got, other, pulled, far_half, heads, tails, heads_tile, lam, *tables, errors, partial, transition)
+        )(got, other, pulled, far_half, heads, tails, heads_tile, lam, *tables, errors, partial, energy, transition)
 
     sent, first, origin, *carried = pl.pallas_call(
         begin_kernel,

time: 63.7 us -> 63.9 us (level)
  no operation moved by 1% of the time
where the time goes in v16:
time: 63.9 us; the launch traced here: 63.6 us
  blocking collectives  51.6 us (81%)
  Pallas kernels  10.8 us (17%)
  between operations  0.72 us (1%)
    all_to_all x2, blocking collectives, collect(): lax.all_to_all(sent, axes, split_axis=0, concat_axis=0, tiled=True, axis_...  26.9 us
    all_to_all x2, blocking collectives, exchange(): lax.all_to_all(sent.reshape(devices, ROWS, share), axes, split_axis=0, co...  24.6 us
    pallas_call x2, Pallas kernels, grouped(): pl.pallas_call(functools.partial(group_kernel, n_time, n_clus, axes), out...  5.11 us
    pallas_call x2, Pallas kernels, grouped(): pl.pallas_call(functools.partial(half_kernel, axes, not tables), out_shap...  2.34 us
    pallas_call x1, Pallas kernels, on_device(): pl.pallas_call(begin_kernel, out_shape=(outgoing, tile, jax.ShapeDtypeStr...  1.86 us
  transfers between devices with their start and end apart: 2, of which 1 were waited for; matrix products, arithmetic and copies ran while one was open for 0% of the time, Pallas kernels for 4%

profile of v16, /device:TPU:0, one launch (start us, length us, event | category | flops | bytes accessed | tf_op | source)
XLA Modules:
  0.0 63.6 jit_solution(2326202361452230843)
XLA Ops:
  0.6 0.0 copy-start
  0.6 1.9 %begin.1 = (f32[8,2,16,128]{3,2,1,0:T(8,128)S(1)}, f32[16,1024]{1,0:T(8,128)S(1)}, s32[1,1024]{1,0:T(1,128)S(1)}, s32[1,2048]{1,0:T(1,128)S(1)}, s32[1,2048]{1,0...) custom-call(f32[15,1024]{1,0:T(8,128)} %right.1, f32[15,15,1024]{2,1,0:T(8,128)} %precond.1, ...), custom_call_target="tpu_custom_call" | custom-call | tf_op jit(solution)/shard_map/begin/pallas_call | solution.py:527
  2.5 15.9 %all_to_all.20.got = f32[16,16,128]{2,1,0:T(8,128)S(1)} all-to-all(f32[16,16,128]{2,1,0:T(8,128)S(1)} %bitcast.7), channel_id=1, replica_groups={{0,2,4,6,8,10,12,14,16,18,20,22,24,26,28,30},{1,3,5,7,9,11,13,15,17,19,..., dimensions={0} | all-to-all | bytes 262144 | tf_op jit(solution)/shard_map/all_to_all | solution.py:486
  18.4 0.0 collective-permute-start
  18.4 0.0 copy-done
  18.4 1.5 %half.2 = (f32[15,16,128]{2,1,0:T(8,128)S(1)}, f32[256,128]{1,0:T(8,128)S(1)}, f32[16,1024]{1,0:T(8,128)S(1)}, f32[16,1024]{1,0:T(8,128)S(1)}, f32[16,128]{1,0:T...) custom-call(f32[16,16,128]{2,1,0:T(8,128)S(1)} %all_to_all.20.got, ...), custom_call_target="tpu_custom_call" | custom-call | tf_op jit(solution)/shard_map/half/pallas_call | solution.py:503
  19.9 0.0 collective-permute-done.other
  20.0 0.0 copy-start.1
  20.0 0.0 copy-start.2
  20.0 0.0 copy-start.3
  20.0 2.6 %group.2 = (f32[32,16,128]{2,1,0:T(8,128)S(1)}, f32[16,1024]{1,0:T(8,128)S(1)}, f32[1,128]{1,0:T(1,128)S(1)}) custom-call(f32[16,16,128]{2,1,0:T(8,128)S(1)} %all_to_all.20.got, f32[16,16,128]{2,1,0:T(8,128)S(1)} %collective-permute-done.other, f32[15,16,128]{2,1,0:T(8,128)S(1)} %get-tuple-element.37.pulled, f32[256,128]{1,0:T(8,128)S(1)} %get-tuple-element.38.far_half, ...), custom_call_target="tpu_custom_call" | custom-call | tf_op jit(solution)/shard_map/group/pallas_call | solution.py:512
  22.6 12.3 %all_to_all.21.got = f32[32,16,128]{2,1,0:T(8,128)S(1)} all-to-all(f32[32,16,128]{2,1,0:T(8,128)S(1)} %get-tuple-element.45), channel_id=1, replica_groups=mesh['tm'=8,'clus'=4] {'tm','clus'}, dimensions={0} | all-to-all | bytes 524288 | tf_op jit(solution)/shard_map/all_to_all | solution.py:471
  34.9 0.0 copy-done.1
  34.9 0.0 copy-done.2
  34.9 0.0 copy-done.3
  34.9 0.6 step.1
  35.5 11.0 %all_to_all.22.got = f32[16,16,128]{2,1,0:T(8,128)S(1)} all-to-all(f32[16,16,128]{2,1,0:T(8,128)S(1)} %bitcast.6), channel_id=1, replica_groups={{0,2,4,6,8,10,12,14,16,18,20,22,24,26,28,30},{1,3,5,7,9,11,13,15,17,19,..., dimensions={0} | all-to-all | bytes 262144 | tf_op jit(solution)/shard_map/all_to_all | solution.py:486
  46.5 0.0 collective-permute-start.1
  46.5 0.8 %half.3 = (f32[15,16,128]{2,1,0:T(8,128)S(1)}, f32[256,128]{1,0:T(8,128)S(1)}, f32[16,1024]{1,0:T(8,128)S(1)}, f32[16,1024]{1,0:T(8,128)S(1)}, f32[16,128]{1,0:T(8,128)S(1)}) custom-call(f32[16,16,128]{2,1,0:T(8,128)S(1)} %all_to_all.22.got, s32[16,128]{1,0:T(8,128)S(1)} %get-tuple-element.33.heads_tile, f32[16,1024]{1,0:T(8,128)S(1)} %get-tuple-element.50.scaled, ...), custom_call_target="tpu_custom_call" | custom-call | tf_op jit(solution)/shard_map/half/pallas_call | solution.py:503
  47.3 0.5 collective-permute-done.1.other
  47.8 2.6 %group.3 = (f32[32,16,128]{2,1,0:T(8,128)S(1)}, f32[16,1024]{1,0:T(8,128)S(1)}, f32[1,128]{1,0:T(1,128)S(1)}) custom-call(f32[16,16,128]{2,1,0:T(8,128)S(1)} %all_to_all.22.got, f32[16,16,128]{2,1,0:T(8,128)S(1)} %collective-permute-done.1.other, f32[15,16,128]{2,1,0:T(8,128)S(1)} %get-tuple-element.51.pulled, f32[256,128]{1,0:T(8,128)S(1)} %get-tuple-element.52.far_half, ...), custom_call_target="tpu_custom_call" | custom-call | tf_op jit(solution)/shard_map/group/pallas_call | solution.py:512
  50.4 12.3 %all_to_all.23.got = f32[32,16,128]{2,1,0:T(8,128)S(1)} all-to-all(f32[32,16,128]{2,1,0:T(8,128)S(1)} %get-tuple-element.56), channel_id=1, replica_groups=mesh['tm'=8,'clus'=4] {'tm','clus'}, dimensions={0} | all-to-all | bytes 524288 | tf_op jit(solution)/shard_map/all_to_all | solution.py:471
  62.7 0.9 %end.1 = (f32[15,1024]{1,0:T(8,128)}, f32[15,1024]{1,0:T(8,128)}) custom-call(f32[32,16,128]{2,1,0:T(8,128)S(1)} %all_to_all.23.got, f32[15,1024]{1,0:T(8,128)S(1)} %get-tuple-element.57.residual, f32[16,1024]{1,0:T(8,128)S(1)} %get-tuple-element.58.inertial, s32[1,1024]{1,0:T(1,128)S(1)} %bitcast.10, f32[16,1024]{1,0:T(8,128)S(1)} %get-tuple-element.34.scaled.first, ...), custom_call_target="tpu_custom_call" | custom-call | tf_op jit(solution)/shard_map/end/pallas_call | solution.py:558
Async XLA Ops:
  0.6 17.8 %copy-start = (f32[15,15,1024]{2,1,0:T(8,128)S(1)}, f32[15,15,1024]{2,1,0:T(8,128)}, u32[]{:S(2)}) copy-start(f32[15,15,1024]{2,1,0:T(8,128)} %transition.7) | copy-start | bytes 2764804
  18.4 1.5 %collective-permute-start = (f32[16,16,128]{2,1,0:T(8,128)S(1)}, f32[16,16,128]{2,1,0:T(8,128)S(1)}, u32[]{:S(2)}, u32[]{:S(2)}) collective-permute-start(f32[16,16,128]{2,1,0:T(8,128)S(1)} %all_to_all.20.got), channel_id=1, source_target_pairs={{0,1},{1,0},{2,3},{3,2},{4,5},{5,4},{6,7},{7,6},{8,9},{9,8},{10,11... | collective-permute-start | bytes 393224 | tf_op jit(solution)/shard_map/ppermute | solution.py:487
  20.0 14.9 %copy-start.1 = (f32[15,15,1024]{2,1,0:T(8,128)S(1)}, f32[15,15,1024]{2,1,0:T(8,128)}, u32[]{:S(2)}) copy-start(f32[15,15,1024]{2,1,0:T(8,128)} %precond.1) | copy-start | bytes 2764804
  20.0 14.9 %copy-start.2 = (f32[15,1024]{1,0:T(8,128)S(1)}, f32[15,1024]{1,0:T(8,128)}, u32[]{:S(2)}) copy-start(f32[15,1024]{1,0:T(8,128)} %right.1) | copy-start | bytes 184324
  20.0 14.9 %copy-start.3 = (s32[1024]{0:T(1024)S(1)}, s32[1024]{0:T(1024)}, u32[]{:S(2)}) copy-start(s32[1024]{0:T(1024)} %param.12) | copy-start | bytes 12292
  46.5 1.3 %collective-permute-start.1 = (f32[16,16,128]{2,1,0:T(8,128)S(1)}, f32[16,16,128]{2,1,0:T(8,128)S(1)}, u32[]{:S(2)}, u32[]{:S(2)}) collective-permute-start(f32[16,16,128]{2,1,0:T(8,128)S(1)} %all_to_all.22.got), channel_id=1, source_target_pairs={{0,1},{1,0},{2,3},{3,2},{4,5},{5,4},{6,7},{7,6},{8,9},{9,8},{10,11... | collective-permute-start | bytes 393224 | tf_op jit(solution)/shard_map/ppermute | solution.py:487
